TPU v7x, 256 devices: a whole 4x4x8 slice. The times are simulated.
256 devices in a mesh: pat: 4 (over y), blk: 64 (over x, z, core).
Axes of the slice: x: 4, y: 4, z: 8, core: 2. Of those that a mesh axis runs over, the one named last changes fastest.
Arguments:
- voltages: bfloat16 [256, 262144], P('pat', 'blk'), may hold values from -6 to 6
- cotangent: float32 [256, 262144], P('pat', 'blk'), may hold values from -12 to 12
- ground: float32 [262144], P('blk'), may hold values from 0.5 to 2
- tile_values: bfloat16 [6144, 128, 128], P('blk'), may hold values from 0.0019989014 to 0.029907227
- tile_rows: int32 [6144], P('blk'), may hold values from 0 to 2047, as said below
- tile_cols: int32 [6144], P('blk'), may hold values from 0 to 2047, as said below
- tile_count: int32 [64], P('blk'), may hold values from 16 to 96, as said below
Outputs:
- adjoint: float32 [256, 262144], P('pat', 'blk')
- grads: bfloat16 [6144, 128, 128], P('blk', 'pat')
Inputs may be any that keep to these rules, and one draw needn't show every extreme that they name: `tile_count`: live slots of each index of blk are its first slots; one index holds 96 live slots. `tile_rows`: each slot's row block lies among the 32 blocks of the index of blk that holds the slot; in the first 4 slots of every index the column block lies on the next index. `tile_cols`: each slot's column block is (its row block + d) mod 2048 for some d in 1 to 4.
All inputs are finite; a program needn't handle non-finite values.
Results may differ from a plain program's by a relative error of at most 0.015.
Values may be sent and summed in bfloat16 or wider, within the bound.
No kernel may reach another device: no remote copies, remote signals or barrier semaphores. Data moves between devices by JAX's collectives and lax.ppermute only.
A program may use at most 128 MiB of HBM per device.

v0:
```python
import math

import jax
import jax.numpy as jnp
from jax import lax
from jax.sharding import PartitionSpec as P

BLOCK = 128
NB_DEV = 32
H = 4
ITERS = 2


spread_precision = lax.Precision.HIGH


def shifted(shard, axis, by):
    size = lax.axis_size(axis)
    return lax.ppermute(shard, axis, [(i, (i + by) % size) for i in range(size)])


def extend(field_b):
    ahead = shifted(field_b[..., :H, :], "blk", -1)
    return jnp.concatenate([field_b, ahead], axis=-2)


def spread_hot(index_local, slot_live, span_blocks):
    hits = index_local[:, None] == jnp.arange(span_blocks, dtype=jnp.int32)[None, :]
    return jnp.where(hits & slot_live[:, None], 1.0, 0.0).astype(jnp.float32)


def slot_terms(ext_b, tile_values, rows_local, cols_local, slot_live):
    span_blocks = ext_b.shape[1]
    near_rows = jnp.take(ext_b, cols_local, axis=1)
    here_rows = jnp.take(ext_b, rows_local, axis=1)
    forward = jnp.einsum("ptj,tij->pti", near_rows, tile_values, preferred_element_type=jnp.float32)
    backward = jnp.einsum(
        "pti,tij->ptj", here_rows, tile_values, preferred_element_type=jnp.float32
    )
    row_hot = spread_hot(rows_local, slot_live, span_blocks)
    col_hot = spread_hot(cols_local, slot_live, span_blocks)
    return jnp.einsum("pti,tb->pbi", forward, row_hot, precision=spread_precision) + jnp.einsum(
        "ptj,tb->pbj", backward, col_hot, precision=spread_precision
    )


def offdiag(field_b, layout):
    tile_values, rows_local, cols_local, live_slots, live_count = layout
    ext_b = extend(field_b)
    summed = slot_terms(ext_b, tile_values, rows_local, cols_local, live_slots)
    spill = shifted(summed[:, NB_DEV:, :].astype(jnp.bfloat16), "blk", 1).astype(jnp.float32)
    return summed[:, :NB_DEV, :].at[:, :H, :].add(spill)


def pattern_sum(left_field, right_field):
    return jnp.sum(left_field * right_field, axis=(1, 2))


def squares(residual):
    return lax.psum(pattern_sum(residual, residual), "blk")


def per_device(voltages, cotangent, ground, tile_values, tile_rows, tile_cols, tile_count):
    pattern_local = voltages.shape[0]
    owner = lax.axis_index("blk")
    blocks_all = NB_DEV * lax.axis_size("blk")
    rows_local = tile_rows - owner * NB_DEV
    cols_local = jnp.mod(tile_cols - owner * NB_DEV, blocks_all)
    live_count = tile_count[0]
    live_slots = jnp.arange(tile_values.shape[0], dtype=jnp.int32) < live_count
    layout = (tile_values, rows_local, cols_local, live_slots, live_count)
    ones_field = jnp.ones((1, NB_DEV, BLOCK), jnp.bfloat16)
    degree = offdiag(ones_field, layout)[0]
    diagonal = ground.reshape(NB_DEV, BLOCK) + degree
    rhs_field = cotangent.reshape(pattern_local, NB_DEV, BLOCK)
    solution = jnp.zeros_like(rhs_field)
    residual = rhs_field
    direction = rhs_field
    norm_now = squares(residual)
    for iteration in range(ITERS):
        image = diagonal[None] * direction - offdiag(direction.astype(jnp.bfloat16), layout)
        curvature = lax.psum(pattern_sum(direction, image), "blk")
        alpha = (norm_now / curvature)[:, None, None]
        solution = solution + alpha * direction
        if iteration + 1 < ITERS:
            residual = residual - alpha * image
            norm_next = squares(residual)
            direction = residual + (norm_next / norm_now)[:, None, None] * direction
            norm_now = norm_next
    lam_b = solution.astype(jnp.bfloat16)
    volt_b = voltages.reshape(pattern_local, NB_DEV, BLOCK)
    stacked = extend(jnp.stack([lam_b, volt_b]))
    scale = 1.0 / math.sqrt(pattern_local * lax.axis_size("pat"))
    slot_weight = jnp.where(live_slots, scale, 0.0).astype(jnp.float32)
    lam_ext = stacked[0]
    volt_ext = stacked[1]
    products = jnp.sum(lam_ext.astype(jnp.float32) * volt_ext.astype(jnp.float32), axis=0)
    lam_row = jnp.take(lam_ext, rows_local, axis=1)
    lam_col = jnp.take(lam_ext, cols_local, axis=1)
    volt_row = jnp.take(volt_ext, rows_local, axis=1)
    volt_col = jnp.take(volt_ext, cols_local, axis=1)
    cross_sum = jnp.einsum("pti,ptj->tij", lam_row, volt_col, preferred_element_type=jnp.float32)
    cross_sum = cross_sum + jnp.einsum(
        "pti,ptj->tij", volt_row, lam_col, preferred_element_type=jnp.float32
    )
    terms = cross_sum - products[rows_local][:, :, None] - products[cols_local][:, None, :]
    terms = terms * slot_weight[:, None, None]
    grads = lax.psum_scatter(terms.astype(jnp.bfloat16), "pat", scatter_dimension=1, tiled=True)
    return (solution.reshape(pattern_local, NB_DEV * BLOCK), grads)


def solution(mesh):
    return jax.shard_map(
        per_device,
        mesh=mesh,
        in_specs=(
            P("pat", "blk"),
            P("pat", "blk"),
            P("blk"),
            P("blk", None, None),
            P("blk"),
            P("blk"),
            P("blk"),
        ),
        out_specs=(P("pat", "blk"), P("blk", "pat", None)),
        check_vma=False,
    )
```

profile of v0, /device:TPU:1, one launch (start us, length us, event | category | flops | bytes accessed | tf_op | source)
XLA Modules:
  0.0 542.2 jit_solution(17871581119189969811)
XLA Ops:
  7.2 3.3 collective-permute-start
  13.9 5.8 %collective-permute-start.2 = (bf16[64,4,128]{2,1,0:T(4,128)(2,1)S(1)}, bf16[64,4,128]{2,1,0:T(4,128)(2,1)S(1)}, u32[]{:S(2)}, u32[]{:S(2)}) collective-permute-start(bf16[64,4,128]{2,1,0:T(4,128)(2,1)S(1)} %slice.156), channel_id=1, source_target_pairs={{0,63},{1,0},{2,1},{3,2},{4,3},{5,4},{6,5},{7,6},{8,7},{9,8},{10,9... | collective-permute-start | bytes 196616 | tf_op jit(solution)/shard_map/ppermute | solution.py:19
  27.9 3.0 gather_fusion.5
  31.0 3.0 gather_fusion.4
  34.0 3.8 fusion.23
  38.8 2.7 fusion.4
  41.4 2.7 fusion.44
  44.2 1.7 collective-permute-start.3
  46.0 4.6 collective-permute-done.3
  52.3 129.6 %all-reduce.1 = (f32[64]{0:T(128)S(1)}, f32[64]{0:T(128)S(1)}) all-reduce(f32[64]{0:T(128)S(1)} %multiply_reduce_fusion.3, f32[64]{0:T(128)S(1)} %fusion.55), channel_id=1, replica_groups=mesh['pat'=4,'blk'=64] {'blk'}, use_global_device_ids=true, to_apply=%region_1.2 | all-reduce | flops 128 | bytes 1024 | tf_op jit(solution)/shard_map/psum | solution.py:60
  181.9 2.5 multiply_reduce_fusion.2
  184.4 124.0 %psum.30 = f32[64]{0:T(128)S(1)} all-reduce(f32[64]{0:T(128)S(1)} %multiply_reduce_fusion.2), channel_id=1, replica_groups=mesh['pat'=4,'blk'=64] {'blk'}, use_global_device_ids=true, to_apply=%region_5.8 | all-reduce | flops 64 | bytes 512 | tf_op jit(solution)/shard_map/psum | solution.py:60
  308.5 1.9 fusion.128
  311.3 3.0 collective-permute-done.4
  315.4 3.0 gather_fusion.7
  318.4 3.0 gather_fusion.6
  321.4 3.8 fusion.19
  326.2 2.7 fusion
  328.9 2.7 fusion.50
  334.5 127.7 %psum.31 = f32[64]{0:T(128)S(1)} all-reduce(f32[64]{0:T(128)S(1)} %multiply_reduce_fusion.1), channel_id=1, replica_groups=mesh['pat'=4,'blk'=64] {'blk'}, use_global_device_ids=true, to_apply=%region_7.10 | all-reduce | flops 64 | bytes 512 | tf_op jit(solution)/shard_map/psum | solution.py:82
  462.2 3.0 convert_bitcast_fusion
  466.3 3.7 collective-permute-done.6
  472.8 2.0 copy.18
  474.9 3.0 gather_fusion.10
  477.9 3.0 gather_fusion.9
  480.9 2.0 copy.17
  482.9 3.0 gather_fusion.11
  485.9 3.0 gather_fusion.8
  489.0 3.3 fusion.14
  492.3 5.3 multiply_convert_fusion
  497.7 2.8 copy.61
  500.5 34.9 %reduce-scatter.2.cloned.1.call-done = bf16[96,32,128]{2,1,0:T(8,128)(2,1)} async-done(((bf16[96,128,128]{2,1,0:T(8,128)(2,1)}), bf16[96,32,128]{2,1,0:T(8,128)(2,1)}) %reduce-scatter.2.cloned.1.call-update) | async-done | bytes 786448 | tf_op jit(solution)/shard_map/reduce_scatter | solution.py:108
  (96 shorter events, 23.3 us)
Async XLA Ops:
  7.2 15.1 %copy-start = (bf16[96,128,128]{2,1,0:T(8,128)(2,1)S(1)}, bf16[96,128,128]{2,1,0:T(8,128)(2,1)}, u32[]{:S(2)}) copy-start(bf16[96,128,128]{2,1,0:T(8,128)(2,1)} %param.20) | copy-start | bytes 9437188
  7.2 528.2 %reduce-scatter.2.cloned.1.call-start = ((), (), s32[]{:S(2)}) async-start(), calls=%async_computation.1 | async-start | bytes 3932160 | tf_op jit(solution)/shard_map/reduce_scatter | solution.py:108
  7.2 13.5 %collective-permute-start = (bf16[1,4,128]{2,1,0:T(4,128)(2,1)S(1)}, bf16[1,4,128]{2,1,0:T(4,128)(2,1)S(1)}, u32[]{:S(2)}, u32[]{:S(2)}) collective-permute-start(bf16[1,4,128]{2,1,0:T(4,128)(2,1)S(1)} %slice.114), channel_id=1, source_target_pairs={{0,63},{1,0},{2,1},{3,2},{4,3},{5,4},{6,5},{7,6},{8,7},{9,8},{10,9... | collective-permute-start | bytes 3080 | tf_op jit(solution)/shard_map/ppermute | solution.py:19
  10.6 9.2 %copy-start.11 = (f32[64,4096]{1,0:T(8,128)S(1)}, f32[64,4096]{1,0:T(8,128)}, u32[]{:S(2)}) copy-start(f32[64,4096]{1,0:T(8,128)} %param.18) | copy-start | bytes 3145732
  12.1 1.0 copy-start.1
  13.0 7.6 %copy-start.16 = (s32[96]{0:T(128)S(1)}, s32[96]{0:T(128)}, u32[]{:S(2)}) copy-start(s32[96]{0:T(128)} %param.21) | copy-start | bytes 1156
  13.0 7.6 %copy-start.17 = (s32[96]{0:T(128)S(1)}, s32[96]{0:T(128)}, u32[]{:S(2)}) copy-start(s32[96]{0:T(128)} %param.22) | copy-start | bytes 1156
  13.1 0.8 copy-start.12
  13.9 13.0 %collective-permute-start.2 = (bf16[64,4,128]{2,1,0:T(4,128)(2,1)S(1)}, bf16[64,4,128]{2,1,0:T(4,128)(2,1)S(1)}, u32[]{:S(2)}, u32[]{:S(2)}) collective-permute-start(bf16[64,4,128]{2,1,0:T(4,128)(2,1)S(1)} %slice.156), channel_id=1, source_target_pairs={{0,63},{1,0},{2,1},{3,2},{4,3},{5,4},{6,5},{7,6},{8,7},{9,8},{10,9... | collective-permute-start | bytes 196616 | tf_op jit(solution)/shard_map/ppermute | solution.py:19
  24.0 2.9 copy-start.13
  25.3 1.6 collective-permute-start.1
  34.0 3.8 copy-start.8
  41.4 4.4 copy-start.15
  44.1 7.6 %copy-start.2 = (f32[8,8,32,128]{3,2,1,0:T(8,128)S(1)}, f32[8,8,32,128]{3,2,1,0:T(8,128)}, u32[]{:S(2)}) copy-start(f32[8,8,32,128]{3,2,1,0:T(8,128)} %copy-done.1) | copy-start | bytes 3145732
  44.2 6.5 %collective-permute-start.3 = (bf16[64,4,128]{2,1,0:T(4,128)(2,1)S(1)}, bf16[64,4,128]{2,1,0:T(4,128)(2,1)S(1)}, u32[]{:S(2)}, u32[]{:S(2)}) collective-permute-start(bf16[64,4,128]{2,1,0:T(4,128)(2,1)S(1)} %slice.188), channel_id=1, source_target_pairs={{0,1},{1,2},{2,3},{3,4},{4,5},{5,6},{6,7},{7,8},{8,9},{9,10},{10,1... | collective-permute-start | bytes 196616 | tf_op jit(solution)/shard_map/ppermute | solution.py:19
  50.7 1.0 copy-start.4
  310.4 4.0 collective-permute-start.4
  321.4 3.8 copy-start.9
  328.9 2.8 copy-start.14
  331.6 1.4 collective-permute-start.5
  331.7 1.4 copy-start.3
  331.7 1.7 copy-start.5
  462.2 3.0 copy-start.10
  465.3 4.7 collective-permute-start.6
  489.0 3.4 copy-start.6
  489.0 3.4 copy-start.7
Sparse Core Ops, SparseCore 0:
  497.8 37.5 reduce-scatter.1
where the time goes:
time: 543 us; the launch traced here: 542 us
  blocking collectives  381 us (70%)
  waiting for transfers between devices  47.9 us (9%)
  local copies, waits for them, and re-layouts  42.6 us (8%)
  matrix products  31.8 us (6%)
  between operations  15.1 us (3%)
  starting transfers between devices  13.2 us (2%)
  other arithmetic  10.2 us (2%)
    psum x2, blocking collectives, squares(): return lax.psum(pattern_sum(residual, residual), 'blk')  254 us
    psum x1, blocking collectives, per_device(): curvature = lax.psum(pattern_sum(direction, image), 'blk')  128 us
    reduce_scatter x1, waiting for transfers between devices, per_device(): lax.psum_scatter(terms.astype(jnp.bfloat16), 'pat', scatter_dimension=1,...  34.9 us
    ppermute x7, starting transfers between devices, shifted(): lax.ppermute(shard, axis, [(i, (i + by) % size) for i in range(size)])  13.1 us
    ppermute x7, waiting for transfers between devices, shifted(): lax.ppermute(shard, axis, [(i, (i + by) % size) for i in range(size)])  13 us
  transfers between devices with their start and end apart: 8, of which 6 were waited for; matrix products, arithmetic and copies ran while one was open for 2% of the time, Pallas kernels for 0%

commit v1 on v0

v1 whole, which is shorter than its diff:
```python
import math

import jax
import jax.numpy as jnp
from jax import lax
from jax.experimental import pallas as pl
from jax.experimental.pallas import tpu as pltpu
from jax.sharding import PartitionSpec as P

BLOCK = 128
NB_DEV = 32
H = 4
UNROLL = 8
MIN_GROUND = 0.5
F32 = jnp.float32
BF16 = jnp.bfloat16
VMEM = pl.BlockSpec(memory_space=pltpu.VMEM)
SMEM = pl.BlockSpec(memory_space=pltpu.SMEM)
EXT = NB_DEV + H
TRASH = EXT

NT = (((1,), (1,)), ((), ()))
NN = (((1,), (0,)), ((), ()))


def dot(a, b, dims):
    return lax.dot_general(a, b, dims, preferred_element_type=F32)


def cols_of(block, width=BLOCK):
    return slice(block * BLOCK, block * BLOCK + width)


def local_ends(rows_ref, cols_ref, slot, blocks_all):
    row = rows_ref[slot] & (NB_DEV - 1)
    ahead = (cols_ref[slot] - rows_ref[slot]) & (blocks_all - 1)
    return row, row + ahead


def steps(count, slots):
    return jnp.minimum((count + UNROLL - 1) // UNROLL, slots // UNROLL)


def first_kernel(
    blocks_all, rows_ref, cols_ref, count_ref, cot_ref, halo_ref, ground_ref, tiles_ref,
    v_ref, diag_ref, spill_ref, head_ref, w_ref, acc_ref,
):
    pats = cot_ref.shape[0]
    wide = w_ref.shape[1]
    count = count_ref[0]
    for b in range(EXT):
        if b < NB_DEV:
            block = cot_ref[:, cols_of(b)]
        else:
            block = halo_ref[:, cols_of(b - NB_DEV)]
        w_ref[b, :pats, :] = block.astype(BF16)
        w_ref[b, pats:, :] = jnp.ones((wide - pats, BLOCK), BF16)
    w_ref[TRASH] = jnp.zeros((wide, BLOCK), BF16)
    acc_ref[...] = jnp.zeros_like(acc_ref)

    def body(step, carry):
        ends, parts = [], []
        for u in range(UNROLL):
            slot = step * UNROLL + u
            row, col = local_ends(rows_ref, cols_ref, slot, blocks_all)
            live = slot < count
            row = jnp.where(live, row, TRASH)
            col = jnp.where(live, col, TRASH)
            tile = tiles_ref[slot]
            parts.append((dot(w_ref[col], tile, NT), dot(w_ref[row], tile, NN)))
            ends.append((row, col))
        for (row, col), (forward, backward) in zip(ends, parts):
            acc_ref[row] += forward
            acc_ref[col] += backward
        return carry

    lax.fori_loop(0, steps(count, tiles_ref.shape[0]), body, 0)
    for b in range(NB_DEV):
        diag = ground_ref[b : b + 1, :] + acc_ref[b, pats : pats + 1, :]
        value = diag * cot_ref[:, cols_of(b)] - acc_ref[b, :pats, :]
        v_ref[b] = value
        diag_ref[b] = jnp.broadcast_to(diag, (8, BLOCK))
        if b < H:
            head_ref[b] = value
    for b in range(H):
        spill_ref[b] = acc_ref[NB_DEV + b, : pats + 8, :]


def split(value):
    high = value.astype(BF16)
    low = (value - high.astype(F32)).astype(BF16)
    return jnp.concatenate([high, low], axis=0)


def quadratic(rows_ref, cols_ref, count_ref, tiles_ref, blocks_all, inside, exact_ref, pair_ref, quad_ref):
    count = count_ref[0]
    pats = exact_ref.shape[1]

    def body(step, carry):
        total = jnp.zeros((pats, BLOCK), F32)
        for u in range(UNROLL):
            slot = step * UNROLL + u
            row, col = local_ends(rows_ref, cols_ref, slot, blocks_all)
            take = (slot < count) & (((row >= H) & (col < NB_DEV)) == inside)
            row = jnp.where(take, row, TRASH)
            col = jnp.where(take, col, TRASH)
            both = dot(pair_ref[col], tiles_ref[slot], NT)
            total = total + (both[:pats] + both[pats:]) * exact_ref[row]
        quad_ref[...] += total
        return carry

    lax.fori_loop(0, steps(count, tiles_ref.shape[0]), body, 0)


def inner_kernel(
    blocks_all, rows_ref, cols_ref, count_ref, cot_ref, v_ref, diag_ref, tiles_ref,
    sums_ref, exact_ref, pair_ref, quad_ref,
):
    pats = cot_ref.shape[0]
    zero = jnp.zeros((pats, BLOCK), F32)
    m0, m1, m2, m3 = zero, zero, zero, zero
    for b in range(NB_DEV):
        c = cot_ref[:, cols_of(b)]
        m0 = m0 + c * c
        if b >= H:
            v = v_ref[b]
            m1 = m1 + c * v
            m2 = m2 + v * v
            m3 = m3 + diag_ref[b, 0:1, :] * (v * v)
            exact_ref[b] = v
            pair_ref[b] = split(v)
    exact_ref[TRASH] = zero
    pair_ref[TRASH] = jnp.zeros((2 * pats, BLOCK), BF16)
    quad_ref[...] = zero
    quadratic(rows_ref, cols_ref, count_ref, tiles_ref, blocks_all, True, exact_ref, pair_ref, quad_ref)
    sums_ref[0] = m0
    sums_ref[1] = m1
    sums_ref[2] = m2
    sums_ref[3] = m3 - 2.0 * quad_ref[...]


def outer_kernel(
    blocks_all, rows_ref, cols_ref, count_ref, cot_ref, halo_ref, v_ref, diag_ref, tiles_ref,
    spill_ref, before_ref, after_ref, sums_ref,
    first_ref, next_ref, moments_ref, exact_ref, pair_ref, quad_ref,
):
    pats = cot_ref.shape[0]
    m1, m2, m3 = sums_ref[1], sums_ref[2], sums_ref[3]
    for b in range(H):
        c = cot_ref[:, cols_of(b)]
        degree = before_ref[b, pats : pats + 1, :]
        v = v_ref[b] + degree * c - before_ref[b, :pats, :]
        first_ref[b] = v
        m1 = m1 + c * v
        m2 = m2 + v * v
        m3 = m3 + (diag_ref[b, 0:1, :] + degree) * (v * v)
        exact_ref[b] = v
        pair_ref[b] = split(v)
        beyond = after_ref[b] + spill_ref[b, pats : pats + 1, :] * halo_ref[:, cols_of(b)] - spill_ref[b, :pats, :]
        next_ref[b] = beyond
        exact_ref[NB_DEV + b] = beyond
        pair_ref[NB_DEV + b] = split(beyond)
    for b in list(range(H, 2 * H)) + list(range(NB_DEV - H, NB_DEV)):
        v = v_ref[b]
        exact_ref[b] = v
        pair_ref[b] = split(v)
    exact_ref[TRASH] = jnp.zeros((pats, BLOCK), F32)
    pair_ref[TRASH] = jnp.zeros((2 * pats, BLOCK), BF16)
    quad_ref[...] = jnp.zeros((pats, BLOCK), F32)
    quadratic(rows_ref, cols_ref, count_ref, tiles_ref, blocks_all, False, exact_ref, pair_ref, quad_ref)
    m3 = m3 - 2.0 * quad_ref[...]
    for k, m in enumerate((sums_ref[0], m1, m2, m3)):
        moments_ref[k : k + 1, :] = jnp.sum(m.T, axis=0, keepdims=True)


def combine_kernel(all_ref, cot_ref, halo_ref, v_ref, first_ref, next_ref, adjoint_ref, lam_ref):
    pats = cot_ref.shape[0]
    m = jnp.sum(all_ref[...], axis=0)
    m0, m1, m2, m3 = m[0:1], m[1:2], m[2:3], m[3:4]
    alpha = m0 / m1
    norm = jnp.maximum(alpha * alpha * m2 - m0, 0.0)
    grown = 1.0 + norm / m0
    curvature = alpha * alpha * m3 - grown * grown * m1
    positive = curvature > 0.0
    second = jnp.where(positive, norm / jnp.where(positive, curvature, 1.0), 0.0)
    second = jnp.minimum(second, 1.0 / MIN_GROUND)
    both = jnp.concatenate([alpha + second * grown, -alpha * second, jnp.zeros((6, pats), F32)], axis=0)
    both = both.T
    on_c = jnp.broadcast_to(both[:, 0:1], (pats, BLOCK))
    on_v = jnp.broadcast_to(both[:, 1:2], (pats, BLOCK))
    for b in range(NB_DEV):
        v = first_ref[b] if b < H else v_ref[b]
        value = on_c * cot_ref[:, cols_of(b)] + on_v * v
        adjoint_ref[:, cols_of(b)] = value
        lam_ref[b] = value.astype(BF16)
    for b in range(H):
        lam_ref[NB_DEV + b] = (on_c * halo_ref[:, cols_of(b)] + on_v * next_ref[b]).astype(BF16)


def chosen(part):
    i = lax.broadcasted_iota(jnp.int32, (BLOCK // 4, BLOCK), 0)
    j = lax.broadcasted_iota(jnp.int32, (BLOCK // 4, BLOCK), 1)
    return jnp.where(j == i + part * (BLOCK // 4), 1.0, 0.0).astype(BF16)


def volt_kernel(part_ref, near_ref, far_ref, volt_ref, turned_ref):
    part = part_ref[0]
    pick = chosen(part)
    pats = near_ref.shape[1]
    for k, by in enumerate((0, 3, 1, 2)):
        source = (part + by) & 3
        for b in range(NB_DEV):
            volt_ref[b, k * pats : (k + 1) * pats, :] = near_ref[source, :, cols_of(b)]
        for b in range(H):
            volt_ref[NB_DEV + b, k * pats : (k + 1) * pats, :] = far_ref[source, :, cols_of(b)]
    for b in range(NB_DEV):
        turned_ref[b] = dot(pick, volt_ref[b], NT).astype(BF16)


def grads_kernel(
    blocks_all, scale, part_ref, rows_ref, cols_ref, count_ref, own_ref, below_ref, above_ref, opp0_ref, opp1_ref,
    volt_ref, turned_ref, grads_ref, lam_ref, lamt_ref, prow_ref, pcol_ref,
):
    pats = own_ref.shape[1]
    part = part_ref[0]
    pick = chosen(part)
    count = count_ref[0]
    half = opp0_ref.shape[0]
    rows_out = grads_ref.shape[1]
    for b in range(EXT):
        lam_ref[b, :pats, :] = own_ref[b]
        lam_ref[b, pats : 2 * pats, :] = below_ref[b]
        lam_ref[b, 2 * pats : 3 * pats, :] = above_ref[b]
        lam_ref[b, 3 * pats :, :] = opp0_ref[b] if b < half else opp1_ref[b - half]
    for b in range(EXT):
        prow_ref[b] = jnp.sum(lam_ref[b].astype(F32) * volt_ref[b].astype(F32), axis=0, keepdims=True)
    for b in range(NB_DEV):
        turned = dot(pick, lam_ref[b], NT)
        lamt_ref[b] = turned.astype(BF16)
        column = jnp.sum(turned * turned_ref[b].astype(F32), axis=1, keepdims=True)
        pcol_ref[b] = jnp.broadcast_to(column, (rows_out, BLOCK))
    grads_ref[...] = jnp.zeros_like(grads_ref)

    def body(step, carry):
        outs = []
        for u in range(UNROLL):
            slot = step * UNROLL + u
            row, col = local_ends(rows_ref, cols_ref, slot, blocks_all)
            cross = dot(lamt_ref[row], volt_ref[col], NN) + dot(turned_ref[row], lam_ref[col], NN)
            value = (cross - pcol_ref[row] - prow_ref[col]) * scale
            outs.append(jnp.where(slot < count, value, 0.0).astype(BF16))
        for u in range(UNROLL):
            grads_ref[step * UNROLL + u] = outs[u]
        return carry

    lax.fori_loop(0, steps(count, grads_ref.shape[0]), body, 0)


def shifted(shard, axis, by):
    size = lax.axis_size(axis)
    return lax.ppermute(shard, axis, [(i, (i + by) % size) for i in range(size)])


def call(kernel, name, outs, specs, scratch, *args, cost=0):
    return pl.pallas_call(
        kernel,
        name=name,
        out_shape=[jax.ShapeDtypeStruct(s, d) for s, d in outs],
        in_specs=specs,
        out_specs=[VMEM] * len(outs),
        scratch_shapes=scratch,
        compiler_params=pltpu.CompilerParams(vmem_limit_bytes=24 * 1024 * 1024),
        cost_estimate=pl.CostEstimate(flops=cost, bytes_accessed=4 * 1024 * 1024, transcendentals=0),
    )(*args)


def per_device(voltages, cotangent, ground, tile_values, tile_rows, tile_cols, tile_count):
    pats = voltages.shape[0]
    slots = tile_values.shape[0]
    devices = lax.axis_size("blk")
    parts = lax.axis_size("pat")
    blocks_all = NB_DEV * devices
    wide = pats + 16
    part = lax.axis_index("pat").astype(jnp.int32).reshape(1)
    meta = (tile_rows, tile_cols, tile_count)
    field = (NB_DEV, pats, BLOCK)
    edge = (H, pats, BLOCK)
    rows_out = BLOCK // parts

    halo = shifted(cotangent[:, : H * BLOCK], "blk", -1)
    near = lax.all_gather(voltages, "pat")
    far = shifted(near[:, :, : H * BLOCK], "blk", -1)

    v, diag, spill, head = call(
        lambda *r: first_kernel(blocks_all, *r), "first_product",
        [(field, F32), ((NB_DEV, 8, BLOCK), F32), ((H, pats + 8, BLOCK), F32), (edge, F32)],
        [SMEM] * 3 + [VMEM] * 4,
        [pltpu.VMEM((EXT + 1, wide, BLOCK), BF16), pltpu.VMEM((EXT + 1, wide, BLOCK), F32)],
        *meta, cotangent, halo, ground.reshape(NB_DEV, BLOCK), tile_values,
    )
    before = shifted(spill, "blk", 1)
    after = shifted(head, "blk", -1)
    work = [
        pltpu.VMEM((EXT + 1, pats, BLOCK), F32),
        pltpu.VMEM((EXT + 1, 2 * pats, BLOCK), BF16),
        pltpu.VMEM((pats, BLOCK), F32),
    ]
    (sums,) = call(
        lambda *r: inner_kernel(blocks_all, *r), "inner_sums",
        [((4, pats, BLOCK), F32)], [SMEM] * 3 + [VMEM] * 4, work,
        *meta, cotangent, v, diag, tile_values,
    )
    first, beyond, moments = call(
        lambda *r: outer_kernel(blocks_all, *r), "outer_sums",
        [(edge, F32), (edge, F32), ((4, pats), F32)], [SMEM] * 3 + [VMEM] * 9, work,
        *meta, cotangent, halo, v, diag, tile_values, spill, before, after, sums,
    )
    spread = jnp.broadcast_to(moments[None], (devices, 4, pats))
    everyone = lax.all_to_all(spread, "blk", 0, 0)
    adjoint, lam = call(
        combine_kernel, "combine",
        [(cotangent.shape, F32), ((EXT, pats, BLOCK), BF16)], [VMEM] * 6, [],
        everyone, cotangent, halo, v, first, beyond,
    )
    half = EXT // 2
    below = shifted(lam, "pat", 1)
    above = shifted(lam, "pat", -1)
    opp0 = shifted(below[:half], "pat", 1)
    opp1 = shifted(above[half:], "pat", -1)
    volt, turned = call(
        volt_kernel, "volt_blocks",
        [((EXT, parts * pats, BLOCK), BF16), ((NB_DEV, rows_out, parts * pats), BF16)],
        [SMEM, VMEM, VMEM], [],
        part, near, far,
    )
    (grads,) = call(
        lambda *r: grads_kernel(blocks_all, 1.0 / math.sqrt(parts * pats), *r), "junction_grads",
        [((slots, rows_out, BLOCK), BF16)], [SMEM] * 4 + [VMEM] * 7,
        [
            pltpu.VMEM((EXT, parts * pats, BLOCK), BF16),
            pltpu.VMEM((NB_DEV, rows_out, parts * pats), BF16),
            pltpu.VMEM((EXT, 1, BLOCK), F32),
            pltpu.VMEM((NB_DEV, rows_out, BLOCK), F32),
        ],
        part, *meta, lam, below, above, opp0, opp1, volt, turned,
    )
    return adjoint, grads


def solution(mesh):
    return jax.shard_map(
        per_device,
        mesh=mesh,
        in_specs=(
            P("pat", "blk"),
            P("pat", "blk"),
            P("blk"),
            P("blk", None, None),
            P("blk"),
            P("blk"),
            P("blk"),
        ),
        out_specs=(P("pat", "blk"), P("blk", "pat", None)),
        check_vma=False,
    )
```

time: 543 us -> 98.5 us (0.18)
  blocking collectives: 381 us -> 22.2 us
  matrix products: 31.8 us -> 0 us
  local copies, waits for them, and re-layouts: 42.6 us -> 10.9 us
  waiting for transfers between devices: 47.9 us -> 19.5 us
  Pallas kernels: 0 us -> 11.4 us
  other arithmetic: 10.2 us -> 0.8 us
    psum x3 -> x0, blocking collectives: 381 us -> none  [the longest x2 254 us: squares(): return lax.psum(pattern_sum(residual, residual), 'blk')]
    reduce_scatter x1 -> x0, waiting for transfers between devices: 34.9 us -> none  [per_device(): lax.psum_scatter(terms.astype(jnp.bfloat16), 'pat', scatter_dimension=1,...]
    dot_general x14 -> x0, matrix products: 31.8 us -> none  [the longest x3 9.23 us: slot_terms(): jnp.einsum('ptj,tij->pti', near_rows, tile_values, preferred_element_type...]
    gather x12 -> x0, local copies, waits for them, and re-layouts: 26.7 us -> none  [the longest x3 6.71 us: slot_terms(): near_rows = jnp.take(ext_b, cols_local, axis=1)]
    all_to_all x0 -> x1, blocking collectives: none -> 22.2 us  [per_device(): everyone = lax.all_to_all(spread, 'blk', 0, 0)]
    pallas_call x0 -> x6, Pallas kernels: none -> 11.4 us  [call(): pl.pallas_call(kernel, name=name, out_shape=[jax.ShapeDtypeStruct(s, d) f...]
    ppermute x7 -> x8, waiting for transfers between devices: 13 us -> 18.9 us  [shifted(): lax.ppermute(shard, axis, [(i, (i + by) % size) for i in range(size)])]
    ppermute x7 -> x8, starting transfers between devices: 13.1 us -> 17.8 us  [shifted(): lax.ppermute(shard, axis, [(i, (i + by) % size) for i in range(size)])]
  transfers between devices with their start and end apart: 8 -> 9, of which waited for: 6 -> 3; matrix products, arithmetic and copies ran while one was open for 2% -> 5% of each run, Pallas kernels for 0% -> 8%
where the time goes in v1:
time: 98.5 us; the launch traced here: 97.5 us
  blocking collectives  22.2 us (23%)
  waiting for transfers between devices  19.5 us (20%)
  starting transfers between devices  17.8 us (18%)
  between operations  14.8 us (15%)
  Pallas kernels  11.4 us (12%)
  local copies, waits for them, and re-layouts  10.9 us (11%)
    all_to_all x1, blocking collectives, per_device(): everyone = lax.all_to_all(spread, 'blk', 0, 0)  22.2 us
    ppermute x8, waiting for transfers between devices, shifted(): lax.ppermute(shard, axis, [(i, (i + by) % size) for i in range(size)])  18.9 us
    ppermute x8, starting transfers between devices, shifted(): lax.ppermute(shard, axis, [(i, (i + by) % size) for i in range(size)])  17.8 us
    pallas_call x6, Pallas kernels, call(): pl.pallas_call(kernel, name=name, out_shape=[jax.ShapeDtypeStruct(s, d) f...  11.4 us
    unnamed x22, local copies, waits for them, and re-layouts  7 us
  transfers between devices with their start and end apart: 9, of which 3 were waited for; matrix products, arithmetic and copies ran while one was open for 5% of the time, Pallas kernels for 8%

profile of v1, /device:TPU:1, one launch (start us, length us, event | category | flops | bytes accessed | tf_op | source)
XLA Modules:
  0.0 97.5 jit_solution(6839961751267446725)
XLA Ops:
  7.2 0.0 all-gather.3.cloned.1.call-start
  7.2 0.7 all-gather.3.cloned.1.call-update
  7.9 0.9 slice.12
  8.8 3.3 %collective-permute-start = (f32[64,512]{1,0:T(8,128)S(1)}, f32[64,512]{1,0:T(8,128)S(1)}, u32[]{:S(2)}, u32[]{:S(2)}) collective-permute-start(f32[64,512]{1,0:T(8,128)S(1)} %slice.12), channel_id=1, source_target_pairs={{0,63},{1,0},{2,1},{3,2},{4,3},{5,4},{6,5},{7,6},{8,7},{9,8},{10,9... | collective-permute-start | bytes 393224 | tf_op jit(solution)/shard_map/ppermute | solution.py:261
  12.8 1.8 %collective-permute-done.r_4_.halo_ref = f32[64,512]{1,0:T(8,128)S(1)} collective-permute-done((f32[64,512]{1,0:T(8,128)S(1)}, f32[64,512]{1,0:T(8,128)S(1)}, u32[]{:S(2)}, u32[]{:S(2)}) %collective-permute-start) | collective-permute-done | bytes 131104 | tf_op jit(solution)/shard_map/ppermute | solution.py:261
  14.6 1.9 %copy-done = bf16[96,128,128]{2,1,0:T(8,128)(2,1)S(1)} copy-done((bf16[96,128,128]{2,1,0:T(8,128)(2,1)S(1)}, bf16[96,128,128]{2,1,0:T(8,128)(2,1)}, u32[]{:S(2)}) %copy-start) | copy-done | bytes 3145752
  16.5 1.2 %copy-done.2 = f32[64,4096]{1,0:T(8,128)S(1)} copy-done((f32[64,4096]{1,0:T(8,128)S(1)}, f32[64,4096]{1,0:T(8,128)}, u32[]{:S(2)}) %copy-start.2) | copy-done | bytes 1048600
  17.7 0.7 copy-done.5
  18.4 0.7 copy-done.6
  19.1 0.7 copy-done.8
  19.7 2.0 %first_product.1 = (f32[32,64,128]{2,1,0:T(8,128)S(1)}, f32[32,8,128]{2,1,0:T(8,128)S(1)}, f32[4,72,128]{2,1,0:T(8,128)S(1)}, f32[4,64,128]{2,1,0:T(8,128)S(1)}) custom-call(s32[96]{0:T(128)S(1)} %copy-done.6, s32[96]{0:T(128)S(1)} %copy-done.8, s32[1]{0:T(128)S(6)} %copy.9.r_2_.r_3_, f32[64,4096]{1,0:T(8,128)S(1)} %copy-done.2, ...), custom_call_target="tpu_custom_call" | custom-call | bytes 4194304 | tf_op jit(solution)/shard_map/first_product/pallas_call | solution.py:265
  21.8 0.7 collective-permute-start.1
  22.5 6.1 %collective-permute-start.2 = (f32[4,64,128]{2,1,0:T(8,128)S(1)}, f32[4,64,128]{2,1,0:T(8,128)S(1)}, u32[]{:S(2)}, u32[]{:S(2)}) collective-permute-start(f32[4,64,128]{2,1,0:T(8,128)S(1)} %get-tuple-element.16), channel_id=1, source_target_pairs={{0,63},{1,0},{2,1},{3,2},{4,3},{5,4},{6,5},{7,6},{8,7},{9,8},{10,9... | collective-permute-start | bytes 393224 | tf_op jit(solution)/shard_map/ppermute | solution.py:261
  28.5 1.8 %inner_sums.1.r_11_ = f32[4,64,128]{2,1,0:T(8,128)S(1)} custom-call(s32[96]{0:T(128)S(1)} %copy-done.6, s32[96]{0:T(128)S(1)} %copy-done.8, s32[1]{0:T(128)S(6)} %copy.9.r_2_.r_3_, f32[64,4096]{1,0:T(8,128)S(1)} %copy-done.2, f32[32,64,128]{2,1,0:T(8,128)S(1)} %get-tuple-element.13.r_4_.r_5_.v_ref, f32[32,8,128]{2,1,0:T(8,128)S(1)} %get-tuple-element.14.r_5_.r_6_, ...), custom_call_target="tpu_custom_call" | custom-call | bytes 4194304 | tf_op jit(solution)/shard_map/inner_sums/pallas_call | solution.py:265
  30.4 1.7 %outer_sums.1 = (f32[4,64,128]{2,1,0:T(8,128)S(1)}, f32[4,64,128]{2,1,0:T(8,128)S(1)}, f32[4,64]{1,0:T(4,128)S(1)}) custom-call(s32[96]{0:T(128)S(1)} %copy-done.6, s32[96]{0:T(128)S(1)} %copy-done.8, s32[1]{0:T(128)S(6)} %copy.9.r_2_.r_3_, f32[64,4096]{1,0:T(8,128)S(1)} %copy-done.2, f32[64,512]{1,0:T(8,128)S(1)} %collective-permute-done.r_4_.halo_ref, ...), custom_call_target="tpu_custom_call" | custom-call | bytes 4194304 | tf_op jit(solution)/shard_map/outer_sums/pallas_call | solution.py:265
  32.2 0.1 reshape.14
  32.3 22.2 %all_to_all.5 = f32[64,1,256]{2,1,0:T(1,128)S(1)} all-to-all(f32[64,1,256]{2,1,0:T(1,128)S(1)} %reshape.14), channel_id=1, replica_groups=mesh['pat'=4,'blk'=64] {'blk'}, dimensions={0} | all-to-all | bytes 131072 | tf_op jit(solution)/shard_map/all_to_all | solution.py:319
  54.5 0.5 broadcast.1
  55.0 0.8 reduce
  55.9 0.1 reshape.15.all_ref
  56.0 1.4 %combine.1 = (f32[64,4096]{1,0:T(8,128)}, bf16[36,64,128]{2,1,0:T(8,128)(2,1)S(1)}) custom-call(f32[64,4,64]{2,1,0:T(4,128)S(1)} %reshape.15.all_ref, f32[64,4096]{1,0:T(8,128)S(1)} %copy-done.3, f32[64,512]{1,0:T(8,128)S(1)} %collective-permute-done.r_4_.halo_ref, f32[32,64,128]{2,1,0:T(8,128)S(1)} %get-tuple-element.13.r_4_.r_5_.v_ref, ...), custom_call_target="tpu_custom_call" | custom-call | bytes 4194304 | tf_op jit(solution)/shard_map/combine/pallas_call | solution.py:265
  57.4 2.7 %collective-permute-start.4 = (bf16[36,64,128]{2,1,0:T(8,128)(2,1)S(1)}, bf16[36,64,128]{2,1,0:T(8,128)(2,1)S(1)}, u32[]{:S(2)}, u32[]{:S(2)}) collective-permute-start(bf16[36,64,128]{2,1,0:T(8,128)(2,1)S(1)} %get-tuple-element.21.r_4_), channel_id=1, source_target_pairs={{0,192},{64,0},{128,64},{192,128},{1,193},{65,1},{129,65},{193,129... | collective-permute-start | bytes 1769480 | tf_op jit(solution)/shard_map/ppermute | solution.py:261
  60.1 12.3 %collective-permute-done.4.r_6_ = bf16[36,64,128]{2,1,0:T(8,128)(2,1)S(1)} collective-permute-done((bf16[36,64,128]{2,1,0:T(8,128)(2,1)S(1)}, bf16[36,64,128]{2,1,0:T(8,128)(2,1)S(1)}, u32[]{:S(2)}, u32[]{:S(2)}) %collective-permute-start.4) | collective-permute-done | bytes 589856 | tf_op jit(solution)/shard_map/ppermute | solution.py:261
  72.5 0.7 slice.17
  73.2 3.4 %collective-permute-start.6 = (bf16[18,64,128]{2,1,0:T(8,128)(2,1)}, bf16[18,64,128]{2,1,0:T(8,128)(2,1)S(1)}, u32[]{:S(2)}, u32[]{:S(2)}) collective-permute-start(bf16[18,64,128]{2,1,0:T(8,128)(2,1)} %slice.17), channel_id=1, source_target_pairs={{0,192},{64,0},{128,64},{192,128},{1,193},{65,1},{129,65},{193,129... | collective-permute-start | bytes 884744 | tf_op jit(solution)/shard_map/ppermute | solution.py:261
  76.6 0.7 slice.16
  77.3 1.0 slice.18
  78.3 1.6 %collective-permute-start.7 = (bf16[4,64,512]{2,1,0:T(8,128)(2,1)S(1)}, bf16[4,64,512]{2,1,0:T(8,128)(2,1)S(1)}, u32[]{:S(2)}, u32[]{:S(2)}) collective-permute-start(bf16[4,64,512]{2,1,0:T(8,128)(2,1)S(1)} %slice.18), channel_id=1, source_target_pairs={{0,63},{1,0},{2,1},{3,2},{4,3},{5,4},{6,5},{7,6},{8,7},{9,8},{10,9... | collective-permute-start | bytes 786440 | tf_op jit(solution)/shard_map/ppermute | solution.py:261
  79.9 4.7 %collective-permute-done.7.far_ref = bf16[4,64,512]{2,1,0:T(8,128)(2,1)S(1)} collective-permute-done((bf16[4,64,512]{2,1,0:T(8,128)(2,1)S(1)}, bf16[4,64,512]{2,1,0:T(8,128)(2,1)S(1)}, u32[]{:S(2)}, u32[]{:S(2)}) %collective-permute-start.7) | collective-permute-done | bytes 262176 | tf_op jit(solution)/shard_map/ppermute | solution.py:261
  84.6 1.6 %copy-done.4 = bf16[256,4096]{1,0:T(8,128)(2,1)S(1)} copy-done((bf16[256,4096]{1,0:T(8,128)(2,1)S(1)}, bf16[256,4096]{1,0:T(8,128)(2,1)}, u32[]{:S(2)}) %copy-start.4) | copy-done | bytes 2097176
  86.2 0.9 volt_blocks.1
  87.2 3.5 %junction_grads.1 = bf16[96,32,128]{2,1,0:T(8,128)(2,1)} custom-call(s32[1]{0:T(128)} %bitcast.1.part_ref.r_0_, s32[96]{0:T(128)S(1)} %copy-done.7, s32[96]{0:T(128)S(1)} %copy-done.9, s32[1]{0:T(128)S(6)} %copy.9.r_2_.r_3_, bf16[36,64,128]{2,1,0:T(8,128)(2,1)S(1)} %get-tuple-element.21.r_4_, bf16[36,64,128]{2,1,0:T(8,128)(2,1)S(1)} %collective-permute-done.3.r_5_, ...), custom_call_target="tpu_custom_call" | custom-call | bytes 4194304 | tf_op jit(solution)/shard_map/junction_grads/pallas_call | solution.py:265
  (23 shorter events, 0.1 us)
Async XLA Ops:
  7.2 70.2 %all-gather.3.cloned.1.call-start = ((), (), s32[]{:S(2)}) async-start(), calls=%async_computation.1 | async-start | bytes 2621440 | tf_op jit(solution)/shard_map/all_gather | solution.py:291
  8.8 5.8 %collective-permute-start = (f32[64,512]{1,0:T(8,128)S(1)}, f32[64,512]{1,0:T(8,128)S(1)}, u32[]{:S(2)}, u32[]{:S(2)}) collective-permute-start(f32[64,512]{1,0:T(8,128)S(1)} %slice.12), channel_id=1, source_target_pairs={{0,63},{1,0},{2,1},{3,2},{4,3},{5,4},{6,5},{7,6},{8,7},{9,8},{10,9... | collective-permute-start | bytes 393224 | tf_op jit(solution)/shard_map/ppermute | solution.py:261
  14.6 1.9 %copy-start = (bf16[96,128,128]{2,1,0:T(8,128)(2,1)S(1)}, bf16[96,128,128]{2,1,0:T(8,128)(2,1)}, u32[]{:S(2)}) copy-start(bf16[96,128,128]{2,1,0:T(8,128)(2,1)} %r_7_.1) | copy-start | bytes 9437188
  16.5 1.2 %copy-start.2 = (f32[64,4096]{1,0:T(8,128)S(1)}, f32[64,4096]{1,0:T(8,128)}, u32[]{:S(2)}) copy-start(f32[64,4096]{1,0:T(8,128)} %cot_ref.1) | copy-start | bytes 3145732
  17.7 0.7 copy-start.5
  18.4 0.7 copy-start.6
  19.1 0.7 copy-start.8
  19.7 8.8 %copy-start.1 = (bf16[96,128,128]{2,1,0:T(8,128)(2,1)S(1)}, bf16[96,128,128]{2,1,0:T(8,128)(2,1)}, u32[]{:S(2)}) copy-start(bf16[96,128,128]{2,1,0:T(8,128)(2,1)} %r_7_.1) | copy-start | bytes 9437188
  21.8 8.6 %collective-permute-start.1 = (f32[4,72,128]{2,1,0:T(8,128)S(1)}, f32[4,72,128]{2,1,0:T(8,128)S(1)}, u32[]{:S(2)}, u32[]{:S(2)}) collective-permute-start(f32[4,72,128]{2,1,0:T(8,128)S(1)} %get-tuple-element.15.r_8_), channel_id=1, source_target_pairs={{0,1},{1,2},{2,3},{3,4},{4,5},{5,6},{6,7},{7,8},{8,9},{9,10},{10,1... | collective-permute-start | bytes 442376 | tf_op jit(solution)/shard_map/ppermute | solution.py:261
  22.5 7.9 %collective-permute-start.2 = (f32[4,64,128]{2,1,0:T(8,128)S(1)}, f32[4,64,128]{2,1,0:T(8,128)S(1)}, u32[]{:S(2)}, u32[]{:S(2)}) collective-permute-start(f32[4,64,128]{2,1,0:T(8,128)S(1)} %get-tuple-element.16), channel_id=1, source_target_pairs={{0,63},{1,0},{2,1},{3,2},{4,3},{5,4},{6,5},{7,6},{8,7},{9,8},{10,9... | collective-permute-start | bytes 393224 | tf_op jit(solution)/shard_map/ppermute | solution.py:261
  30.4 25.6 %copy-start.3 = (f32[64,4096]{1,0:T(8,128)S(1)}, f32[64,4096]{1,0:T(8,128)}, u32[]{:S(2)}) copy-start(f32[64,4096]{1,0:T(8,128)} %cot_ref.1) | copy-start | bytes 3145732
  57.4 29.7 %copy-start.7 = (s32[96]{0:T(128)S(1)}, s32[96]{0:T(128)}, u32[]{:S(2)}) copy-start(s32[96]{0:T(128)} %r_1_.7) | copy-start | bytes 1156
  57.4 29.7 %copy-start.9 = (s32[96]{0:T(128)S(1)}, s32[96]{0:T(128)}, u32[]{:S(2)}) copy-start(s32[96]{0:T(128)} %r_2_.4) | copy-start | bytes 1156
  57.4 15.0 %collective-permute-start.4 = (bf16[36,64,128]{2,1,0:T(8,128)(2,1)S(1)}, bf16[36,64,128]{2,1,0:T(8,128)(2,1)S(1)}, u32[]{:S(2)}, u32[]{:S(2)}) collective-permute-start(bf16[36,64,128]{2,1,0:T(8,128)(2,1)S(1)} %get-tuple-element.21.r_4_), channel_id=1, source_target_pairs={{0,192},{64,0},{128,64},{192,128},{1,193},{65,1},{129,65},{193,129... | collective-permute-start | bytes 1769480 | tf_op jit(solution)/shard_map/ppermute | solution.py:261
  60.1 16.5 %collective-permute-start.3 = (bf16[36,64,128]{2,1,0:T(8,128)(2,1)S(1)}, bf16[36,64,128]{2,1,0:T(8,128)(2,1)S(1)}, u32[]{:S(2)}, u32[]{:S(2)}) collective-permute-start(bf16[36,64,128]{2,1,0:T(8,128)(2,1)S(1)} %get-tuple-element.21.r_4_), channel_id=1, source_target_pairs={{0,64},{64,128},{128,192},{192,0},{1,65},{65,129},{129,193},{193,1... | collective-permute-start | bytes 1769480 | tf_op jit(solution)/shard_map/ppermute | solution.py:261
  73.2 13.9 %collective-permute-start.6 = (bf16[18,64,128]{2,1,0:T(8,128)(2,1)}, bf16[18,64,128]{2,1,0:T(8,128)(2,1)S(1)}, u32[]{:S(2)}, u32[]{:S(2)}) collective-permute-start(bf16[18,64,128]{2,1,0:T(8,128)(2,1)} %slice.17), channel_id=1, source_target_pairs={{0,192},{64,0},{128,64},{192,128},{1,193},{65,1},{129,65},{193,129... | collective-permute-start | bytes 884744 | tf_op jit(solution)/shard_map/ppermute | solution.py:261
  77.3 9.8 %collective-permute-start.5 = (bf16[18,64,128]{2,1,0:T(8,128)(2,1)}, bf16[18,64,128]{2,1,0:T(8,128)(2,1)S(1)}, u32[]{:S(2)}, u32[]{:S(2)}) collective-permute-start(bf16[18,64,128]{2,1,0:T(8,128)(2,1)} %slice.16), channel_id=1, source_target_pairs={{0,64},{64,128},{128,192},{192,0},{1,65},{65,129},{129,193},{193,1... | collective-permute-start | bytes 884744 | tf_op jit(solution)/shard_map/ppermute | solution.py:261
  78.3 6.3 %collective-permute-start.7 = (bf16[4,64,512]{2,1,0:T(8,128)(2,1)S(1)}, bf16[4,64,512]{2,1,0:T(8,128)(2,1)S(1)}, u32[]{:S(2)}, u32[]{:S(2)}) collective-permute-start(bf16[4,64,512]{2,1,0:T(8,128)(2,1)S(1)} %slice.18), channel_id=1, source_target_pairs={{0,63},{1,0},{2,1},{3,2},{4,3},{5,4},{6,5},{7,6},{8,7},{9,8},{10,9... | collective-permute-start | bytes 786440 | tf_op jit(solution)/shard_map/ppermute | solution.py:261
  84.6 1.6 %copy-start.4 = (bf16[256,4096]{1,0:T(8,128)(2,1)S(1)}, bf16[256,4096]{1,0:T(8,128)(2,1)}, u32[]{:S(2)}) copy-start(bf16[256,4096]{1,0:T(8,128)(2,1)} %all-gather.3.cloned.1.call-done) | copy-start | bytes 6291460
Sparse Core Ops, SparseCore 0:
  9.8 37.2 all-gather.2

commit v2 on v1

v2 whole, which is shorter than its diff:
```python
import math

import jax
import jax.numpy as jnp
from jax import lax
from jax.experimental import pallas as pl
from jax.experimental.pallas import tpu as pltpu
from jax.sharding import PartitionSpec as P

BLOCK = 128
NB_DEV = 32
H = 4
UNROLL = 8
MIN_GROUND = 0.5
F32 = jnp.float32
BF16 = jnp.bfloat16
VMEM = pl.BlockSpec(memory_space=pltpu.VMEM)
SMEM = pl.BlockSpec(memory_space=pltpu.SMEM)
ANY = pl.BlockSpec(memory_space=pl.ANY)
EXT = NB_DEV + H
TRASH = EXT
HEAD = 8

NT = (((1,), (1,)), ((), ()))
NN = (((1,), (0,)), ((), ()))


def dot(a, b, dims):
    return lax.dot_general(a, b, dims, preferred_element_type=F32)


def cols_of(block, width=BLOCK):
    return slice(block * BLOCK, block * BLOCK + width)


def local_ends(rows_ref, cols_ref, slot, blocks_all):
    row = rows_ref[slot] & (NB_DEV - 1)
    ahead = (cols_ref[slot] - rows_ref[slot]) & (blocks_all - 1)
    return row, row + ahead


def steps(count, slots):
    return jnp.minimum((count + UNROLL - 1) // UNROLL, slots // UNROLL)


def sort_tiles(blocks_all, rows_ref, cols_ref, count, lists_ref):
    slots = rows_ref.shape[0]
    room = slots + UNROLL
    none = TRASH | (TRASH << 8)

    def body(slot, sizes):
        inside, crossing, edge = sizes
        row = rows_ref[slot] & (NB_DEV - 1)
        col = row + ((cols_ref[slot] - rows_ref[slot]) & (blocks_all - 1))
        packed = row | (col << 8) | (slot << 16)
        is_in = (row >= H) & (row < NB_DEV - H) & (col < NB_DEV - H)
        lists_ref[HEAD + inside] = packed
        lists_ref[HEAD + room + crossing] = packed
        lists_ref[HEAD + 2 * room + edge] = packed
        one = is_in.astype(jnp.int32)
        return inside + one, crossing + (col >= NB_DEV).astype(jnp.int32), edge + 1 - one

    zero = jnp.int32(0)
    sizes = lax.fori_loop(0, count, body, (zero, zero, zero))
    for k in range(3):
        lists_ref[k] = sizes[k]
        for u in range(UNROLL):
            lists_ref[HEAD + k * room + sizes[k] + u] = none


def listed(lists_ref, k, body, carry):
    room = (lists_ref.shape[0] - HEAD) // 3

    def group(step, carry):
        tiles = []
        for u in range(UNROLL):
            packed = lists_ref[HEAD + k * room + step * UNROLL + u]
            tiles.append((packed & 255, (packed >> 8) & 255, packed >> 16))
        return body(tiles, carry)

    return lax.fori_loop(0, (lists_ref[k] + UNROLL - 1) // UNROLL, group, carry)


def first_kernel(
    blocks_all, rows_hbm, cols_hbm, count_hbm, cot_hbm, ground_hbm, tiles_hbm,
    v_ref, diag_ref, spill_ref, head_ref, cot_ref, tiles_ref, lists_ref,
    rows_ref, cols_ref, count_ref, ground_ref, w_ref, acc_ref, sems,
):
    pairs = (
        (rows_hbm, rows_ref), (cols_hbm, cols_ref), (count_hbm, count_ref),
        (cot_hbm, cot_ref), (ground_hbm, ground_ref), (tiles_hbm, tiles_ref),
    )
    copies = [pltpu.make_async_copy(src, dst, sems.at[k]) for k, (src, dst) in enumerate(pairs)]
    for copy in copies:
        copy.start()
    pats = cot_ref.shape[0]
    wide = w_ref.shape[1]
    acc_ref[...] = jnp.zeros_like(acc_ref)
    w_ref[:, pats:, :] = jnp.ones((EXT + 1, wide - pats, BLOCK), BF16)
    w_ref[NB_DEV:, :pats, :] = jnp.zeros((H + 1, pats, BLOCK), BF16)
    for copy in copies[:3]:
        copy.wait()
    count = count_ref[0]
    sort_tiles(blocks_all, rows_ref, cols_ref, count, lists_ref)
    copies[3].wait()
    for b in range(NB_DEV):
        w_ref[b, :pats, :] = cot_ref[:, cols_of(b)].astype(BF16)
    copies[4].wait()
    copies[5].wait()

    def body(step, carry):
        ends, parts = [], []
        for u in range(UNROLL):
            slot = step * UNROLL + u
            row, col = local_ends(rows_ref, cols_ref, slot, blocks_all)
            live = slot < count
            row = jnp.where(live, row, TRASH)
            col = jnp.where(live, col, TRASH)
            tile = tiles_ref[slot]
            parts.append((dot(w_ref[col], tile, NT), dot(w_ref[row], tile, NN)))
            ends.append((row, col))
        for (row, col), (forward, backward) in zip(ends, parts):
            acc_ref[row] += forward
            acc_ref[col] += backward
        return carry

    lax.fori_loop(0, steps(count, tiles_ref.shape[0]), body, 0)
    for b in range(NB_DEV):
        diag = ground_ref[b : b + 1, :] + acc_ref[b, pats : pats + 1, :]
        c = cot_ref[:, cols_of(b)]
        value = diag * c - acc_ref[b, :pats, :]
        v_ref[b] = value
        diag_ref[b] = jnp.broadcast_to(diag, (8, BLOCK))
        if b < H:
            head_ref[b] = c
            head_ref[H + b] = value
    for b in range(H):
        spill_ref[b] = acc_ref[NB_DEV + b, : pats + 8, :]


def split(value):
    high = value.astype(BF16)
    low = (value - high.astype(F32)).astype(BF16)
    return jnp.concatenate([high, low], axis=0)


def quadratic(lists_ref, k, tiles_ref, exact_ref, pair_ref):
    pats = exact_ref.shape[1]

    def body(tiles, total):
        for row, col, slot in tiles:
            both = dot(pair_ref[col], tiles_ref[slot], NT)
            total = total + (both[:pats] + both[pats:]) * exact_ref[row]
        return total

    return listed(lists_ref, k, body, jnp.zeros((pats, BLOCK), F32))


def inner_kernel(lists_ref, cot_ref, v_ref, diag_ref, tiles_ref, sums_ref, exact_ref, pair_ref):
    pats = cot_ref.shape[0]
    zero = jnp.zeros((pats, BLOCK), F32)
    m0, m1, m2, m3 = zero, zero, zero, zero
    for b in range(NB_DEV):
        c = cot_ref[:, cols_of(b)]
        m0 = m0 + c * c
        if H <= b < NB_DEV - H:
            v = v_ref[b]
            m1 = m1 + c * v
            m2 = m2 + v * v
            m3 = m3 + diag_ref[b, 0:1, :] * (v * v)
            exact_ref[b] = v
            pair_ref[b] = split(v)
    exact_ref[TRASH] = zero
    pair_ref[TRASH] = jnp.zeros((2 * pats, BLOCK), BF16)
    sums_ref[0] = m0
    sums_ref[1] = m1
    sums_ref[2] = m2
    sums_ref[3] = m3 - 2.0 * quadratic(lists_ref, 0, tiles_ref, exact_ref, pair_ref)


def outer_kernel(
    lists_ref, cot_ref, v_ref, diag_ref, tiles_ref, spill_ref, before_ref, after_ref, sums_ref,
    edges_ref, moments_ref, exact_ref, pair_ref, halo_ref, cross_ref,
):
    pats = cot_ref.shape[0]
    zero = jnp.zeros((pats, BLOCK), F32)
    for b in range(H):
        halo_ref[b] = after_ref[b].astype(BF16)
        cross_ref[b] = zero
    halo_ref[H] = jnp.zeros((pats, BLOCK), BF16)
    cross_ref[H] = zero

    def body(tiles, carry):
        parts = [dot(halo_ref[col - NB_DEV], tiles_ref[slot], NT) for row, col, slot in tiles]
        for (row, col, slot), part in zip(tiles, parts):
            cross_ref[jnp.minimum(row - (NB_DEV - H), H)] += part
        return carry

    listed(lists_ref, 1, body, 0)
    m1, m2, m3 = sums_ref[1], sums_ref[2], sums_ref[3]
    for b in range(H):
        c = cot_ref[:, cols_of(b)]
        degree = before_ref[b, pats : pats + 1, :]
        v = v_ref[b] + degree * c - before_ref[b, :pats, :]
        m1 = m1 + c * v
        m2 = m2 + v * v
        m3 = m3 + (diag_ref[b, 0:1, :] + degree) * (v * v)
        edges_ref[b] = v
        last = NB_DEV - H + b
        c = cot_ref[:, cols_of(last)]
        u = v_ref[last] - cross_ref[b]
        m1 = m1 + c * u
        m2 = m2 + u * u
        m3 = m3 + diag_ref[last, 0:1, :] * (u * u)
        edges_ref[H + b] = u
        beyond = after_ref[H + b] + spill_ref[b, pats : pats + 1, :] * after_ref[b] - spill_ref[b, :pats, :]
        edges_ref[2 * H + b] = beyond
        for where, value in ((b, v), (last, u), (NB_DEV + b, beyond), (H + b, v_ref[H + b]), (last - H, v_ref[last - H])):
            exact_ref[where] = value
            pair_ref[where] = split(value)
    exact_ref[TRASH] = zero
    pair_ref[TRASH] = jnp.zeros((2 * pats, BLOCK), BF16)
    m3 = m3 - 2.0 * quadratic(lists_ref, 2, tiles_ref, exact_ref, pair_ref)
    low = jnp.sum(jnp.concatenate([sums_ref[0], m1], axis=0).T, axis=0, keepdims=True)
    high = jnp.sum(jnp.concatenate([m2, m3], axis=0).T, axis=0, keepdims=True)
    devices = moments_ref.shape[0]
    moments_ref[:, :, :BLOCK] = jnp.broadcast_to(low[None], (devices, 1, BLOCK))
    moments_ref[:, :, BLOCK:] = jnp.broadcast_to(high[None], (devices, 1, BLOCK))


def combine_kernel(all_ref, cot_ref, after_ref, v_ref, edges_ref, adjoint_ref, lam_ref):
    pats = cot_ref.shape[0]
    total = jnp.sum(all_ref[...], axis=0)
    low = jnp.broadcast_to(total[:, :BLOCK], (8, BLOCK)).T
    high = jnp.broadcast_to(total[:, BLOCK:], (8, BLOCK)).T
    m0, m1, m2, m3 = low[:pats], low[pats:], high[:pats], high[pats:]
    alpha = m0 / m1
    norm = jnp.maximum(alpha * alpha * m2 - m0, 0.0)
    grown = 1.0 + norm / m0
    curvature = alpha * alpha * m3 - grown * grown * m1
    positive = curvature > 0.0
    second = jnp.where(positive, norm / jnp.where(positive, curvature, 1.0), 0.0)
    second = jnp.minimum(second, 1.0 / MIN_GROUND)
    on_c = jnp.broadcast_to((alpha + second * grown)[:, 0:1], (pats, BLOCK))
    on_v = jnp.broadcast_to((-alpha * second)[:, 0:1], (pats, BLOCK))
    for b in range(NB_DEV):
        if b < H:
            v = edges_ref[b]
        elif b < NB_DEV - H:
            v = v_ref[b]
        else:
            v = edges_ref[2 * H + b - NB_DEV]
        value = on_c * cot_ref[:, cols_of(b)] + on_v * v
        adjoint_ref[:, cols_of(b)] = value
        lam_ref[b] = value.astype(BF16)
    for b in range(H):
        lam_ref[NB_DEV + b] = (on_c * after_ref[b] + on_v * edges_ref[2 * H + b]).astype(BF16)


def chosen(part):
    i = lax.broadcasted_iota(jnp.int32, (BLOCK // 4, BLOCK), 0)
    j = lax.broadcasted_iota(jnp.int32, (BLOCK // 4, BLOCK), 1)
    return jnp.where(j == i + part * (BLOCK // 4), 1.0, 0.0).astype(BF16)


def volt_kernel(
    part_ref, own_hbm, below_hbm, above_hbm, opposite_hbm, far_hbm, volt_ref, turned_ref, near_ref, far_ref, sems
):
    sources = (own_hbm, below_hbm, above_hbm, opposite_hbm)
    copies = [pltpu.make_async_copy(src, near_ref.at[k], sems.at[k]) for k, src in enumerate(sources)]
    copies.append(pltpu.make_async_copy(far_hbm, far_ref, sems.at[4]))
    for copy in copies:
        copy.start()
    for copy in copies:
        copy.wait()
    pick = chosen(part_ref[0])
    pats = near_ref.shape[1]
    for k in range(4):
        for b in range(NB_DEV):
            volt_ref[b, k * pats : (k + 1) * pats, :] = near_ref[k, :, cols_of(b)]
        for b in range(H):
            volt_ref[NB_DEV + b, k * pats : (k + 1) * pats, :] = far_ref[k, :, cols_of(b)]
    for b in range(NB_DEV):
        turned_ref[b] = dot(pick, volt_ref[b], NT).astype(BF16)


def grads_kernel(
    blocks_all, scale, part_ref, rows_ref, cols_ref, count_ref, own_ref, below_ref, above_ref, opp0_ref, opp1_ref,
    volt_ref, turned_ref, grads_ref, lam_ref, lamt_ref, prow_ref, pcol_ref,
):
    pats = own_ref.shape[1]
    part = part_ref[0]
    pick = chosen(part)
    count = count_ref[0]
    half = opp0_ref.shape[0]
    rows_out = grads_ref.shape[1]
    for b in range(EXT):
        lam_ref[b, :pats, :] = own_ref[b]
        lam_ref[b, pats : 2 * pats, :] = below_ref[b]
        lam_ref[b, 2 * pats : 3 * pats, :] = above_ref[b]
        lam_ref[b, 3 * pats :, :] = opp0_ref[b] if b < half else opp1_ref[b - half]
    for b in range(EXT):
        prow_ref[b] = jnp.sum(lam_ref[b].astype(F32) * volt_ref[b].astype(F32), axis=0, keepdims=True)
    for b in range(NB_DEV):
        turned = dot(pick, lam_ref[b], NT)
        lamt_ref[b] = turned.astype(BF16)
        column = jnp.sum(turned * turned_ref[b].astype(F32), axis=1, keepdims=True)
        pcol_ref[b] = jnp.broadcast_to(column, (rows_out, BLOCK))
    grads_ref[...] = jnp.zeros_like(grads_ref)

    def body(step, carry):
        outs = []
        for u in range(UNROLL):
            slot = step * UNROLL + u
            row, col = local_ends(rows_ref, cols_ref, slot, blocks_all)
            cross = dot(lamt_ref[row], volt_ref[col], NN) + dot(turned_ref[row], lam_ref[col], NN)
            value = (cross - pcol_ref[row] - prow_ref[col]) * scale
            outs.append(jnp.where(slot < count, value, 0.0).astype(BF16))
        for u in range(UNROLL):
            grads_ref[step * UNROLL + u] = outs[u]
        return carry

    lax.fori_loop(0, steps(count, grads_ref.shape[0]), body, 0)


def shifted(shard, axis, by):
    size = lax.axis_size(axis)
    return lax.ppermute(shard, axis, [(i, (i + by) % size) for i in range(size)])


def in_hbm(x):
    return pltpu.with_memory_space_constraint(x, pltpu.HBM)


def call(kernel, name, outs, specs, scratch, *args, cost=0, last=VMEM):
    return pl.pallas_call(
        kernel,
        name=name,
        out_shape=[jax.ShapeDtypeStruct(s, d) for s, d in outs],
        in_specs=specs,
        out_specs=[VMEM] * (len(outs) - 1) + [last],
        scratch_shapes=scratch,
        compiler_params=pltpu.CompilerParams(vmem_limit_bytes=24 * 1024 * 1024),
        cost_estimate=pl.CostEstimate(flops=cost, bytes_accessed=4 * 1024 * 1024, transcendentals=0),
    )(*args)


def per_device(voltages, cotangent, ground, tile_values, tile_rows, tile_cols, tile_count):
    pats = voltages.shape[0]
    slots = tile_values.shape[0]
    devices = lax.axis_size("blk")
    parts = lax.axis_size("pat")
    blocks_all = NB_DEV * devices
    wide = pats + 16
    part = lax.axis_index("pat").astype(jnp.int32).reshape(1)
    meta = (tile_rows, tile_cols, tile_count)
    field = (NB_DEV, pats, BLOCK)
    edge = (H, pats, BLOCK)
    rows_out = BLOCK // parts

    below_v = shifted(voltages, "pat", 1)
    above_v = shifted(voltages, "pat", -1)
    opposite_v = shifted(voltages, "pat", 2)
    v, diag, spill, head, cot, tiles, lists = call(
        lambda *r: first_kernel(blocks_all, *r), "first_product",
        [
            (field, F32), ((NB_DEV, 8, BLOCK), F32), ((H, pats + 8, BLOCK), F32), ((2 * H, pats, BLOCK), F32),
            (cotangent.shape, F32), (tile_values.shape, BF16), ((HEAD + 3 * (slots + UNROLL),), jnp.int32),
        ],
        [ANY] * 6,
        [
            pltpu.SMEM((slots,), jnp.int32), pltpu.SMEM((slots,), jnp.int32), pltpu.SMEM((1,), jnp.int32),
            pltpu.VMEM((NB_DEV, BLOCK), F32),
            pltpu.VMEM((EXT + 1, wide, BLOCK), BF16), pltpu.VMEM((EXT + 1, wide, BLOCK), F32),
            pltpu.SemaphoreType.DMA((6,)),
        ],
        *meta, in_hbm(cotangent), in_hbm(ground.reshape(NB_DEV, BLOCK)), in_hbm(tile_values), last=SMEM,
    )
    before = shifted(spill, "blk", 1)
    after = shifted(head, "blk", -1)
    work = [pltpu.VMEM((EXT + 1, pats, BLOCK), F32), pltpu.VMEM((EXT + 1, 2 * pats, BLOCK), BF16)]
    (sums,) = call(
        inner_kernel, "inner_sums",
        [((4, pats, BLOCK), F32)], [SMEM] + [VMEM] * 4, work,
        lists, cot, v, diag, tiles,
    )
    edges, moments = call(
        outer_kernel, "outer_sums",
        [((3 * H, pats, BLOCK), F32), ((devices, 1, 4 * pats), F32)], [SMEM] + [VMEM] * 8,
        [*work, pltpu.VMEM((H + 1, pats, BLOCK), BF16), pltpu.VMEM((H + 1, pats, BLOCK), F32)],
        lists, cot, v, diag, tiles, spill, before, after, sums,
    )
    everyone = lax.all_to_all(moments, "blk", 0, 0)
    everyone, below_v, above_v, opposite_v = lax.optimization_barrier((everyone, below_v, above_v, opposite_v))
    adjoint, lam = call(
        combine_kernel, "combine",
        [(cotangent.shape, F32), ((EXT, pats, BLOCK), BF16)], [VMEM] * 5, [],
        everyone, cot, after, v, edges,
    )
    near = jnp.stack([voltages, below_v, above_v, opposite_v])[:, :, : H * BLOCK]
    far = shifted(near, "blk", -1)
    half = EXT // 2
    below = shifted(lam, "pat", 1)
    above = shifted(lam, "pat", -1)
    opp0 = shifted(below[:half], "pat", 1)
    opp1 = shifted(above[half:], "pat", -1)
    volt, turned = call(
        volt_kernel, "volt_blocks",
        [((EXT, parts * pats, BLOCK), BF16), ((NB_DEV, rows_out, parts * pats), BF16)],
        [SMEM] + [ANY] * 5,
        [
            pltpu.VMEM((parts, pats, NB_DEV * BLOCK), BF16), pltpu.VMEM((parts, pats, H * BLOCK), BF16),
            pltpu.SemaphoreType.DMA((5,)),
        ],
        part, voltages, below_v, above_v, opposite_v, far,
    )
    (grads,) = call(
        lambda *r: grads_kernel(blocks_all, 1.0 / math.sqrt(parts * pats), *r), "junction_grads",
        [((slots, rows_out, BLOCK), BF16)], [SMEM] * 4 + [VMEM] * 7,
        [
            pltpu.VMEM((EXT, parts * pats, BLOCK), BF16),
            pltpu.VMEM((NB_DEV, rows_out, parts * pats), BF16),
            pltpu.VMEM((EXT, 1, BLOCK), F32),
            pltpu.VMEM((NB_DEV, rows_out, BLOCK), F32),
        ],
        part, *meta, lam, below, above, opp0, opp1, volt, turned,
    )
    return adjoint, grads


def solution(mesh):
    return jax.shard_map(
        per_device,
        mesh=mesh,
        in_specs=(
            P("pat", "blk"),
            P("pat", "blk"),
            P("blk"),
            P("blk", None, None),
            P("blk"),
            P("blk"),
            P("blk"),
        ),
        out_specs=(P("pat", "blk"), P("blk", "pat", None)),
        check_vma=False,
    )
```

time: 98.5 us -> 79.1 us (0.80); the launches traced: 97.5 us -> 79.1 us
  between operations: 14.8 us -> 1.39 us
  local copies, waits for them, and re-layouts: 10.9 us -> 3.89 us
  Pallas kernels: 11.4 us -> 15 us
  waiting for transfers between devices: 19.5 us -> 22.2 us
  starting transfers between devices: 17.8 us -> 15.6 us
  blocking collectives: 22.2 us -> 20.3 us
    unnamed x22 -> x14, local copies, waits for them, and re-layouts: 7 us -> 2.38 us
    pallas_call x6, Pallas kernels: 11.4 us -> 15 us  [call(): pl.pallas_call(kernel, name=name, out_shape=[jax.ShapeDtypeStruct(s, d) f...]
    ppermute x8 -> x10, waiting for transfers between devices: 18.9 us -> 22.2 us  [shifted(): lax.ppermute(shard, axis, [(i, (i + by) % size) for i in range(size)])]
    ppermute x8 -> x10, starting transfers between devices: 17.8 us -> 15.6 us  [shifted(): lax.ppermute(shard, axis, [(i, (i + by) % size) for i in range(size)])]
    all_to_all x1, blocking collectives: 22.2 us -> 20.3 us  [per_device(): everyone = lax.all_to_all(moments, 'blk', 0, 0)]
    slice x2 -> x0, local copies, waits for them, and re-layouts: 1.88 us -> none  [the longest x1 0.97 us: per_device(): far = shifted(near[:, :, :H * BLOCK], 'blk', -1)]
  transfers between devices with their start and end apart: 9 -> 10, of which waited for: 3 -> 3; matrix products, arithmetic and copies ran while one was open for 5% -> 3% of each run, Pallas kernels for 8% -> 12%
where the time goes in v2:
time: 79.1 us
  waiting for transfers between devices  22.2 us (28%)
  blocking collectives  20.3 us (26%)
  starting transfers between devices  15.6 us (20%)
  Pallas kernels  15 us (19%)
  local copies, waits for them, and re-layouts  3.89 us (5%)
  between operations  1.39 us (2%)
    ppermute x10, waiting for transfers between devices, shifted(): lax.ppermute(shard, axis, [(i, (i + by) % size) for i in range(size)])  22.2 us
    all_to_all x1, blocking collectives, per_device(): everyone = lax.all_to_all(moments, 'blk', 0, 0)  20.3 us
    ppermute x10, starting transfers between devices, shifted(): lax.ppermute(shard, axis, [(i, (i + by) % size) for i in range(size)])  15.6 us
    pallas_call x6, Pallas kernels, call(): pl.pallas_call(kernel, name=name, out_shape=[jax.ShapeDtypeStruct(s, d) f...  15 us
    unnamed x14, local copies, waits for them, and re-layouts  2.38 us
  transfers between devices with their start and end apart: 10, of which 3 were waited for; matrix products, arithmetic and copies ran while one was open for 3% of the time, Pallas kernels for 12%

profile of v2, /device:TPU:1, one launch (start us, length us, event | category | flops | bytes accessed | tf_op | source)
XLA Modules:
  0.0 79.1 jit_solution(15245450174752552847)
XLA Ops:
  0.6 2.2 %collective-permute-start.2 = (bf16[64,4096]{1,0:T(8,128)(2,1)}, bf16[64,4096]{1,0:T(8,128)(2,1)S(1)}, u32[]{:S(2)}, u32[]{:S(2)}) collective-permute-start(bf16[64,4096]{1,0:T(8,128)(2,1)} %own_hbm.1), channel_id=1, source_target_pairs={{0,64},{64,128},{128,192},{192,0},{1,65},{65,129},{129,193},{193,1... | collective-permute-start | bytes 1572872 | tf_op jit(solution)/shard_map/ppermute | solution.py:328
  2.8 1.5 %collective-permute-start.3 = (bf16[64,4096]{1,0:T(8,128)(2,1)}, bf16[64,4096]{1,0:T(8,128)(2,1)S(1)}, u32[]{:S(2)}, u32[]{:S(2)}) collective-permute-start(bf16[64,4096]{1,0:T(8,128)(2,1)} %own_hbm.1), channel_id=1, source_target_pairs={{0,192},{64,0},{128,64},{192,128},{1,193},{65,1},{129,65},{193,129... | collective-permute-start | bytes 1572872 | tf_op jit(solution)/shard_map/ppermute | solution.py:328
  4.4 1.6 %collective-permute-start.4 = (bf16[64,4096]{1,0:T(8,128)(2,1)}, bf16[64,4096]{1,0:T(8,128)(2,1)S(1)}, u32[]{:S(2)}, u32[]{:S(2)}) collective-permute-start(bf16[64,4096]{1,0:T(8,128)(2,1)} %own_hbm.1), channel_id=1, source_target_pairs={{0,128},{64,192},{128,0},{192,64},{1,129},{65,193},{129,1},{193,65... | collective-permute-start | bytes 1572872 | tf_op jit(solution)/shard_map/ppermute | solution.py:328
  6.6 0.0 copy-start.3
  6.6 0.6 copy-done.3
  7.2 0.7 copy-done.5
  7.9 4.4 %first_product.1 = (f32[32,64,128]{2,1,0:T(8,128)S(1)}, f32[32,8,128]{2,1,0:T(8,128)S(1)}, f32[4,72,128]{2,1,0:T(8,128)S(1)}, f32[8,64,128]{2,1,0:T(8,128)S(1)},...) custom-call(s32[96]{0:T(128)S(1)} %copy-done.3, s32[96]{0:T(128)S(1)} %copy-done.5, ...), custom_call_target="tpu_custom_call" | custom-call | bytes 4194304 | tf_op jit(solution)/shard_map/first_product/pallas_call | solution.py:336
  12.3 1.6 %collective-permute-start.1 = (f32[8,64,128]{2,1,0:T(8,128)S(1)}, f32[8,64,128]{2,1,0:T(8,128)S(1)}, u32[]{:S(2)}, u32[]{:S(2)}) collective-permute-start(f32[8,64,128]{2,1,0:T(8,128)S(1)} %get-tuple-element.25), channel_id=1, source_target_pairs={{0,63},{1,0},{2,1},{3,2},{4,3},{5,4},{6,5},{7,6},{8,7},{9,8},{10,9... | collective-permute-start | bytes 786440 | tf_op jit(solution)/shard_map/ppermute | solution.py:328
  13.9 1.6 %collective-permute-start = (f32[4,72,128]{2,1,0:T(8,128)S(1)}, f32[4,72,128]{2,1,0:T(8,128)S(1)}, u32[]{:S(2)}, u32[]{:S(2)}) collective-permute-start(f32[4,72,128]{2,1,0:T(8,128)S(1)} %get-tuple-element.24.spill_ref), channel_id=1, source_target_pairs={{0,1},{1,2},{2,3},{3,4},{4,5},{5,6},{6,7},{7,8},{8,9},{9,10},{10,1... | collective-permute-start | bytes 442376 | tf_op jit(solution)/shard_map/ppermute | solution.py:328
  15.5 1.8 %inner_sums.1.sums_ref = f32[4,64,128]{2,1,0:T(8,128)S(1)} custom-call(s32[320]{0:T(512)S(1)} %get-tuple-element.19.lists_ref, f32[64,4096]{1,0:T(8,128)S(1)} %get-tuple-element.20.cot_ref, f32[32,64,128]{2,1,0:T(8,128)S(1)} %get-tuple-element.21.v_ref, f32[32,8,128]{2,1,0:T(8,128)S(1)} %get-tuple-element.22.diag_ref, ...), custom_call_target="tpu_custom_call" | custom-call | bytes 4194304 | tf_op jit(solution)/shard_map/inner_sums/pallas_call | solution.py:336
  17.3 4.5 %collective-permute-done.before_ref = f32[4,72,128]{2,1,0:T(8,128)S(1)} collective-permute-done((f32[4,72,128]{2,1,0:T(8,128)S(1)}, f32[4,72,128]{2,1,0:T(8,128)S(1)}, u32[]{:S(2)}, u32[]{:S(2)}) %collective-permute-start) | collective-permute-done | bytes 147488 | tf_op jit(solution)/shard_map/ppermute | solution.py:328
  21.8 0.0 collective-permute-done.1.after_ref
  21.8 1.8 %outer_sums.1 = (f32[12,64,128]{2,1,0:T(8,128)S(1)}, f32[64,1,256]{2,1,0:T(1,128)S(1)}) custom-call(s32[320]{0:T(512)S(1)} %get-tuple-element.19.lists_ref, f32[64,4096]{1,0:T(8,128)S(1)} %get-tuple-element.20.cot_ref, f32[32,64,128]{2,1,0:T(8,128)S(1)} %get-tuple-element.21.v_ref, f32[32,8,128]{2,1,0:T(8,128)S(1)} %get-tuple-element.22.diag_ref, ...), custom_call_target="tpu_custom_call" | custom-call | bytes 4194304 | tf_op jit(solution)/shard_map/outer_sums/pallas_call | solution.py:336
  23.6 0.0 copy-start
  23.6 20.3 %all_to_all.5.all_ref = f32[64,1,256]{2,1,0:T(1,128)S(1)} all-to-all(f32[64,1,256]{2,1,0:T(1,128)S(1)} %get-tuple-element.26), channel_id=1, replica_groups=mesh['pat'=4,'blk'=64] {'blk'}, dimensions={0} | all-to-all | bytes 131072 | tf_op jit(solution)/shard_map/all_to_all | solution.py:393
  43.9 1.5 %combine.1 = (f32[64,4096]{1,0:T(8,128)}, bf16[36,64,128]{2,1,0:T(8,128)(2,1)S(1)}) custom-call(f32[64,1,256]{2,1,0:T(1,128)S(1)} %all_to_all.5.all_ref, f32[64,4096]{1,0:T(8,128)S(1)} %get-tuple-element.20.cot_ref, f32[8,64,128]{2,1,0:T(8,128)S(1)} %collective-permute-done.1.after_ref, f32[32,64,128]{2,1,0:T(8,128)S(1)} %get-tuple-element.21.v_ref, ...), custom_call_target="tpu_custom_call" | custom-call | bytes 4194304 | tf_op jit(solution)/shard_map/combine/pallas_call | solution.py:336
  45.4 0.4 collective-permute-start.5
  45.8 2.3 %collective-permute-start.6 = (bf16[36,64,128]{2,1,0:T(8,128)(2,1)S(1)}, bf16[36,64,128]{2,1,0:T(8,128)(2,1)S(1)}, u32[]{:S(2)}, u32[]{:S(2)}) collective-permute-start(bf16[36,64,128]{2,1,0:T(8,128)(2,1)S(1)} %get-tuple-element.30.r_4_), channel_id=1, source_target_pairs={{0,192},{64,0},{128,64},{192,128},{1,193},{65,1},{129,65},{193,129... | collective-permute-start | bytes 1769480 | tf_op jit(solution)/shard_map/ppermute | solution.py:328
  48.1 13.0 %collective-permute-done.5.r_5_ = bf16[36,64,128]{2,1,0:T(8,128)(2,1)S(1)} collective-permute-done((bf16[36,64,128]{2,1,0:T(8,128)(2,1)S(1)}, bf16[36,64,128]{2,1,0:T(8,128)(2,1)S(1)}, u32[]{:S(2)}, u32[]{:S(2)}) %collective-permute-start.5) | collective-permute-done | bytes 589856 | tf_op jit(solution)/shard_map/ppermute | solution.py:328
  61.1 0.7 slice.12
  61.9 0.0 collective-permute-start.7
  61.9 0.0 collective-permute-done.6.r_6_
  61.9 0.8 slice.13
  62.7 2.7 %collective-permute-start.8 = (bf16[18,64,128]{2,1,0:T(8,128)(2,1)}, bf16[18,64,128]{2,1,0:T(8,128)(2,1)}, u32[]{:S(2)}, u32[]{:S(2)}) collective-permute-start(bf16[18,64,128]{2,1,0:T(8,128)(2,1)} %slice.13), channel_id=1, source_target_pairs={{0,192},{64,0},{128,64},{192,128},{1,193},{65,1},{129,65},{193,129... | collective-permute-start | bytes 884744 | tf_op jit(solution)/shard_map/ppermute | solution.py:328
  65.3 0.7 pad_maximum_fusion
  66.1 1.8 %collective-permute-start.9 = (bf16[4,64,512]{2,1,0:T(8,128)(2,1)}, bf16[4,64,512]{2,1,0:T(8,128)(2,1)S(1)}, u32[]{:S(2)}, u32[]{:S(2)}) collective-permute-start(bf16[4,64,512]{2,1,0:T(8,128)(2,1)} %pad_maximum_fusion), channel_id=1, source_target_pairs={{0,63},{1,0},{2,1},{3,2},{4,3},{5,4},{6,5},{7,6},{8,7},{9,8},{10,9... | collective-permute-start | bytes 786440 | tf_op jit(solution)/shard_map/ppermute | solution.py:328
  67.9 4.7 %collective-permute-done.9.far_hbm = bf16[4,64,512]{2,1,0:T(8,128)(2,1)S(1)} collective-permute-done((bf16[4,64,512]{2,1,0:T(8,128)(2,1)}, bf16[4,64,512]{2,1,0:T(8,128)(2,1)S(1)}, u32[]{:S(2)}, u32[]{:S(2)}) %collective-permute-start.9) | collective-permute-done | bytes 262176 | tf_op jit(solution)/shard_map/ppermute | solution.py:328
  72.5 1.1 %volt_blocks.1 = (bf16[36,256,128]{2,1,0:T(8,128)(2,1)S(1)}, bf16[32,32,256]{2,1,0:T(8,128)(2,1)S(1)}) custom-call(s32[1]{0:T(128)} %bitcast.1.part_ref.r_0_, bf16[64,4096]{1,0:T(8,128)(2,1)S(1)} %copy-done, bf16[64,4096]{1,0:T(8,128)(2,1)S(1)} %collective-permute-done.2.below_hbm, bf16[64,4096]{1,0:T(8,128)(2,1)S(1)} %collective-permute-done.3.above_hbm, ...), custom_call_target="tpu_custom_call" | custom-call | bytes 4194304 | tf_op jit(solution)/shard_map/volt_blocks/pallas_call | solution.py:336
  73.7 0.0 collective-permute-done.7.r_7_
  73.7 0.0 copy-start.2
  73.7 1.1 %copy-done.2 = bf16[36,64,128]{2,1,0:T(8,128)(2,1)S(1)} copy-done((bf16[36,64,128]{2,1,0:T(8,128)(2,1)S(1)}, bf16[36,64,128]{2,1,0:T(8,128)(2,1)}, u32[]{:S(2)}) %copy-start.2) | copy-done | bytes 589848
  74.8 4.3 %junction_grads.1 = bf16[96,32,128]{2,1,0:T(8,128)(2,1)} custom-call(s32[1]{0:T(128)} %bitcast.1.part_ref.r_0_, s32[96]{0:T(128)S(1)} %copy-done.4, s32[96]{0:T(128)S(1)} %copy-done.6, s32[1]{0:T(128)S(6)} %copy.9.r_2_.r_3_, bf16[36,64,128]{2,1,0:T(8,128)(2,1)S(1)} %copy-done.2, bf16[36,64,128]{2,1,0:T(8,128)(2,1)S(1)} %collective-permute-done.5.r_5_, ...), custom_call_target="tpu_custom_call" | custom-call | bytes 4194304 | tf_op jit(solution)/shard_map/junction_grads/pallas_call | solution.py:336
  (12 shorter events, 0.0 us)
Async XLA Ops:
  0.6 43.3 %collective-permute-start.2 = (bf16[64,4096]{1,0:T(8,128)(2,1)}, bf16[64,4096]{1,0:T(8,128)(2,1)S(1)}, u32[]{:S(2)}, u32[]{:S(2)}) collective-permute-start(bf16[64,4096]{1,0:T(8,128)(2,1)} %own_hbm.1), channel_id=1, source_target_pairs={{0,64},{64,128},{128,192},{192,0},{1,65},{65,129},{129,193},{193,1... | collective-permute-start | bytes 1572872 | tf_op jit(solution)/shard_map/ppermute | solution.py:328
  2.8 41.1 %collective-permute-start.3 = (bf16[64,4096]{1,0:T(8,128)(2,1)}, bf16[64,4096]{1,0:T(8,128)(2,1)S(1)}, u32[]{:S(2)}, u32[]{:S(2)}) collective-permute-start(bf16[64,4096]{1,0:T(8,128)(2,1)} %own_hbm.1), channel_id=1, source_target_pairs={{0,192},{64,0},{128,64},{192,128},{1,193},{65,1},{129,65},{193,129... | collective-permute-start | bytes 1572872 | tf_op jit(solution)/shard_map/ppermute | solution.py:328
  4.4 39.5 %collective-permute-start.4 = (bf16[64,4096]{1,0:T(8,128)(2,1)}, bf16[64,4096]{1,0:T(8,128)(2,1)S(1)}, u32[]{:S(2)}, u32[]{:S(2)}) collective-permute-start(bf16[64,4096]{1,0:T(8,128)(2,1)} %own_hbm.1), channel_id=1, source_target_pairs={{0,128},{64,192},{128,0},{192,64},{1,129},{65,193},{129,1},{193,65... | collective-permute-start | bytes 1572872 | tf_op jit(solution)/shard_map/ppermute | solution.py:328
  6.6 0.7 copy-start.3
  7.2 0.7 copy-start.5
  12.3 9.5 %collective-permute-start.1 = (f32[8,64,128]{2,1,0:T(8,128)S(1)}, f32[8,64,128]{2,1,0:T(8,128)S(1)}, u32[]{:S(2)}, u32[]{:S(2)}) collective-permute-start(f32[8,64,128]{2,1,0:T(8,128)S(1)} %get-tuple-element.25), channel_id=1, source_target_pairs={{0,63},{1,0},{2,1},{3,2},{4,3},{5,4},{6,5},{7,6},{8,7},{9,8},{10,9... | collective-permute-start | bytes 786440 | tf_op jit(solution)/shard_map/ppermute | solution.py:328
  13.9 7.9 %collective-permute-start = (f32[4,72,128]{2,1,0:T(8,128)S(1)}, f32[4,72,128]{2,1,0:T(8,128)S(1)}, u32[]{:S(2)}, u32[]{:S(2)}) collective-permute-start(f32[4,72,128]{2,1,0:T(8,128)S(1)} %get-tuple-element.24.spill_ref), channel_id=1, source_target_pairs={{0,1},{1,2},{2,3},{3,4},{4,5},{5,6},{6,7},{7,8},{8,9},{9,10},{10,1... | collective-permute-start | bytes 442376 | tf_op jit(solution)/shard_map/ppermute | solution.py:328
  23.6 41.7 %copy-start = (bf16[64,4096]{1,0:T(8,128)(2,1)S(1)}, bf16[64,4096]{1,0:T(8,128)(2,1)}, u32[]{:S(2)}) copy-start(bf16[64,4096]{1,0:T(8,128)(2,1)} %own_hbm.1) | copy-start | bytes 1572868
  45.4 16.5 %copy-start.1 = (bf16[36,64,128]{2,1,0:T(8,128)(2,1)}, bf16[36,64,128]{2,1,0:T(8,128)(2,1)S(1)}, u32[]{:S(2)}) copy-start(bf16[36,64,128]{2,1,0:T(8,128)(2,1)S(1)} %get-tuple-element.30.r_4_) | copy-start | bytes 1769476
  45.4 28.3 %copy-start.4 = (s32[96]{0:T(128)S(1)}, s32[96]{0:T(128)}, u32[]{:S(2)}) copy-start(s32[96]{0:T(128)} %r_1_.3) | copy-start | bytes 1156
  45.4 28.3 %copy-start.6 = (s32[96]{0:T(128)S(1)}, s32[96]{0:T(128)}, u32[]{:S(2)}) copy-start(s32[96]{0:T(128)} %r_2_.2) | copy-start | bytes 1156
  45.4 15.7 %collective-permute-start.5 = (bf16[36,64,128]{2,1,0:T(8,128)(2,1)S(1)}, bf16[36,64,128]{2,1,0:T(8,128)(2,1)S(1)}, u32[]{:S(2)}, u32[]{:S(2)}) collective-permute-start(bf16[36,64,128]{2,1,0:T(8,128)(2,1)S(1)} %get-tuple-element.30.r_4_), channel_id=1, source_target_pairs={{0,64},{64,128},{128,192},{192,0},{1,65},{65,129},{129,193},{193,1... | collective-permute-start | bytes 1769480 | tf_op jit(solution)/shard_map/ppermute | solution.py:328
  45.8 16.1 %collective-permute-start.6 = (bf16[36,64,128]{2,1,0:T(8,128)(2,1)S(1)}, bf16[36,64,128]{2,1,0:T(8,128)(2,1)S(1)}, u32[]{:S(2)}, u32[]{:S(2)}) collective-permute-start(bf16[36,64,128]{2,1,0:T(8,128)(2,1)S(1)} %get-tuple-element.30.r_4_), channel_id=1, source_target_pairs={{0,192},{64,0},{128,64},{192,128},{1,193},{65,1},{129,65},{193,129... | collective-permute-start | bytes 1769480 | tf_op jit(solution)/shard_map/ppermute | solution.py:328
  61.9 11.8 %collective-permute-start.7 = (bf16[18,64,128]{2,1,0:T(8,128)(2,1)}, bf16[18,64,128]{2,1,0:T(8,128)(2,1)}, u32[]{:S(2)}, u32[]{:S(2)}) collective-permute-start(bf16[18,64,128]{2,1,0:T(8,128)(2,1)} %slice.12), channel_id=1, source_target_pairs={{0,64},{64,128},{128,192},{192,0},{1,65},{65,129},{129,193},{193,1... | collective-permute-start | bytes 884744 | tf_op jit(solution)/shard_map/ppermute | solution.py:328
  62.7 11.0 %collective-permute-start.8 = (bf16[18,64,128]{2,1,0:T(8,128)(2,1)}, bf16[18,64,128]{2,1,0:T(8,128)(2,1)}, u32[]{:S(2)}, u32[]{:S(2)}) collective-permute-start(bf16[18,64,128]{2,1,0:T(8,128)(2,1)} %slice.13), channel_id=1, source_target_pairs={{0,192},{64,0},{128,64},{192,128},{1,193},{65,1},{129,65},{193,129... | collective-permute-start | bytes 884744 | tf_op jit(solution)/shard_map/ppermute | solution.py:328
  66.1 6.4 %collective-permute-start.9 = (bf16[4,64,512]{2,1,0:T(8,128)(2,1)}, bf16[4,64,512]{2,1,0:T(8,128)(2,1)S(1)}, u32[]{:S(2)}, u32[]{:S(2)}) collective-permute-start(bf16[4,64,512]{2,1,0:T(8,128)(2,1)} %pad_maximum_fusion), channel_id=1, source_target_pairs={{0,63},{1,0},{2,1},{3,2},{4,3},{5,4},{6,5},{7,6},{8,7},{9,8},{10,9... | collective-permute-start | bytes 786440 | tf_op jit(solution)/shard_map/ppermute | solution.py:328
  73.7 1.1 %copy-start.2 = (bf16[36,64,128]{2,1,0:T(8,128)(2,1)S(1)}, bf16[36,64,128]{2,1,0:T(8,128)(2,1)}, u32[]{:S(2)}) copy-start(bf16[36,64,128]{2,1,0:T(8,128)(2,1)} %copy-done.1) | copy-start | bytes 1769476

commit v3 on v2

v3 whole, which is shorter than its diff:
```python
import math

import jax
import jax.numpy as jnp
from jax import lax
from jax.experimental import pallas as pl
from jax.experimental.pallas import tpu as pltpu
from jax.sharding import PartitionSpec as P

BLOCK = 128
NB_DEV = 32
H = 4
UNROLL = 32
MIN_GROUND = 0.5
F32 = jnp.float32
BF16 = jnp.bfloat16
VMEM = pl.BlockSpec(memory_space=pltpu.VMEM)
SMEM = pl.BlockSpec(memory_space=pltpu.SMEM)
ANY = pl.BlockSpec(memory_space=pl.ANY)
EXT = NB_DEV + H
TRASH = EXT
HEAD = 8
LISTS = 4

NT = (((1,), (1,)), ((), ()))
NN = (((1,), (0,)), ((), ()))


def dot(a, b, dims):
    return lax.dot_general(a, b, dims, preferred_element_type=F32)


def cols_of(block, width=BLOCK):
    return slice(block * BLOCK, block * BLOCK + width)


def sort_tiles(blocks_all, rows_ref, cols_ref, count, lists_ref):
    room = (lists_ref.shape[0] - HEAD) // LISTS
    none = TRASH | (TRASH << 8)

    def body(slot, sizes):
        inside, crossing, edge = sizes
        row = rows_ref[slot] & (NB_DEV - 1)
        col = row + ((cols_ref[slot] - rows_ref[slot]) & (blocks_all - 1))
        packed = row | (col << 8) | (slot << 16)
        is_in = (row >= H) & (row < NB_DEV - H) & (col < NB_DEV - H)
        lists_ref[HEAD + inside] = packed
        lists_ref[HEAD + room + crossing] = packed
        lists_ref[HEAD + 2 * room + edge] = packed
        lists_ref[HEAD + 3 * room + slot] = packed
        one = is_in.astype(jnp.int32)
        return inside + one, crossing + (col >= NB_DEV).astype(jnp.int32), edge + 1 - one

    zero = jnp.int32(0)
    sizes = (*lax.fori_loop(0, count, body, (zero, zero, zero)), count)
    for k in range(LISTS):
        lists_ref[k] = sizes[k]
        for u in range(UNROLL):
            lists_ref[HEAD + k * room + sizes[k] + u] = none


def listed(lists_ref, k, body, carry, unroll=UNROLL):
    room = (lists_ref.shape[0] - HEAD) // LISTS

    def group(step, carry):
        tiles = []
        for u in range(unroll):
            packed = lists_ref[HEAD + k * room + step * unroll + u]
            tiles.append((packed & 255, (packed >> 8) & 255, packed >> 16))
        return body(step * unroll, tiles, carry)

    return lax.fori_loop(0, (lists_ref[k] + unroll - 1) // unroll, group, carry)


def first_kernel(
    blocks_all, rows_hbm, cols_hbm, count_hbm, cot_hbm, ground_hbm, tiles_hbm,
    v_ref, diag_ref, spill_ref, head_ref, cot_ref, tiles_ref, lists_ref,
    rows_ref, cols_ref, count_ref, ground_ref, w_ref, acc_ref, sems,
):
    pairs = (
        (rows_hbm, rows_ref), (cols_hbm, cols_ref), (count_hbm, count_ref),
        (cot_hbm, cot_ref), (ground_hbm, ground_ref), (tiles_hbm, tiles_ref),
    )
    copies = [pltpu.make_async_copy(src, dst, sems.at[k]) for k, (src, dst) in enumerate(pairs)]
    for copy in copies:
        copy.start()
    pats = cot_ref.shape[0]
    wide = w_ref.shape[1]
    acc_ref[...] = jnp.zeros_like(acc_ref)
    w_ref[:, pats:, :] = jnp.ones((EXT + 1, wide - pats, BLOCK), BF16)
    w_ref[NB_DEV:, :pats, :] = jnp.zeros((H + 1, pats, BLOCK), BF16)
    for copy in copies[:3]:
        copy.wait()
    count = count_ref[0]
    sort_tiles(blocks_all, rows_ref, cols_ref, count, lists_ref)
    copies[3].wait()
    for b in range(NB_DEV):
        w_ref[b, :pats, :] = cot_ref[:, cols_of(b)].astype(BF16)
    copies[4].wait()
    copies[5].wait()

    kept = acc_ref.shape[1]

    def body(first, tiles, carry):
        parts = []
        for row, col, slot in tiles:
            tile = tiles_ref[slot]
            parts.append((dot(w_ref[col], tile, NT)[:kept], dot(w_ref[row], tile, NN)[:kept]))
        for (row, col, slot), (forward, backward) in zip(tiles, parts):
            acc_ref[row] += forward
            acc_ref[col] += backward
        return carry

    listed(lists_ref, 3, body, 0)
    for b in range(NB_DEV):
        diag = ground_ref[b : b + 1, :] + acc_ref[b, pats : pats + 1, :]
        c = cot_ref[:, cols_of(b)]
        value = diag * c - acc_ref[b, :pats, :]
        v_ref[b] = value
        diag_ref[b] = jnp.broadcast_to(diag, (8, BLOCK))
        if b < H:
            head_ref[b] = c
            head_ref[H + b] = value
    for b in range(H):
        spill_ref[b] = acc_ref[NB_DEV + b]


def split(value):
    high = value.astype(BF16)
    low = (value - high.astype(F32)).astype(BF16)
    return jnp.concatenate([high, low], axis=0)


def quadratic(lists_ref, k, tiles_ref, exact_ref, pair_ref, unroll):
    pats = exact_ref.shape[1]

    def body(first, tiles, total):
        for row, col, slot in tiles:
            both = dot(pair_ref[col], tiles_ref[slot], NT)
            total = total + (both[:pats] + both[pats:]) * exact_ref[row]
        return total

    return listed(lists_ref, k, body, jnp.zeros((pats, BLOCK), F32), unroll)


def inner_kernel(lists_ref, cot_ref, v_ref, diag_ref, tiles_ref, sums_ref, exact_ref, pair_ref):
    pats = cot_ref.shape[0]
    zero = jnp.zeros((pats, BLOCK), F32)
    m0, m1, m2, m3 = zero, zero, zero, zero
    for b in range(NB_DEV):
        c = cot_ref[:, cols_of(b)]
        m0 = m0 + c * c
        if H <= b < NB_DEV - H:
            v = v_ref[b]
            m1 = m1 + c * v
            m2 = m2 + v * v
            m3 = m3 + diag_ref[b, 0:1, :] * (v * v)
            exact_ref[b] = v
            pair_ref[b] = split(v)
    exact_ref[TRASH] = zero
    pair_ref[TRASH] = jnp.zeros((2 * pats, BLOCK), BF16)
    sums_ref[0] = m0
    sums_ref[1] = m1
    sums_ref[2] = m2
    sums_ref[3] = m3 - 2.0 * quadratic(lists_ref, 0, tiles_ref, exact_ref, pair_ref, UNROLL)


def outer_kernel(
    lists_ref, cot_ref, v_ref, diag_ref, tiles_ref, spill_ref, before_ref, after_ref, sums_ref,
    edges_ref, moments_ref, exact_ref, pair_ref, halo_ref, cross_ref,
):
    pats = cot_ref.shape[0]
    zero = jnp.zeros((pats, BLOCK), F32)
    for b in range(H):
        halo_ref[b] = after_ref[b].astype(BF16)
        cross_ref[b] = zero
    halo_ref[H] = jnp.zeros((pats, BLOCK), BF16)
    cross_ref[H] = zero

    def body(first, tiles, carry):
        parts = [dot(halo_ref[col - NB_DEV], tiles_ref[slot], NT) for row, col, slot in tiles]
        for (row, col, slot), part in zip(tiles, parts):
            cross_ref[jnp.minimum(row - (NB_DEV - H), H)] += part
        return carry

    listed(lists_ref, 1, body, 0, 8)
    m1, m2, m3 = sums_ref[1], sums_ref[2], sums_ref[3]
    for b in range(H):
        c = cot_ref[:, cols_of(b)]
        degree = before_ref[b, pats : pats + 1, :]
        v = v_ref[b] + degree * c - before_ref[b, :pats, :]
        m1 = m1 + c * v
        m2 = m2 + v * v
        m3 = m3 + (diag_ref[b, 0:1, :] + degree) * (v * v)
        edges_ref[b] = v
        last = NB_DEV - H + b
        c = cot_ref[:, cols_of(last)]
        u = v_ref[last] - cross_ref[b]
        m1 = m1 + c * u
        m2 = m2 + u * u
        m3 = m3 + diag_ref[last, 0:1, :] * (u * u)
        edges_ref[H + b] = u
        beyond = after_ref[H + b] + spill_ref[b, pats : pats + 1, :] * after_ref[b] - spill_ref[b, :pats, :]
        edges_ref[2 * H + b] = beyond
        for where, value in ((b, v), (last, u), (NB_DEV + b, beyond), (H + b, v_ref[H + b]), (last - H, v_ref[last - H])):
            exact_ref[where] = value
            pair_ref[where] = split(value)
    exact_ref[TRASH] = zero
    pair_ref[TRASH] = jnp.zeros((2 * pats, BLOCK), BF16)
    m3 = m3 - 2.0 * quadratic(lists_ref, 2, tiles_ref, exact_ref, pair_ref, 16)
    low = jnp.sum(jnp.concatenate([sums_ref[0], m1], axis=0).T, axis=0, keepdims=True)
    high = jnp.sum(jnp.concatenate([m2, m3], axis=0).T, axis=0, keepdims=True)
    devices = moments_ref.shape[0]
    moments_ref[:, :, :BLOCK] = jnp.broadcast_to(low[None], (devices, 1, BLOCK))
    moments_ref[:, :, BLOCK:] = jnp.broadcast_to(high[None], (devices, 1, BLOCK))


def combine_kernel(all_ref, cot_ref, after_ref, v_ref, edges_ref, adjoint_ref, low_ref, high_ref):
    pats = cot_ref.shape[0]
    total = jnp.sum(all_ref[...], axis=0)
    low = jnp.broadcast_to(total[:, :BLOCK], (8, BLOCK)).T
    high = jnp.broadcast_to(total[:, BLOCK:], (8, BLOCK)).T
    m0, m1, m2, m3 = low[:pats], low[pats:], high[:pats], high[pats:]
    alpha = m0 / m1
    norm = jnp.maximum(alpha * alpha * m2 - m0, 0.0)
    grown = 1.0 + norm / m0
    curvature = alpha * alpha * m3 - grown * grown * m1
    positive = curvature > 0.0
    second = jnp.where(positive, norm / jnp.where(positive, curvature, 1.0), 0.0)
    second = jnp.minimum(second, 1.0 / MIN_GROUND)
    on_c = jnp.broadcast_to((alpha + second * grown)[:, 0:1], (pats, BLOCK))
    on_v = jnp.broadcast_to((-alpha * second)[:, 0:1], (pats, BLOCK))
    half = low_ref.shape[0]
    for b in range(NB_DEV):
        if b < H:
            v = edges_ref[b]
        elif b < NB_DEV - H:
            v = v_ref[b]
        else:
            v = edges_ref[2 * H + b - NB_DEV]
        value = on_c * cot_ref[:, cols_of(b)] + on_v * v
        adjoint_ref[:, cols_of(b)] = value
        if b < half:
            low_ref[b] = value.astype(BF16)
        else:
            high_ref[b - half] = value.astype(BF16)
    for b in range(H):
        high_ref[NB_DEV + b - half] = (on_c * after_ref[b] + on_v * edges_ref[2 * H + b]).astype(BF16)


def chosen(part):
    i = lax.broadcasted_iota(jnp.int32, (BLOCK // 4, BLOCK), 0)
    j = lax.broadcasted_iota(jnp.int32, (BLOCK // 4, BLOCK), 1)
    return jnp.where(j == i + part * (BLOCK // 4), 1.0, 0.0).astype(BF16)


def volt_kernel(own_hbm, below_hbm, above_hbm, opposite_hbm, far_hbm, volt_ref, near_ref, far_ref, sems):
    sources = (own_hbm, below_hbm, above_hbm, opposite_hbm)
    copies = [pltpu.make_async_copy(src, near_ref.at[k], sems.at[k]) for k, src in enumerate(sources)]
    copies.append(pltpu.make_async_copy(far_hbm, far_ref, sems.at[4]))
    for copy in copies:
        copy.start()
    for copy in copies:
        copy.wait()
    pats = near_ref.shape[1]
    for k in range(4):
        for b in range(NB_DEV):
            volt_ref[b, k * pats : (k + 1) * pats, :] = near_ref[k, :, cols_of(b)]
        for b in range(H):
            volt_ref[NB_DEV + b, k * pats : (k + 1) * pats, :] = far_ref[k, :, cols_of(b)]


def gather_fields(part, first, volt_hbm, lam_hbm, field_ref, turned_ref, prow_ref, pcol_ref, sems):
    groups = field_ref.shape[1] // BLOCK
    pats = volt_hbm.shape[1] // 4
    half = lam_hbm[0].shape[0]
    copies = []

    def copy(src, dst):
        made = pltpu.make_async_copy(src, dst, sems.at[len(copies)])
        made.start()
        copies.append(made)

    for g in range(groups):
        at = g * BLOCK
        copy(volt_hbm.at[:, pl.ds((first + g) * pats, pats), :], field_ref.at[pl.ds(0, EXT), pl.ds(at, pats), :])
        copy(lam_hbm[2 * g], field_ref.at[pl.ds(0, half), pl.ds(at + pats, pats), :])
        copy(lam_hbm[2 * g + 1], field_ref.at[pl.ds(half, EXT - half), pl.ds(at + pats, pats), :])
    for made in copies:
        made.wait()
    pick = chosen(part)
    for b in range(EXT):
        row = jnp.zeros((1, BLOCK), F32)
        for g in range(groups):
            v = field_ref[b, g * BLOCK : g * BLOCK + pats, :].astype(F32)
            m = field_ref[b, g * BLOCK + pats : (g + 1) * BLOCK, :].astype(F32)
            row = row + jnp.sum(v * m, axis=0, keepdims=True)
        prow_ref[b] = row
    for b in range(NB_DEV):
        straight = dot(pick, field_ref[b], NT)
        column = jnp.zeros((straight.shape[0], BLOCK), F32)
        for g in range(groups):
            part_of = straight[:, cols_of(g)]
            other = pltpu.roll(part_of, pats, 1)
            column = column + part_of * other
            turned_ref[b, :, cols_of(g)] = other.astype(BF16)
        column = jnp.sum(column, axis=1, keepdims=True) * 0.5
        pcol_ref[b] = jnp.broadcast_to(column, (straight.shape[0], BLOCK))
    prow_ref[TRASH] = jnp.zeros((1, BLOCK), F32)
    pcol_ref[TRASH] = jnp.zeros(pcol_ref.shape[1:], F32)
    turned_ref[TRASH] = jnp.zeros(turned_ref.shape[1:], BF16)
    field_ref[TRASH] = jnp.zeros(field_ref.shape[1:], BF16)


def early_grads_kernel(part_ref, lists_ref, volt_hbm, *refs):
    lam_hbm, (partial_ref, field_ref, turned_ref, prow_ref, pcol_ref, sems) = refs[:6], refs[6:]
    gather_fields(part_ref[0], 0, volt_hbm, lam_hbm, field_ref, turned_ref, prow_ref, pcol_ref, sems)

    def body(first, tiles, carry):
        for u, (row, col, slot) in enumerate(tiles):
            partial_ref[first + u] = dot(turned_ref[row], field_ref[col], NN) - pcol_ref[row] - prow_ref[col]
        return carry

    listed(lists_ref, 3, body, 0)


def late_grads_kernel(scale, part_ref, lists_ref, volt_hbm, low_hbm, high_hbm, partial_ref, grads_ref, *refs):
    field_ref, turned_ref, prow_ref, pcol_ref, sems = refs
    grads_ref[...] = jnp.zeros_like(grads_ref)
    gather_fields(part_ref[0], 3, volt_hbm, (low_hbm, high_hbm), field_ref, turned_ref, prow_ref, pcol_ref, sems)
    count = lists_ref[3]

    def body(first, tiles, carry):
        for u, (row, col, slot) in enumerate(tiles):
            value = partial_ref[first + u] + dot(turned_ref[row], field_ref[col], NN) - pcol_ref[row] - prow_ref[col]
            grads_ref[first + u] = jnp.where(first + u < count, value * scale, 0.0).astype(BF16)
        return carry

    listed(lists_ref, 3, body, 0)


def shifted(shard, axis, by):
    size = lax.axis_size(axis)
    return lax.ppermute(shard, axis, [(i, (i + by) % size) for i in range(size)])


def in_hbm(x):
    return pltpu.with_memory_space_constraint(x, pltpu.HBM)


def call(kernel, name, outs, specs, scratch, *args, cost=0, last=VMEM):
    return pl.pallas_call(
        kernel,
        name=name,
        out_shape=[jax.ShapeDtypeStruct(s, d) for s, d in outs],
        in_specs=specs,
        out_specs=[VMEM] * (len(outs) - 1) + [last],
        scratch_shapes=scratch,
        compiler_params=pltpu.CompilerParams(vmem_limit_bytes=24 * 1024 * 1024),
        cost_estimate=pl.CostEstimate(flops=cost, bytes_accessed=4 * 1024 * 1024, transcendentals=0),
    )(*args)


def per_device(voltages, cotangent, ground, tile_values, tile_rows, tile_cols, tile_count):
    pats = voltages.shape[0]
    slots = tile_values.shape[0]
    devices = lax.axis_size("blk")
    parts = lax.axis_size("pat")
    blocks_all = NB_DEV * devices
    wide = pats + 16
    half = EXT // 2
    part = lax.axis_index("pat").astype(jnp.int32).reshape(1)
    field = (NB_DEV, pats, BLOCK)
    edge = (H, pats, BLOCK)
    rows_out = BLOCK // parts

    v, diag, spill, head, cot, tiles, lists = call(
        lambda *r: first_kernel(blocks_all, *r), "first_product",
        [
            (field, F32), ((NB_DEV, 8, BLOCK), F32), ((H, pats + 8, BLOCK), F32), ((2 * H, pats, BLOCK), F32),
            (cotangent.shape, F32), (tile_values.shape, BF16), ((HEAD + LISTS * (slots + UNROLL),), jnp.int32),
        ],
        [ANY] * 6,
        [
            pltpu.SMEM((slots,), jnp.int32), pltpu.SMEM((slots,), jnp.int32), pltpu.SMEM((1,), jnp.int32),
            pltpu.VMEM((NB_DEV, BLOCK), F32),
            pltpu.VMEM((EXT + 1, wide, BLOCK), BF16), pltpu.VMEM((EXT + 1, pats + 8, BLOCK), F32),
            pltpu.SemaphoreType.DMA((6,)),
        ],
        in_hbm(tile_rows), in_hbm(tile_cols), tile_count,
        in_hbm(cotangent), in_hbm(ground.reshape(NB_DEV, BLOCK)), in_hbm(tile_values), last=SMEM,
    )
    spill, head, volt = lax.optimization_barrier((spill, head, voltages))
    before = shifted(spill, "blk", 1)
    after = shifted(head, "blk", -1)
    below_v = shifted(volt, "pat", 1)
    above_v = shifted(volt, "pat", -1)
    opposite_v = shifted(volt, "pat", 2)
    work = [pltpu.VMEM((EXT + 1, pats, BLOCK), F32), pltpu.VMEM((EXT + 1, 2 * pats, BLOCK), BF16)]
    (sums,) = call(
        inner_kernel, "inner_sums",
        [((4, pats, BLOCK), F32)], [SMEM] + [VMEM] * 4, work,
        lists, cot, v, diag, tiles,
    )
    edges, moments = call(
        outer_kernel, "outer_sums",
        [((3 * H, pats, BLOCK), F32), ((devices, 1, 4 * pats), F32)], [SMEM] + [VMEM] * 8,
        [*work, pltpu.VMEM((H + 1, pats, BLOCK), BF16), pltpu.VMEM((H + 1, pats, BLOCK), F32)],
        lists, cot, v, diag, tiles, spill, before, after, sums,
    )
    everyone = lax.all_to_all(moments, "blk", 0, 0)
    everyone, below_v, above_v, opposite_v = lax.optimization_barrier((everyone, below_v, above_v, opposite_v))
    adjoint, low, high = call(
        combine_kernel, "combine",
        [(cotangent.shape, F32), ((half, pats, BLOCK), BF16), ((EXT - half, pats, BLOCK), BF16)], [VMEM] * 5, [],
        everyone, cot, after, v, edges,
    )
    low_below = shifted(low, "pat", 1)
    high_above = shifted(high, "pat", -1)
    low_above = shifted(low, "pat", -1)
    high_below = shifted(high, "pat", 1)
    near = jnp.stack([voltages, below_v, above_v, opposite_v])[:, :, : H * BLOCK]
    far = shifted(near, "blk", -1)
    (volt,) = call(
        volt_kernel, "volt_blocks",
        [((EXT, parts * pats, BLOCK), BF16)], [ANY] * 5,
        [
            pltpu.VMEM((parts, pats, NB_DEV * BLOCK), BF16), pltpu.VMEM((parts, pats, H * BLOCK), BF16),
            pltpu.SemaphoreType.DMA((5,)),
        ],
        voltages, below_v, above_v, opposite_v, far,
    )
    low_below, high_above, volt = lax.optimization_barrier((low_below, high_above, volt))
    low_opposite = shifted(low_below, "pat", 1)
    high_opposite = shifted(high_above, "pat", -1)

    def grad_work(groups):
        return [
            pltpu.VMEM((EXT + 1, groups * BLOCK, BLOCK), BF16),
            pltpu.VMEM((NB_DEV + H + 1, rows_out, groups * BLOCK), BF16),
            pltpu.VMEM((EXT + 1, 1, BLOCK), F32),
            pltpu.VMEM((EXT + 1, rows_out, BLOCK), F32),
            pltpu.SemaphoreType.DMA((3 * groups,)),
        ]

    (partial,) = call(
        early_grads_kernel, "early_grads",
        [((slots, rows_out, BLOCK), F32)], [SMEM] * 2 + [ANY] * 7, grad_work(parts - 1),
        part, lists, volt, low, high, low_below, high_below, low_above, high_above,
    )
    (grads,) = call(
        lambda *r: late_grads_kernel(1.0 / math.sqrt(parts * pats), *r), "late_grads",
        [((slots, rows_out, BLOCK), BF16)], [SMEM] * 2 + [ANY] * 3 + [VMEM], grad_work(1),
        part, lists, volt, low_opposite, high_opposite, partial,
    )
    return adjoint, grads


def solution(mesh):
    return jax.shard_map(
        per_device,
        mesh=mesh,
        in_specs=(
            P("pat", "blk"),
            P("pat", "blk"),
            P("blk"),
            P("blk", None, None),
            P("blk"),
            P("blk"),
            P("blk"),
        ),
        out_specs=(P("pat", "blk"), P("blk", "pat", None)),
        check_vma=False,
    )
```

time: 79.1 us -> 71.6 us (0.905)
  waiting for transfers between devices: 22.2 us -> 10.5 us
  Pallas kernels: 15 us -> 22.2 us
  local copies, waits for them, and re-layouts: 3.89 us -> 0.01 us
  starting transfers between devices: 15.6 us -> 17.4 us
    ppermute x10 -> x12, waiting for transfers between devices: 22.2 us -> 10.5 us  [shifted(): lax.ppermute(shard, axis, [(i, (i + by) % size) for i in range(size)])]
    pallas_call x6 -> x7, Pallas kernels: 15 us -> 22.2 us  [call(): pl.pallas_call(kernel, name=name, out_shape=[jax.ShapeDtypeStruct(s, d) f...]
    unnamed x14 -> x2, local copies, waits for them, and re-layouts: 2.38 us -> 0.01 us
    ppermute x10 -> x12, starting transfers between devices: 15.6 us -> 17.4 us  [shifted(): lax.ppermute(shard, axis, [(i, (i + by) % size) for i in range(size)])]
    slice x2 -> x0, local copies, waits for them, and re-layouts: 1.5 us -> none  [the longest x1 0.76 us: per_device(): opp1 = shifted(above[half:], 'pat', -1)]
  transfers between devices with their start and end apart: 10 -> 12, of which waited for: 3 -> 4; matrix products, arithmetic and copies ran while one was open for 3% -> 0% of each run, Pallas kernels for 12% -> 14%
where the time goes in v3:
time: 71.6 us; the launch traced here: 71.9 us
  Pallas kernels  22.2 us (31%)
  blocking collectives  20.2 us (28%)
  starting transfers between devices  17.4 us (24%)
  waiting for transfers between devices  10.5 us (15%)
  between operations  1.59 us (2%)
    pallas_call x7, Pallas kernels, call(): pl.pallas_call(kernel, name=name, out_shape=[jax.ShapeDtypeStruct(s, d) f...  22.2 us
    all_to_all x1, blocking collectives, per_device(): everyone = lax.all_to_all(moments, 'blk', 0, 0)  20.2 us
    ppermute x12, starting transfers between devices, shifted(): lax.ppermute(shard, axis, [(i, (i + by) % size) for i in range(size)])  17.4 us
    ppermute x12, waiting for transfers between devices, shifted(): lax.ppermute(shard, axis, [(i, (i + by) % size) for i in range(size)])  10.5 us
  transfers between devices with their start and end apart: 12, of which 4 were waited for; matrix products, arithmetic and copies ran while one was open for 0% of the time, Pallas kernels for 14%

profile of v3, /device:TPU:1, one launch (start us, length us, event | category | flops | bytes accessed | tf_op | source)
XLA Modules:
  0.0 71.9 jit_solution(6963261905384668621)
XLA Ops:
  1.3 5.1 %first_product.1 = (f32[32,64,128]{2,1,0:T(8,128)S(1)}, f32[32,8,128]{2,1,0:T(8,128)S(1)}, f32[4,72,128]{2,1,0:T(8,128)S(1)}, f32[8,64,128]{2,1,0:T(8,128)S(1)},...) custom-call(s32[96]{0:T(128)} %r_0_.1, s32[96]{0:T(128)} %r_1_.1, s32[1]{0:T(128)S(6)} %copy.9.r_2_, ...), custom_call_target="tpu_custom_call" | custom-call | bytes 4194304 | tf_op jit(solution)/shard_map/first_product/pallas_call | solution.py:352
  6.4 2.2 %collective-permute-start.2 = (bf16[64,4096]{1,0:T(8,128)(2,1)S(1)}, bf16[64,4096]{1,0:T(8,128)(2,1)S(1)}, u32[]{:S(2)}, u32[]{:S(2)}) collective-permute-start(bf16[64,4096]{1,0:T(8,128)(2,1)S(1)} %copy-done), channel_id=1, source_target_pairs={{0,64},{64,128},{128,192},{192,0},{1,65},{65,129},{129,193},{193,1... | collective-permute-start | bytes 1572872 | tf_op jit(solution)/shard_map/ppermute | solution.py:344
  8.6 1.5 %collective-permute-start.3 = (bf16[64,4096]{1,0:T(8,128)(2,1)S(1)}, bf16[64,4096]{1,0:T(8,128)(2,1)S(1)}, u32[]{:S(2)}, u32[]{:S(2)}) collective-permute-start(bf16[64,4096]{1,0:T(8,128)(2,1)S(1)} %copy-done), channel_id=1, source_target_pairs={{0,192},{64,0},{128,64},{192,128},{1,193},{65,1},{129,65},{193,129... | collective-permute-start | bytes 1572872 | tf_op jit(solution)/shard_map/ppermute | solution.py:344
  10.2 1.6 %collective-permute-start.4 = (bf16[64,4096]{1,0:T(8,128)(2,1)S(1)}, bf16[64,4096]{1,0:T(8,128)(2,1)S(1)}, u32[]{:S(2)}, u32[]{:S(2)}) collective-permute-start(bf16[64,4096]{1,0:T(8,128)(2,1)S(1)} %copy-done), channel_id=1, source_target_pairs={{0,128},{64,192},{128,0},{192,64},{1,129},{65,193},{129,1},{193,65... | collective-permute-start | bytes 1572872 | tf_op jit(solution)/shard_map/ppermute | solution.py:344
  11.7 0.4 collective-permute-start.1
  12.2 2.6 %collective-permute-start = (f32[4,72,128]{2,1,0:T(8,128)S(1)}, f32[4,72,128]{2,1,0:T(8,128)S(1)}, u32[]{:S(2)}, u32[]{:S(2)}) collective-permute-start(f32[4,72,128]{2,1,0:T(8,128)S(1)} %get-tuple-element.31.spill_ref), channel_id=1, source_target_pairs={{0,1},{1,2},{2,3},{3,4},{4,5},{5,6},{6,7},{7,8},{8,9},{9,10},{10,1... | collective-permute-start | bytes 442376 | tf_op jit(solution)/shard_map/ppermute | solution.py:344
  14.7 1.7 %inner_sums.1.sums_ref = f32[4,64,128]{2,1,0:T(8,128)S(1)} custom-call(s32[520]{0:T(1024)S(1)} %get-tuple-element.24.lists_ref.r_1_, f32[64,4096]{1,0:T(8,128)S(1)} %get-tuple-element.25.cot_ref, f32[32,64,128]{2,1,0:T(8,128)S(1)} %get-tuple-element.26.v_ref, f32[32,8,128]{2,1,0:T(8,128)S(1)} %get-tuple-element.27.diag_ref, ...), custom_call_target="tpu_custom_call" | custom-call | bytes 4194304 | tf_op jit(solution)/shard_map/inner_sums/pallas_call | solution.py:352
  16.5 4.2 %collective-permute-done.before_ref = f32[4,72,128]{2,1,0:T(8,128)S(1)} collective-permute-done((f32[4,72,128]{2,1,0:T(8,128)S(1)}, f32[4,72,128]{2,1,0:T(8,128)S(1)}, u32[]{:S(2)}, u32[]{:S(2)}) %collective-permute-start) | collective-permute-done | bytes 147488 | tf_op jit(solution)/shard_map/ppermute | solution.py:344
  20.7 0.0 collective-permute-done.1.after_ref
  20.7 1.7 %outer_sums.1 = (f32[12,64,128]{2,1,0:T(8,128)S(1)}, f32[64,1,256]{2,1,0:T(1,128)S(1)}) custom-call(s32[520]{0:T(1024)S(1)} %get-tuple-element.24.lists_ref.r_1_, f32[64,4096]{1,0:T(8,128)S(1)} %get-tuple-element.25.cot_ref, f32[32,64,128]{2,1,0:T(8,128)S(1)} %get-tuple-element.26.v_ref, f32[32,8,128]{2,1,0:T(8,128)S(1)} %get-tuple-element.27.diag_ref, ...), custom_call_target="tpu_custom_call" | custom-call | bytes 4194304 | tf_op jit(solution)/shard_map/outer_sums/pallas_call | solution.py:352
  22.4 20.2 %all_to_all.5.all_ref = f32[64,1,256]{2,1,0:T(1,128)S(1)} all-to-all(f32[64,1,256]{2,1,0:T(1,128)S(1)} %get-tuple-element.33), channel_id=1, replica_groups=mesh['pat'=4,'blk'=64] {'blk'}, dimensions={0} | all-to-all | bytes 131072 | tf_op jit(solution)/shard_map/all_to_all | solution.py:411
  42.6 0.0 collective-permute-done.2.below_hbm
  42.6 0.0 collective-permute-done.3.above_hbm
  42.6 0.0 collective-permute-done.4.opposite_hbm
  42.6 1.5 %combine.1 = (f32[64,4096]{1,0:T(8,128)}, bf16[18,64,128]{2,1,0:T(8,128)(2,1)S(1)}, bf16[18,64,128]{2,1,0:T(8,128)(2,1)S(1)}) custom-call(f32[64,1,256]{2,1,0:T(1,128)S(1)} %all_to_all.5.all_ref, f32[64,4096]{1,0:T(8,128)S(1)} %get-tuple-element.25.cot_ref, f32[8,64,128]{2,1,0:T(8,128)S(1)} %collective-permute-done.1.after_ref, ...), custom_call_target="tpu_custom_call" | custom-call | bytes 4194304 | tf_op jit(solution)/shard_map/combine/pallas_call | solution.py:352
  44.1 0.4 collective-permute-start.5
  44.5 2.3 %collective-permute-start.6 = (bf16[18,64,128]{2,1,0:T(8,128)(2,1)S(1)}, bf16[18,64,128]{2,1,0:T(8,128)(2,1)S(1)}, u32[]{:S(2)}, u32[]{:S(2)}) collective-permute-start(bf16[18,64,128]{2,1,0:T(8,128)(2,1)S(1)} %get-tuple-element.39.refs_1_), channel_id=1, source_target_pairs={{0,192},{64,0},{128,64},{192,128},{1,193},{65,1},{129,65},{193,129... | collective-permute-start | bytes 884744 | tf_op jit(solution)/shard_map/ppermute | solution.py:344
  46.8 1.0 %collective-permute-start.7 = (bf16[4,64,512]{2,1,0:T(8,128)(2,1)S(1)}, bf16[4,64,512]{2,1,0:T(8,128)(2,1)S(1)}, u32[]{:S(2)}, u32[]{:S(2)}) collective-permute-start(bf16[4,64,512]{2,1,0:T(8,128)(2,1)S(1)} %pad_maximum_fusion), channel_id=1, source_target_pairs={{0,63},{1,0},{2,1},{3,2},{4,3},{5,4},{6,5},{7,6},{8,7},{9,8},{10,9... | collective-permute-start | bytes 786440 | tf_op jit(solution)/shard_map/ppermute | solution.py:344
  47.8 0.0 collective-permute-start.10
  47.8 2.7 %collective-permute-start.11 = (bf16[18,64,128]{2,1,0:T(8,128)(2,1)S(1)}, bf16[18,64,128]{2,1,0:T(8,128)(2,1)}, u32[]{:S(2)}, u32[]{:S(2)}) collective-permute-start(bf16[18,64,128]{2,1,0:T(8,128)(2,1)S(1)} %get-tuple-element.38.refs_0_), channel_id=1, source_target_pairs={{0,192},{64,0},{128,64},{192,128},{1,193},{65,1},{129,65},{193,129... | collective-permute-start | bytes 884744 | tf_op jit(solution)/shard_map/ppermute | solution.py:344
  50.5 2.5 %collective-permute-done.7.far_hbm = bf16[4,64,512]{2,1,0:T(8,128)(2,1)S(1)} collective-permute-done((bf16[4,64,512]{2,1,0:T(8,128)(2,1)S(1)}, bf16[4,64,512]{2,1,0:T(8,128)(2,1)S(1)}, u32[]{:S(2)}, u32[]{:S(2)}) %collective-permute-start.7) | collective-permute-done | bytes 262176 | tf_op jit(solution)/shard_map/ppermute | solution.py:344
  53.0 0.6 volt_blocks.1.volt_hbm.r_2_
  53.6 0.0 collective-permute-done.5.refs_2_
  53.6 0.0 collective-permute-done.6.refs_5_
  53.6 0.1 collective-permute-start.8
  53.7 2.7 %collective-permute-start.9 = (bf16[18,64,128]{2,1,0:T(8,128)(2,1)S(1)}, bf16[18,64,128]{2,1,0:T(8,128)(2,1)}, u32[]{:S(2)}, u32[]{:S(2)}) collective-permute-start(bf16[18,64,128]{2,1,0:T(8,128)(2,1)S(1)} %collective-permute-done.6.refs_5_), channel_id=1, source_target_pairs={{0,192},{64,0},{128,64},{192,128},{1,193},{65,1},{129,65},{193,129... | collective-permute-start | bytes 884744 | tf_op jit(solution)/shard_map/ppermute | solution.py:344
  56.4 3.6 %collective-permute-done.10.refs_3_ = bf16[18,64,128]{2,1,0:T(8,128)(2,1)} collective-permute-done((bf16[18,64,128]{2,1,0:T(8,128)(2,1)S(1)}, bf16[18,64,128]{2,1,0:T(8,128)(2,1)}, u32[]{:S(2)}, u32[]{:S(2)}) %collective-permute-start.10) | collective-permute-done | bytes 294944 | tf_op jit(solution)/shard_map/ppermute | solution.py:344
  59.9 0.0 collective-permute-done.11.refs_4_
  59.9 6.1 %early_grads.1.r_5_ = f32[96,32,128]{2,1,0:T(8,128)S(1)} custom-call(s32[1]{0:T(128)} %bitcast.1.part_ref.r_0_, s32[520]{0:T(1024)S(1)} %get-tuple-element.24.lists_ref.r_1_, bf16[36,256,128]{2,1,0:T(8,128)(2,1)S(1)} %volt_blocks.1.volt_hbm.r_2_, bf16[18,64,128]{2,1,0:T(8,128)(2,1)S(1)} %get-tuple-element.38.refs_0_, ...), custom_call_target="tpu_custom_call" | custom-call | bytes 4194304 | tf_op jit(solution)/shard_map/early_grads/pallas_call | solution.py:352
  66.1 0.2 collective-permute-done.8.r_3_
  66.3 0.0 collective-permute-done.9.r_4_
  66.3 5.5 %late_grads.1 = bf16[96,32,128]{2,1,0:T(8,128)(2,1)} custom-call(s32[1]{0:T(128)} %bitcast.1.part_ref.r_0_, s32[520]{0:T(1024)S(1)} %get-tuple-element.24.lists_ref.r_1_, bf16[36,256,128]{2,1,0:T(8,128)(2,1)S(1)} %volt_blocks.1.volt_hbm.r_2_, bf16[18,64,128]{2,1,0:T(8,128)(2,1)} %collective-permute-done.8.r_3_, ...), custom_call_target="tpu_custom_call" | custom-call | bytes 4194304 | tf_op jit(solution)/shard_map/late_grads/pallas_call | solution.py:352
  (3 shorter events, 0.0 us)
Async XLA Ops:
  0.6 5.8 %copy-start = (bf16[64,4096]{1,0:T(8,128)(2,1)S(1)}, bf16[64,4096]{1,0:T(8,128)(2,1)}, u32[]{:S(2)}) copy-start(bf16[64,4096]{1,0:T(8,128)(2,1)} %own_hbm.1) | copy-start | bytes 1572868
  6.4 36.2 %collective-permute-start.2 = (bf16[64,4096]{1,0:T(8,128)(2,1)S(1)}, bf16[64,4096]{1,0:T(8,128)(2,1)S(1)}, u32[]{:S(2)}, u32[]{:S(2)}) collective-permute-start(bf16[64,4096]{1,0:T(8,128)(2,1)S(1)} %copy-done), channel_id=1, source_target_pairs={{0,64},{64,128},{128,192},{192,0},{1,65},{65,129},{129,193},{193,1... | collective-permute-start | bytes 1572872 | tf_op jit(solution)/shard_map/ppermute | solution.py:344
  8.6 34.0 %collective-permute-start.3 = (bf16[64,4096]{1,0:T(8,128)(2,1)S(1)}, bf16[64,4096]{1,0:T(8,128)(2,1)S(1)}, u32[]{:S(2)}, u32[]{:S(2)}) collective-permute-start(bf16[64,4096]{1,0:T(8,128)(2,1)S(1)} %copy-done), channel_id=1, source_target_pairs={{0,192},{64,0},{128,64},{192,128},{1,193},{65,1},{129,65},{193,129... | collective-permute-start | bytes 1572872 | tf_op jit(solution)/shard_map/ppermute | solution.py:344
  10.2 32.4 %collective-permute-start.4 = (bf16[64,4096]{1,0:T(8,128)(2,1)S(1)}, bf16[64,4096]{1,0:T(8,128)(2,1)S(1)}, u32[]{:S(2)}, u32[]{:S(2)}) collective-permute-start(bf16[64,4096]{1,0:T(8,128)(2,1)S(1)} %copy-done), channel_id=1, source_target_pairs={{0,128},{64,192},{128,0},{192,64},{1,129},{65,193},{129,1},{193,65... | collective-permute-start | bytes 1572872 | tf_op jit(solution)/shard_map/ppermute | solution.py:344
  11.7 9.0 %collective-permute-start.1 = (f32[8,64,128]{2,1,0:T(8,128)S(1)}, f32[8,64,128]{2,1,0:T(8,128)S(1)}, u32[]{:S(2)}, u32[]{:S(2)}) collective-permute-start(f32[8,64,128]{2,1,0:T(8,128)S(1)} %get-tuple-element.32), channel_id=1, source_target_pairs={{0,63},{1,0},{2,1},{3,2},{4,3},{5,4},{6,5},{7,6},{8,7},{9,8},{10,9... | collective-permute-start | bytes 786440 | tf_op jit(solution)/shard_map/ppermute | solution.py:344
  12.2 8.6 %collective-permute-start = (f32[4,72,128]{2,1,0:T(8,128)S(1)}, f32[4,72,128]{2,1,0:T(8,128)S(1)}, u32[]{:S(2)}, u32[]{:S(2)}) collective-permute-start(f32[4,72,128]{2,1,0:T(8,128)S(1)} %get-tuple-element.31.spill_ref), channel_id=1, source_target_pairs={{0,1},{1,2},{2,3},{3,4},{4,5},{5,6},{6,7},{7,8},{8,9},{9,10},{10,1... | collective-permute-start | bytes 442376 | tf_op jit(solution)/shard_map/ppermute | solution.py:344
  44.1 9.5 %collective-permute-start.5 = (bf16[18,64,128]{2,1,0:T(8,128)(2,1)S(1)}, bf16[18,64,128]{2,1,0:T(8,128)(2,1)S(1)}, u32[]{:S(2)}, u32[]{:S(2)}) collective-permute-start(bf16[18,64,128]{2,1,0:T(8,128)(2,1)S(1)} %get-tuple-element.38.refs_0_), channel_id=1, source_target_pairs={{0,64},{64,128},{128,192},{192,0},{1,65},{65,129},{129,193},{193,1... | collective-permute-start | bytes 884744 | tf_op jit(solution)/shard_map/ppermute | solution.py:344
  44.5 9.1 %collective-permute-start.6 = (bf16[18,64,128]{2,1,0:T(8,128)(2,1)S(1)}, bf16[18,64,128]{2,1,0:T(8,128)(2,1)S(1)}, u32[]{:S(2)}, u32[]{:S(2)}) collective-permute-start(bf16[18,64,128]{2,1,0:T(8,128)(2,1)S(1)} %get-tuple-element.39.refs_1_), channel_id=1, source_target_pairs={{0,192},{64,0},{128,64},{192,128},{1,193},{65,1},{129,65},{193,129... | collective-permute-start | bytes 884744 | tf_op jit(solution)/shard_map/ppermute | solution.py:344
  46.8 6.2 %collective-permute-start.7 = (bf16[4,64,512]{2,1,0:T(8,128)(2,1)S(1)}, bf16[4,64,512]{2,1,0:T(8,128)(2,1)S(1)}, u32[]{:S(2)}, u32[]{:S(2)}) collective-permute-start(bf16[4,64,512]{2,1,0:T(8,128)(2,1)S(1)} %pad_maximum_fusion), channel_id=1, source_target_pairs={{0,63},{1,0},{2,1},{3,2},{4,3},{5,4},{6,5},{7,6},{8,7},{9,8},{10,9... | collective-permute-start | bytes 786440 | tf_op jit(solution)/shard_map/ppermute | solution.py:344
  47.8 12.1 %collective-permute-start.10 = (bf16[18,64,128]{2,1,0:T(8,128)(2,1)S(1)}, bf16[18,64,128]{2,1,0:T(8,128)(2,1)}, u32[]{:S(2)}, u32[]{:S(2)}) collective-permute-start(bf16[18,64,128]{2,1,0:T(8,128)(2,1)S(1)} %get-tuple-element.39.refs_1_), channel_id=1, source_target_pairs={{0,64},{64,128},{128,192},{192,0},{1,65},{65,129},{129,193},{193,1... | collective-permute-start | bytes 884744 | tf_op jit(solution)/shard_map/ppermute | solution.py:344
  47.8 12.1 %collective-permute-start.11 = (bf16[18,64,128]{2,1,0:T(8,128)(2,1)S(1)}, bf16[18,64,128]{2,1,0:T(8,128)(2,1)}, u32[]{:S(2)}, u32[]{:S(2)}) collective-permute-start(bf16[18,64,128]{2,1,0:T(8,128)(2,1)S(1)} %get-tuple-element.38.refs_0_), channel_id=1, source_target_pairs={{0,192},{64,0},{128,64},{192,128},{1,193},{65,1},{129,65},{193,129... | collective-permute-start | bytes 884744 | tf_op jit(solution)/shard_map/ppermute | solution.py:344
  53.6 12.6 %collective-permute-start.8 = (bf16[18,64,128]{2,1,0:T(8,128)(2,1)S(1)}, bf16[18,64,128]{2,1,0:T(8,128)(2,1)}, u32[]{:S(2)}, u32[]{:S(2)}) collective-permute-start(bf16[18,64,128]{2,1,0:T(8,128)(2,1)S(1)} %collective-permute-done.5.refs_2_), channel_id=1, source_target_pairs={{0,64},{64,128},{128,192},{192,0},{1,65},{65,129},{129,193},{193,1... | collective-permute-start | bytes 884744 | tf_op jit(solution)/shard_map/ppermute | solution.py:344
  53.7 12.5 %collective-permute-start.9 = (bf16[18,64,128]{2,1,0:T(8,128)(2,1)S(1)}, bf16[18,64,128]{2,1,0:T(8,128)(2,1)}, u32[]{:S(2)}, u32[]{:S(2)}) collective-permute-start(bf16[18,64,128]{2,1,0:T(8,128)(2,1)S(1)} %collective-permute-done.6.refs_5_), channel_id=1, source_target_pairs={{0,192},{64,0},{128,64},{192,128},{1,193},{65,1},{129,65},{193,129... | collective-permute-start | bytes 884744 | tf_op jit(solution)/shard_map/ppermute | solution.py:344

commit v4 on v3

--- a/solution.py
+++ b/solution.py
@@ -270,10 +270,7 @@
             volt_ref[NB_DEV + b, k * pats : (k + 1) * pats, :] = far_ref[k, :, cols_of(b)]
 
 
-def gather_fields(part, first, volt_hbm, lam_hbm, field_ref, turned_ref, prow_ref, pcol_ref, sems):
-    groups = field_ref.shape[1] // BLOCK
-    pats = volt_hbm.shape[1] // 4
-    half = lam_hbm[0].shape[0]
+def gather_fields(part, groups, field_ref, turned_ref, swapped_ref, prow_ref, sems):
     copies = []
 
     def copy(src, dst):
@@ -281,59 +278,93 @@
         made.start()
         copies.append(made)
 
-    for g in range(groups):
-        at = g * BLOCK
-        copy(volt_hbm.at[:, pl.ds((first + g) * pats, pats), :], field_ref.at[pl.ds(0, EXT), pl.ds(at, pats), :])
-        copy(lam_hbm[2 * g], field_ref.at[pl.ds(0, half), pl.ds(at + pats, pats), :])
-        copy(lam_hbm[2 * g + 1], field_ref.at[pl.ds(half, EXT - half), pl.ds(at + pats, pats), :])
+    for g, (first, volt_hbm, low_hbm, high_hbm) in enumerate(groups):
+        half, pats = low_hbm.shape[:2]
+        for ref, volt_at, lam_at in ((field_ref, 0, pats), (swapped_ref, pats, 0)):
+            at = g * BLOCK
+            volt = volt_hbm.at[:, pl.ds(first * pats, pats), :]
+            copy(volt, ref.at[pl.ds(0, EXT), pl.ds(at + volt_at, pats), :])
+            copy(low_hbm, ref.at[pl.ds(0, half), pl.ds(at + lam_at, pats), :])
+            copy(high_hbm, ref.at[pl.ds(half, EXT - half), pl.ds(at + lam_at, pats), :])
     for made in copies:
         made.wait()
-    pick = chosen(part)
+    count = len(groups)
     for b in range(EXT):
-        row = jnp.zeros((1, BLOCK), F32)
-        for g in range(groups):
+        row = prow_ref[b : b + 1, :]
+        for g in range(count):
             v = field_ref[b, g * BLOCK : g * BLOCK + pats, :].astype(F32)
             m = field_ref[b, g * BLOCK + pats : (g + 1) * BLOCK, :].astype(F32)
             row = row + jnp.sum(v * m, axis=0, keepdims=True)
-        prow_ref[b] = row
-    for b in range(NB_DEV):
-        straight = dot(pick, field_ref[b], NT)
-        column = jnp.zeros((straight.shape[0], BLOCK), F32)
-        for g in range(groups):
-            part_of = straight[:, cols_of(g)]
-            other = pltpu.roll(part_of, pats, 1)
-            column = column + part_of * other
-            turned_ref[b, :, cols_of(g)] = other.astype(BF16)
-        column = jnp.sum(column, axis=1, keepdims=True) * 0.5
-        pcol_ref[b] = jnp.broadcast_to(column, (straight.shape[0], BLOCK))
-    prow_ref[TRASH] = jnp.zeros((1, BLOCK), F32)
-    pcol_ref[TRASH] = jnp.zeros(pcol_ref.shape[1:], F32)
+        prow_ref[b : b + 1, :] = row
     turned_ref[TRASH] = jnp.zeros(turned_ref.shape[1:], BF16)
     field_ref[TRASH] = jnp.zeros(field_ref.shape[1:], BF16)
 
 
-def early_grads_kernel(part_ref, lists_ref, volt_hbm, *refs):
-    lam_hbm, (partial_ref, field_ref, turned_ref, prow_ref, pcol_ref, sems) = refs[:6], refs[6:]
-    gather_fields(part_ref[0], 0, volt_hbm, lam_hbm, field_ref, turned_ref, prow_ref, pcol_ref, sems)
+def turn(part, turned_ref, swapped_ref):
+    pick = chosen(part)
+    for b in range(NB_DEV):
+        turned_ref[b] = dot(pick, swapped_ref[b], NT).astype(BF16)
+
+
+def own_grads_kernel(part_ref, lists_ref, volt_hbm, low_hbm, high_hbm, partial_ref, prow_ref, *refs):
+    field_ref, turned_ref, swapped_ref, sems = refs
+    prow_ref[...] = jnp.zeros_like(prow_ref)
+    gather_fields(part_ref[0], [(0, volt_hbm, low_hbm, high_hbm)], field_ref, turned_ref, swapped_ref, prow_ref, sems)
+    turn(part_ref[0], turned_ref, swapped_ref)
 
     def body(first, tiles, carry):
         for u, (row, col, slot) in enumerate(tiles):
-            partial_ref[first + u] = dot(turned_ref[row], field_ref[col], NN) - pcol_ref[row] - prow_ref[col]
+            partial_ref[first + u] = dot(turned_ref[row], field_ref[col], NN)
         return carry
 
     listed(lists_ref, 3, body, 0)
 
 
-def late_grads_kernel(scale, part_ref, lists_ref, volt_hbm, low_hbm, high_hbm, partial_ref, grads_ref, *refs):
-    field_ref, turned_ref, prow_ref, pcol_ref, sems = refs
-    grads_ref[...] = jnp.zeros_like(grads_ref)
-    gather_fields(part_ref[0], 3, volt_hbm, (low_hbm, high_hbm), field_ref, turned_ref, prow_ref, pcol_ref, sems)
-    count = lists_ref[3]
+def near_grads_kernel(
+    part_ref, lists_ref, volt_hbm, low0_hbm, high0_hbm, low1_hbm, high1_hbm, before_ref, prow0_ref,
+    partial_ref, prow_ref, field_ref, turned_ref, swapped_ref, sems,
+):
+    prow_ref[...] = prow0_ref[...]
+    groups = [(1, volt_hbm, low0_hbm, high0_hbm), (2, volt_hbm, low1_hbm, high1_hbm)]
+    gather_fields(part_ref[0], groups, field_ref, turned_ref, swapped_ref, prow_ref, sems)
+    turn(part_ref[0], turned_ref, swapped_ref)
 
     def body(first, tiles, carry):
         for u, (row, col, slot) in enumerate(tiles):
-            value = partial_ref[first + u] + dot(turned_ref[row], field_ref[col], NN) - pcol_ref[row] - prow_ref[col]
-            grads_ref[first + u] = jnp.where(first + u < count, value * scale, 0.0).astype(BF16)
+            partial_ref[first + u] = before_ref[first + u] + dot(turned_ref[row], field_ref[col], NN)
+        return carry
+
+    listed(lists_ref, 3, body, 0)
+
+
+def late_grads_kernel(
+    scale, part_ref, lists_ref, volt_hbm, low_hbm, high_hbm, partial_ref, prow0_ref, grads_ref,
+    field_ref, turned_ref, swapped_ref, prow_ref, sems,
+):
+    grads_ref[...] = jnp.zeros_like(grads_ref)
+    prow_ref[...] = prow0_ref[...]
+    gather_fields(part_ref[0], [(3, volt_hbm, low_hbm, high_hbm)], field_ref, turned_ref, swapped_ref, prow_ref, sems)
+    rows = lax.broadcasted_iota(jnp.int32, (16, BLOCK), 0)
+    ones = jnp.where(rows < 3, 1.0, 0.0).astype(BF16)
+    for b in range(EXT):
+        rest = -prow_ref[b : b + 1, :]
+        extra = jnp.zeros((16, BLOCK), F32)
+        for k in range(3):
+            piece = rest.astype(BF16).astype(F32)
+            rest = rest - piece
+            extra = jnp.where(rows == k, piece, extra)
+        extra = extra.astype(BF16)
+        field_ref[b, BLOCK : BLOCK + 16, :] = ones
+        field_ref[b, BLOCK + 16 :, :] = extra
+        swapped_ref[b, BLOCK : BLOCK + 16, :] = extra
+        swapped_ref[b, BLOCK + 16 :, :] = ones
+    turn(part_ref[0], turned_ref, swapped_ref)
+    count = lists_ref[3]
+
+    def body(first, tiles, carry):
+        for u, (row, col, slot) in enumerate(tiles):
+            value = (partial_ref[first + u] + dot(turned_ref[row], field_ref[col], NN)) * scale
+            grads_ref[first + u] = jnp.where(first + u < count, value, 0.0).astype(BF16)
         return carry
 
     listed(lists_ref, 3, body, 0)
@@ -348,7 +379,7 @@
     return pltpu.with_memory_space_constraint(x, pltpu.HBM)
 
 
-def call(kernel, name, outs, specs, scratch, *args, cost=0, last=VMEM):
+def call(kernel, name, outs, specs, scratch, *args, us=1.0, last=VMEM):
     return pl.pallas_call(
         kernel,
         name=name,
@@ -357,7 +388,7 @@
         out_specs=[VMEM] * (len(outs) - 1) + [last],
         scratch_shapes=scratch,
         compiler_params=pltpu.CompilerParams(vmem_limit_bytes=24 * 1024 * 1024),
-        cost_estimate=pl.CostEstimate(flops=cost, bytes_accessed=4 * 1024 * 1024, transcendentals=0),
+        cost_estimate=pl.CostEstimate(flops=0, bytes_accessed=int(us * 3.69e6), transcendentals=0),
     )(*args)
 
 
@@ -388,32 +419,31 @@
             pltpu.SemaphoreType.DMA((6,)),
         ],
         in_hbm(tile_rows), in_hbm(tile_cols), tile_count,
-        in_hbm(cotangent), in_hbm(ground.reshape(NB_DEV, BLOCK)), in_hbm(tile_values), last=SMEM,
+        in_hbm(cotangent), in_hbm(ground.reshape(NB_DEV, BLOCK)), in_hbm(tile_values), us=4.0, last=SMEM,
     )
     spill, head, volt = lax.optimization_barrier((spill, head, voltages))
-    before = shifted(spill, "blk", 1)
-    after = shifted(head, "blk", -1)
     below_v = shifted(volt, "pat", 1)
     above_v = shifted(volt, "pat", -1)
     opposite_v = shifted(volt, "pat", 2)
+    before = shifted(spill, "blk", 1)
+    after = shifted(head, "blk", -1)
     work = [pltpu.VMEM((EXT + 1, pats, BLOCK), F32), pltpu.VMEM((EXT + 1, 2 * pats, BLOCK), BF16)]
     (sums,) = call(
         inner_kernel, "inner_sums",
         [((4, pats, BLOCK), F32)], [SMEM] + [VMEM] * 4, work,
-        lists, cot, v, diag, tiles,
+        lists, cot, v, diag, tiles, us=5.0,
     )
     edges, moments = call(
         outer_kernel, "outer_sums",
         [((3 * H, pats, BLOCK), F32), ((devices, 1, 4 * pats), F32)], [SMEM] + [VMEM] * 8,
         [*work, pltpu.VMEM((H + 1, pats, BLOCK), BF16), pltpu.VMEM((H + 1, pats, BLOCK), F32)],
-        lists, cot, v, diag, tiles, spill, before, after, sums,
+        lists, cot, v, diag, tiles, spill, before, after, sums, us=60.0,
     )
     everyone = lax.all_to_all(moments, "blk", 0, 0)
-    everyone, below_v, above_v, opposite_v = lax.optimization_barrier((everyone, below_v, above_v, opposite_v))
     adjoint, low, high = call(
         combine_kernel, "combine",
         [(cotangent.shape, F32), ((half, pats, BLOCK), BF16), ((EXT - half, pats, BLOCK), BF16)], [VMEM] * 5, [],
-        everyone, cot, after, v, edges,
+        everyone, cot, after, v, edges, us=0.1,
     )
     low_below = shifted(low, "pat", 1)
     high_above = shifted(high, "pat", -1)
@@ -430,28 +460,34 @@
         ],
         voltages, below_v, above_v, opposite_v, far,
     )
+
+    def grad_work(groups, depth):
+        return [
+            pltpu.VMEM((EXT + 1, depth, BLOCK), BF16),
+            pltpu.VMEM((EXT + 1, rows_out, depth), BF16),
+            pltpu.VMEM((EXT + 1, depth, BLOCK), BF16),
+        ], pltpu.SemaphoreType.DMA((6 * groups,))
+
+    shares = [((slots, rows_out, BLOCK), F32), ((EXT, BLOCK), F32)]
+    scratch, sems = grad_work(1, BLOCK)
+    partial, prow = call(
+        own_grads_kernel, "own_grads", shares, [SMEM] * 2 + [ANY] * 3, [*scratch, sems], part, lists, volt, low, high,
+        us=3.0,
+    )
     low_below, high_above, volt = lax.optimization_barrier((low_below, high_above, volt))
     low_opposite = shifted(low_below, "pat", 1)
     high_opposite = shifted(high_above, "pat", -1)
-
-    def grad_work(groups):
-        return [
-            pltpu.VMEM((EXT + 1, groups * BLOCK, BLOCK), BF16),
-            pltpu.VMEM((NB_DEV + H + 1, rows_out, groups * BLOCK), BF16),
-            pltpu.VMEM((EXT + 1, 1, BLOCK), F32),
-            pltpu.VMEM((EXT + 1, rows_out, BLOCK), F32),
-            pltpu.SemaphoreType.DMA((3 * groups,)),
-        ]
-
-    (partial,) = call(
-        early_grads_kernel, "early_grads",
-        [((slots, rows_out, BLOCK), F32)], [SMEM] * 2 + [ANY] * 7, grad_work(parts - 1),
-        part, lists, volt, low, high, low_below, high_below, low_above, high_above,
-    )
+    scratch, sems = grad_work(2, 2 * BLOCK)
+    partial, prow = call(
+        near_grads_kernel, "near_grads", shares, [SMEM] * 2 + [ANY] * 5 + [VMEM] * 2, [*scratch, sems],
+        part, lists, volt, low_below, high_below, low_above, high_above, partial, prow, us=4.0,
+    )
+    scratch, sems = grad_work(1, BLOCK + 32)
     (grads,) = call(
         lambda *r: late_grads_kernel(1.0 / math.sqrt(parts * pats), *r), "late_grads",
-        [((slots, rows_out, BLOCK), BF16)], [SMEM] * 2 + [ANY] * 3 + [VMEM], grad_work(1),
-        part, lists, volt, low_opposite, high_opposite, partial,
+        [((slots, rows_out, BLOCK), BF16)], [SMEM] * 2 + [ANY] * 3 + [VMEM] * 2,
+        [*scratch, pltpu.VMEM((EXT, BLOCK), F32), sems],
+        part, lists, volt, low_opposite, high_opposite, partial, prow,
     )
     return adjoint, grads
 

time: 71.6 us -> 70.3 us (0.982)
  starting transfers between devices: 17.4 us -> 15.2 us
  waiting for transfers between devices: 10.5 us -> 11.9 us
    ppermute x12, starting transfers between devices: 17.4 us -> 15.2 us  [shifted(): lax.ppermute(shard, axis, [(i, (i + by) % size) for i in range(size)])]
    ppermute x12, waiting for transfers between devices: 10.5 us -> 11.9 us  [shifted(): lax.ppermute(shard, axis, [(i, (i + by) % size) for i in range(size)])]
    pallas_call x7 -> x8, Pallas kernels: 22.2 us -> 21.8 us  [call(): pl.pallas_call(kernel, name=name, out_shape=[jax.ShapeDtypeStruct(s, d) f...]
  transfers between devices with their start and end apart: 12 -> 12, of which waited for: 4 -> 4; matrix products, arithmetic and copies ran while one was open for 0% -> 0% of each run, Pallas kernels for 14% -> 18%
where the time goes in v4:
time: 70.3 us; the launch traced here: 70.2 us
  Pallas kernels  21.8 us (31%)
  blocking collectives  19.7 us (28%)
  starting transfers between devices  15.2 us (22%)
  waiting for transfers between devices  11.9 us (17%)
  between operations  1.61 us (2%)
    pallas_call x8, Pallas kernels, call(): pl.pallas_call(kernel, name=name, out_shape=[jax.ShapeDtypeStruct(s, d) f...  21.8 us
    all_to_all x1, blocking collectives, per_device(): everyone = lax.all_to_all(moments, 'blk', 0, 0)  19.7 us
    ppermute x12, starting transfers between devices, shifted(): lax.ppermute(shard, axis, [(i, (i + by) % size) for i in range(size)])  15.2 us
    ppermute x12, waiting for transfers between devices, shifted(): lax.ppermute(shard, axis, [(i, (i + by) % size) for i in range(size)])  11.9 us
  transfers between devices with their start and end apart: 12, of which 4 were waited for; matrix products, arithmetic and copies ran while one was open for 0% of the time, Pallas kernels for 18%

profile of v4, /device:TPU:1, one launch (start us, length us, event | category | flops | bytes accessed | tf_op | source)
XLA Modules:
  0.0 70.2 jit_solution(14763624659451098356)
XLA Ops:
  1.3 5.1 %first_product.1 = (f32[32,64,128]{2,1,0:T(8,128)S(1)}, f32[32,8,128]{2,1,0:T(8,128)S(1)}, f32[4,72,128]{2,1,0:T(8,128)S(1)}, f32[8,64,128]{2,1,0:T(8,128)S(1)},...) custom-call(s32[96]{0:T(128)} %r_0_.1, s32[96]{0:T(128)} %r_1_.1, s32[1]{0:T(128)S(6)} %copy.9.r_2_, ...), custom_call_target="tpu_custom_call" | custom-call | bytes 14760000 | tf_op jit(solution)/shard_map/first_product/pallas_call | solution.py:383
  6.4 3.8 %collective-permute-start.6 = (bf16[64,4096]{1,0:T(8,128)(2,1)S(1)}, bf16[64,4096]{1,0:T(8,128)(2,1)S(1)}, u32[]{:S(2)}, u32[]{:S(2)}) collective-permute-start(bf16[64,4096]{1,0:T(8,128)(2,1)S(1)} %copy-done), channel_id=1, source_target_pairs={{0,128},{64,192},{128,0},{192,64},{1,129},{65,193},{129,1},{193,65... | collective-permute-start | bytes 1572872 | tf_op jit(solution)/shard_map/ppermute | solution.py:375
  10.2 0.8 %collective-permute-start.5 = (bf16[64,4096]{1,0:T(8,128)(2,1)S(1)}, bf16[64,4096]{1,0:T(8,128)(2,1)S(1)}, u32[]{:S(2)}, u32[]{:S(2)}) collective-permute-start(bf16[64,4096]{1,0:T(8,128)(2,1)S(1)} %copy-done), channel_id=1, source_target_pairs={{0,192},{64,0},{128,64},{192,128},{1,193},{65,1},{129,65},{193,129... | collective-permute-start | bytes 1572872 | tf_op jit(solution)/shard_map/ppermute | solution.py:375
  11.0 0.7 collective-permute-start.4
  11.7 0.4 collective-permute-start.1
  12.2 1.5 %collective-permute-start = (f32[4,72,128]{2,1,0:T(8,128)S(1)}, f32[4,72,128]{2,1,0:T(8,128)S(1)}, u32[]{:S(2)}, u32[]{:S(2)}) collective-permute-start(f32[4,72,128]{2,1,0:T(8,128)S(1)} %get-tuple-element.31.spill_ref), channel_id=1, source_target_pairs={{0,1},{1,2},{2,3},{3,4},{4,5},{5,6},{6,7},{7,8},{8,9},{9,10},{10,1... | collective-permute-start | bytes 442376 | tf_op jit(solution)/shard_map/ppermute | solution.py:375
  13.7 1.7 %inner_sums.1.sums_ref = f32[4,64,128]{2,1,0:T(8,128)S(1)} custom-call(s32[520]{0:T(1024)S(1)} %get-tuple-element.24.lists_ref.r_1_, f32[64,4096]{1,0:T(8,128)S(1)} %get-tuple-element.25.cot_ref, f32[32,64,128]{2,1,0:T(8,128)S(1)} %get-tuple-element.26.v_ref, f32[32,8,128]{2,1,0:T(8,128)S(1)} %get-tuple-element.27.diag_ref, ...), custom_call_target="tpu_custom_call" | custom-call | bytes 18450000 | tf_op jit(solution)/shard_map/inner_sums/pallas_call | solution.py:383
  15.5 5.3 %collective-permute-done.before_ref = f32[4,72,128]{2,1,0:T(8,128)S(1)} collective-permute-done((f32[4,72,128]{2,1,0:T(8,128)S(1)}, f32[4,72,128]{2,1,0:T(8,128)S(1)}, u32[]{:S(2)}, u32[]{:S(2)}) %collective-permute-start) | collective-permute-done | bytes 147488 | tf_op jit(solution)/shard_map/ppermute | solution.py:375
  20.8 0.0 collective-permute-done.1.after_ref
  20.8 2.2 %outer_sums.1 = (f32[12,64,128]{2,1,0:T(8,128)S(1)}, f32[64,1,256]{2,1,0:T(1,128)S(1)}) custom-call(s32[520]{0:T(1024)S(1)} %get-tuple-element.24.lists_ref.r_1_, f32[64,4096]{1,0:T(8,128)S(1)} %get-tuple-element.25.cot_ref, f32[32,64,128]{2,1,0:T(8,128)S(1)} %get-tuple-element.26.v_ref, f32[32,8,128]{2,1,0:T(8,128)S(1)} %get-tuple-element.27.diag_ref, ...), custom_call_target="tpu_custom_call" | custom-call | bytes 221400000 | tf_op jit(solution)/shard_map/outer_sums/pallas_call | solution.py:383
  22.9 19.7 %all_to_all.5.all_ref = f32[64,1,256]{2,1,0:T(1,128)S(1)} all-to-all(f32[64,1,256]{2,1,0:T(1,128)S(1)} %get-tuple-element.33), channel_id=1, replica_groups=mesh['pat'=4,'blk'=64] {'blk'}, dimensions={0} | all-to-all | bytes 131072 | tf_op jit(solution)/shard_map/all_to_all | solution.py:442
  42.6 1.5 %combine.1 = (f32[64,4096]{1,0:T(8,128)}, bf16[18,64,128]{2,1,0:T(8,128)(2,1)S(1)}, bf16[18,64,128]{2,1,0:T(8,128)(2,1)S(1)}) custom-call(f32[64,1,256]{2,1,0:T(1,128)S(1)} %all_to_all.5.all_ref, f32[64,4096]{1,0:T(8,128)S(1)} %get-tuple-element.25.cot_ref, f32[8,64,128]{2,1,0:T(8,128)S(1)} %collective-permute-done.1.after_ref, ...), custom_call_target="tpu_custom_call" | custom-call | bytes 369000 | tf_op jit(solution)/shard_map/combine/pallas_call | solution.py:383
  44.1 0.4 collective-permute-start.2
  44.5 2.3 %collective-permute-start.3 = (bf16[18,64,128]{2,1,0:T(8,128)(2,1)S(1)}, bf16[18,64,128]{2,1,0:T(8,128)(2,1)}, u32[]{:S(2)}, u32[]{:S(2)}) collective-permute-start(bf16[18,64,128]{2,1,0:T(8,128)(2,1)S(1)} %get-tuple-element.37.high_hbm), channel_id=1, source_target_pairs={{0,192},{64,0},{128,64},{192,128},{1,193},{65,1},{129,65},{193,129... | collective-permute-start | bytes 884744 | tf_op jit(solution)/shard_map/ppermute | solution.py:375
  46.8 0.0 collective-permute-done.6.opposite_hbm
  46.8 0.0 collective-permute-done.5.above_hbm
  46.8 0.0 collective-permute-done.4.below_hbm
  46.8 1.0 %collective-permute-start.7 = (bf16[4,64,512]{2,1,0:T(8,128)(2,1)S(1)}, bf16[4,64,512]{2,1,0:T(8,128)(2,1)S(1)}, u32[]{:S(2)}, u32[]{:S(2)}) collective-permute-start(bf16[4,64,512]{2,1,0:T(8,128)(2,1)S(1)} %pad_maximum_fusion), channel_id=1, source_target_pairs={{0,63},{1,0},{2,1},{3,2},{4,3},{5,4},{6,5},{7,6},{8,7},{9,8},{10,9... | collective-permute-start | bytes 786440 | tf_op jit(solution)/shard_map/ppermute | solution.py:375
  47.9 0.8 %collective-permute-start.11 = (bf16[18,64,128]{2,1,0:T(8,128)(2,1)S(1)}, bf16[18,64,128]{2,1,0:T(8,128)(2,1)}, u32[]{:S(2)}, u32[]{:S(2)}) collective-permute-start(bf16[18,64,128]{2,1,0:T(8,128)(2,1)S(1)} %get-tuple-element.36.low_hbm), channel_id=1, source_target_pairs={{0,192},{64,0},{128,64},{192,128},{1,193},{65,1},{129,65},{193,129... | collective-permute-start | bytes 884744 | tf_op jit(solution)/shard_map/ppermute | solution.py:375
  48.6 0.7 collective-permute-start.10
  49.3 3.8 %collective-permute-done.7.far_hbm = bf16[4,64,512]{2,1,0:T(8,128)(2,1)S(1)} collective-permute-done((bf16[4,64,512]{2,1,0:T(8,128)(2,1)S(1)}, bf16[4,64,512]{2,1,0:T(8,128)(2,1)S(1)}, u32[]{:S(2)}, u32[]{:S(2)}) %collective-permute-start.7) | collective-permute-done | bytes 262176 | tf_op jit(solution)/shard_map/ppermute | solution.py:375
  53.1 0.6 volt_blocks.1.volt_hbm.r_2_
  53.7 0.0 collective-permute-done.2.low0_hbm
  53.7 0.0 collective-permute-done.3.high1_hbm
  53.7 0.1 collective-permute-start.8
  53.8 2.7 %collective-permute-start.9 = (bf16[18,64,128]{2,1,0:T(8,128)(2,1)}, bf16[18,64,128]{2,1,0:T(8,128)(2,1)S(1)}, u32[]{:S(2)}, u32[]{:S(2)}) collective-permute-start(bf16[18,64,128]{2,1,0:T(8,128)(2,1)} %collective-permute-done.3.high1_hbm), channel_id=1, source_target_pairs={{0,192},{64,0},{128,64},{192,128},{1,193},{65,1},{129,65},{193,129... | collective-permute-start | bytes 884744 | tf_op jit(solution)/shard_map/ppermute | solution.py:375
  56.5 2.4 %own_grads.1 = (f32[96,32,128]{2,1,0:T(8,128)S(1)}, f32[36,128]{1,0:T(8,128)S(1)}) custom-call(s32[1]{0:T(128)} %bitcast.1.part_ref.r_0_, s32[520]{0:T(1024)S(1)} %get-tuple-element.24.lists_ref.r_1_, bf16[36,256,128]{2,1,0:T(8,128)(2,1)S(1)} %volt_blocks.1.volt_hbm.r_2_, bf16[18,64,128]{2,1,0:T(8,128)(2,1)S(1)} %get-tuple-element.36.low_hbm, ...), custom_call_target="tpu_custom_call" | custom-call | bytes 11070000 | tf_op jit(solution)/shard_map/own_grads/pallas_call | solution.py:383
  58.9 1.0 %collective-permute-done.10.high0_hbm = bf16[18,64,128]{2,1,0:T(8,128)(2,1)} collective-permute-done((bf16[18,64,128]{2,1,0:T(8,128)(2,1)S(1)}, bf16[18,64,128]{2,1,0:T(8,128)(2,1)}, u32[]{:S(2)}, u32[]{:S(2)}) %collective-permute-start.10) | collective-permute-done | bytes 294944 | tf_op jit(solution)/shard_map/ppermute | solution.py:375
  59.9 4.4 %near_grads.1 = (f32[96,32,128]{2,1,0:T(8,128)S(1)}, f32[36,128]{1,0:T(8,128)S(1)}) custom-call(s32[1]{0:T(128)} %bitcast.1.part_ref.r_0_, s32[520]{0:T(1024)S(1)} %get-tuple-element.24.lists_ref.r_1_, bf16[36,256,128]{2,1,0:T(8,128)(2,1)S(1)} %volt_blocks.1.volt_hbm.r_2_, bf16[18,64,128]{2,1,0:T(8,128)(2,1)} %collective-permute-done.2.low0_hbm, ...), custom_call_target="tpu_custom_call" | custom-call | bytes 14760000 | tf_op jit(solution)/shard_map/near_grads/pallas_call | solution.py:383
  64.3 1.8 %collective-permute-done.8.r_3_ = bf16[18,64,128]{2,1,0:T(8,128)(2,1)S(1)} collective-permute-done((bf16[18,64,128]{2,1,0:T(8,128)(2,1)}, bf16[18,64,128]{2,1,0:T(8,128)(2,1)S(1)}, u32[]{:S(2)}, u32[]{:S(2)}) %collective-permute-start.8) | collective-permute-done | bytes 294944 | tf_op jit(solution)/shard_map/ppermute | solution.py:375
  66.2 0.0 collective-permute-done.9.r_4_
  66.2 3.9 %late_grads.1 = bf16[96,32,128]{2,1,0:T(8,128)(2,1)} custom-call(s32[1]{0:T(128)} %bitcast.1.part_ref.r_0_, s32[520]{0:T(1024)S(1)} %get-tuple-element.24.lists_ref.r_1_, bf16[36,256,128]{2,1,0:T(8,128)(2,1)S(1)} %volt_blocks.1.volt_hbm.r_2_, bf16[18,64,128]{2,1,0:T(8,128)(2,1)S(1)} %collective-permute-done.8.r_3_, ...), custom_call_target="tpu_custom_call" | custom-call | bytes 3690000 | tf_op jit(solution)/shard_map/late_grads/pallas_call | solution.py:383
  (4 shorter events, 0.0 us)
Async XLA Ops:
  0.6 5.8 %copy-start = (bf16[64,4096]{1,0:T(8,128)(2,1)S(1)}, bf16[64,4096]{1,0:T(8,128)(2,1)}, u32[]{:S(2)}) copy-start(bf16[64,4096]{1,0:T(8,128)(2,1)} %own_hbm.1) | copy-start | bytes 1572868
  6.4 40.4 %collective-permute-start.6 = (bf16[64,4096]{1,0:T(8,128)(2,1)S(1)}, bf16[64,4096]{1,0:T(8,128)(2,1)S(1)}, u32[]{:S(2)}, u32[]{:S(2)}) collective-permute-start(bf16[64,4096]{1,0:T(8,128)(2,1)S(1)} %copy-done), channel_id=1, source_target_pairs={{0,128},{64,192},{128,0},{192,64},{1,129},{65,193},{129,1},{193,65... | collective-permute-start | bytes 1572872 | tf_op jit(solution)/shard_map/ppermute | solution.py:375
  10.2 36.5 %collective-permute-start.5 = (bf16[64,4096]{1,0:T(8,128)(2,1)S(1)}, bf16[64,4096]{1,0:T(8,128)(2,1)S(1)}, u32[]{:S(2)}, u32[]{:S(2)}) collective-permute-start(bf16[64,4096]{1,0:T(8,128)(2,1)S(1)} %copy-done), channel_id=1, source_target_pairs={{0,192},{64,0},{128,64},{192,128},{1,193},{65,1},{129,65},{193,129... | collective-permute-start | bytes 1572872 | tf_op jit(solution)/shard_map/ppermute | solution.py:375
  11.0 35.8 %collective-permute-start.4 = (bf16[64,4096]{1,0:T(8,128)(2,1)S(1)}, bf16[64,4096]{1,0:T(8,128)(2,1)S(1)}, u32[]{:S(2)}, u32[]{:S(2)}) collective-permute-start(bf16[64,4096]{1,0:T(8,128)(2,1)S(1)} %copy-done), channel_id=1, source_target_pairs={{0,64},{64,128},{128,192},{192,0},{1,65},{65,129},{129,193},{193,1... | collective-permute-start | bytes 1572872 | tf_op jit(solution)/shard_map/ppermute | solution.py:375
  11.7 9.0 %collective-permute-start.1 = (f32[8,64,128]{2,1,0:T(8,128)S(1)}, f32[8,64,128]{2,1,0:T(8,128)S(1)}, u32[]{:S(2)}, u32[]{:S(2)}) collective-permute-start(f32[8,64,128]{2,1,0:T(8,128)S(1)} %get-tuple-element.32), channel_id=1, source_target_pairs={{0,63},{1,0},{2,1},{3,2},{4,3},{5,4},{6,5},{7,6},{8,7},{9,8},{10,9... | collective-permute-start | bytes 786440 | tf_op jit(solution)/shard_map/ppermute | solution.py:375
  12.2 8.6 %collective-permute-start = (f32[4,72,128]{2,1,0:T(8,128)S(1)}, f32[4,72,128]{2,1,0:T(8,128)S(1)}, u32[]{:S(2)}, u32[]{:S(2)}) collective-permute-start(f32[4,72,128]{2,1,0:T(8,128)S(1)} %get-tuple-element.31.spill_ref), channel_id=1, source_target_pairs={{0,1},{1,2},{2,3},{3,4},{4,5},{5,6},{6,7},{7,8},{8,9},{9,10},{10,1... | collective-permute-start | bytes 442376 | tf_op jit(solution)/shard_map/ppermute | solution.py:375
  44.1 9.6 %collective-permute-start.2 = (bf16[18,64,128]{2,1,0:T(8,128)(2,1)S(1)}, bf16[18,64,128]{2,1,0:T(8,128)(2,1)}, u32[]{:S(2)}, u32[]{:S(2)}) collective-permute-start(bf16[18,64,128]{2,1,0:T(8,128)(2,1)S(1)} %get-tuple-element.36.low_hbm), channel_id=1, source_target_pairs={{0,64},{64,128},{128,192},{192,0},{1,65},{65,129},{129,193},{193,1... | collective-permute-start | bytes 884744 | tf_op jit(solution)/shard_map/ppermute | solution.py:375
  44.5 9.2 %collective-permute-start.3 = (bf16[18,64,128]{2,1,0:T(8,128)(2,1)S(1)}, bf16[18,64,128]{2,1,0:T(8,128)(2,1)}, u32[]{:S(2)}, u32[]{:S(2)}) collective-permute-start(bf16[18,64,128]{2,1,0:T(8,128)(2,1)S(1)} %get-tuple-element.37.high_hbm), channel_id=1, source_target_pairs={{0,192},{64,0},{128,64},{192,128},{1,193},{65,1},{129,65},{193,129... | collective-permute-start | bytes 884744 | tf_op jit(solution)/shard_map/ppermute | solution.py:375
  46.8 6.3 %collective-permute-start.7 = (bf16[4,64,512]{2,1,0:T(8,128)(2,1)S(1)}, bf16[4,64,512]{2,1,0:T(8,128)(2,1)S(1)}, u32[]{:S(2)}, u32[]{:S(2)}) collective-permute-start(bf16[4,64,512]{2,1,0:T(8,128)(2,1)S(1)} %pad_maximum_fusion), channel_id=1, source_target_pairs={{0,63},{1,0},{2,1},{3,2},{4,3},{5,4},{6,5},{7,6},{8,7},{9,8},{10,9... | collective-permute-start | bytes 786440 | tf_op jit(solution)/shard_map/ppermute | solution.py:375
  47.9 11.1 %collective-permute-start.11 = (bf16[18,64,128]{2,1,0:T(8,128)(2,1)S(1)}, bf16[18,64,128]{2,1,0:T(8,128)(2,1)}, u32[]{:S(2)}, u32[]{:S(2)}) collective-permute-start(bf16[18,64,128]{2,1,0:T(8,128)(2,1)S(1)} %get-tuple-element.36.low_hbm), channel_id=1, source_target_pairs={{0,192},{64,0},{128,64},{192,128},{1,193},{65,1},{129,65},{193,129... | collective-permute-start | bytes 884744 | tf_op jit(solution)/shard_map/ppermute | solution.py:375
  48.6 11.3 %collective-permute-start.10 = (bf16[18,64,128]{2,1,0:T(8,128)(2,1)S(1)}, bf16[18,64,128]{2,1,0:T(8,128)(2,1)}, u32[]{:S(2)}, u32[]{:S(2)}) collective-permute-start(bf16[18,64,128]{2,1,0:T(8,128)(2,1)S(1)} %get-tuple-element.37.high_hbm), channel_id=1, source_target_pairs={{0,64},{64,128},{128,192},{192,0},{1,65},{65,129},{129,193},{193,1... | collective-permute-start | bytes 884744 | tf_op jit(solution)/shard_map/ppermute | solution.py:375
  53.7 12.4 %collective-permute-start.8 = (bf16[18,64,128]{2,1,0:T(8,128)(2,1)}, bf16[18,64,128]{2,1,0:T(8,128)(2,1)S(1)}, u32[]{:S(2)}, u32[]{:S(2)}) collective-permute-start(bf16[18,64,128]{2,1,0:T(8,128)(2,1)} %collective-permute-done.2.low0_hbm), channel_id=1, source_target_pairs={{0,64},{64,128},{128,192},{192,0},{1,65},{65,129},{129,193},{193,1... | collective-permute-start | bytes 884744 | tf_op jit(solution)/shard_map/ppermute | solution.py:375
  53.8 12.3 %collective-permute-start.9 = (bf16[18,64,128]{2,1,0:T(8,128)(2,1)}, bf16[18,64,128]{2,1,0:T(8,128)(2,1)S(1)}, u32[]{:S(2)}, u32[]{:S(2)}) collective-permute-start(bf16[18,64,128]{2,1,0:T(8,128)(2,1)} %collective-permute-done.3.high1_hbm), channel_id=1, source_target_pairs={{0,192},{64,0},{128,64},{192,128},{1,193},{65,1},{129,65},{193,129... | collective-permute-start | bytes 884744 | tf_op jit(solution)/shard_map/ppermute | solution.py:375

commit v5 on v4

--- a/solution.py
+++ b/solution.py
@@ -21,6 +21,7 @@
 TRASH = EXT
 HEAD = 8
 LISTS = 4
+CHUNKS = ((0, 32), (32, 16), (48, 16), (64, 32))
 
 NT = (((1,), (1,)), ((), ()))
 NN = (((1,), (0,)), ((), ()))
@@ -59,15 +60,18 @@
             lists_ref[HEAD + k * room + sizes[k] + u] = none
 
 
+def tiles_of(lists_ref, k, first, unroll):
+    room = (lists_ref.shape[0] - HEAD) // LISTS
+    tiles = []
+    for u in range(unroll):
+        packed = lists_ref[HEAD + k * room + first + u]
+        tiles.append((packed & 255, (packed >> 8) & 255, packed >> 16))
+    return tiles
+
+
 def listed(lists_ref, k, body, carry, unroll=UNROLL):
-    room = (lists_ref.shape[0] - HEAD) // LISTS
-
     def group(step, carry):
-        tiles = []
-        for u in range(unroll):
-            packed = lists_ref[HEAD + k * room + step * unroll + u]
-            tiles.append((packed & 255, (packed >> 8) & 255, packed >> 16))
-        return body(step * unroll, tiles, carry)
+        return body(step * unroll, tiles_of(lists_ref, k, step * unroll, unroll), carry)
 
     return lax.fori_loop(0, (lists_ref[k] + unroll - 1) // unroll, group, carry)
 
@@ -77,10 +81,12 @@
     v_ref, diag_ref, spill_ref, head_ref, cot_ref, tiles_ref, lists_ref,
     rows_ref, cols_ref, count_ref, ground_ref, w_ref, acc_ref, sems,
 ):
-    pairs = (
+    pairs = [
         (rows_hbm, rows_ref), (cols_hbm, cols_ref), (count_hbm, count_ref),
-        (cot_hbm, cot_ref), (ground_hbm, ground_ref), (tiles_hbm, tiles_ref),
-    )
+        (cot_hbm, cot_ref), (ground_hbm, ground_ref),
+    ]
+    for k, size in CHUNKS:
+        pairs.append((tiles_hbm.at[pl.ds(k, size)], tiles_ref.at[pl.ds(k, size)]))
     copies = [pltpu.make_async_copy(src, dst, sems.at[k]) for k, (src, dst) in enumerate(pairs)]
     for copy in copies:
         copy.start()
@@ -97,21 +103,23 @@
     for b in range(NB_DEV):
         w_ref[b, :pats, :] = cot_ref[:, cols_of(b)].astype(BF16)
     copies[4].wait()
-    copies[5].wait()
 
     kept = acc_ref.shape[1]
 
-    def body(first, tiles, carry):
-        parts = []
-        for row, col, slot in tiles:
-            tile = tiles_ref[slot]
-            parts.append((dot(w_ref[col], tile, NT)[:kept], dot(w_ref[row], tile, NN)[:kept]))
-        for (row, col, slot), (forward, backward) in zip(tiles, parts):
-            acc_ref[row] += forward
-            acc_ref[col] += backward
-        return carry
-
-    listed(lists_ref, 3, body, 0)
+    for (k, size), copy in zip(CHUNKS, copies[5:]):
+        copy.wait()
+
+        @pl.when(k < count)
+        def _(k=k, size=size):
+            tiles = tiles_of(lists_ref, 3, k, size)
+            parts = []
+            for row, col, slot in tiles:
+                tile = tiles_ref[slot]
+                parts.append((dot(w_ref[col], tile, NT)[:kept], dot(w_ref[row], tile, NN)[:kept]))
+            for (row, col, slot), (forward, backward) in zip(tiles, parts):
+                acc_ref[row] += forward
+                acc_ref[col] += backward
+
     for b in range(NB_DEV):
         diag = ground_ref[b : b + 1, :] + acc_ref[b, pats : pats + 1, :]
         c = cot_ref[:, cols_of(b)]
@@ -166,7 +174,7 @@
 
 
 def outer_kernel(
-    lists_ref, cot_ref, v_ref, diag_ref, tiles_ref, spill_ref, before_ref, after_ref, sums_ref,
+    lists_ref, cot_ref, v_ref, diag_ref, tiles_ref, spill_ref, after_ref, before_ref, sums_ref,
     edges_ref, moments_ref, exact_ref, pair_ref, halo_ref, cross_ref,
 ):
     pats = cot_ref.shape[0]
@@ -339,31 +347,27 @@
 
 def late_grads_kernel(
     scale, part_ref, lists_ref, volt_hbm, low_hbm, high_hbm, partial_ref, prow0_ref, grads_ref,
-    field_ref, turned_ref, swapped_ref, prow_ref, sems,
+    field_ref, turned_ref, swapped_ref, prow_ref, rows_ref, cols_ref, sems,
 ):
     grads_ref[...] = jnp.zeros_like(grads_ref)
     prow_ref[...] = prow0_ref[...]
     gather_fields(part_ref[0], [(3, volt_hbm, low_hbm, high_hbm)], field_ref, turned_ref, swapped_ref, prow_ref, sems)
-    rows = lax.broadcasted_iota(jnp.int32, (16, BLOCK), 0)
-    ones = jnp.where(rows < 3, 1.0, 0.0).astype(BF16)
+    turn(part_ref[0], turned_ref, swapped_ref)
+    pick = chosen(part_ref[0]).astype(F32)
+    ones = jnp.ones((BLOCK, BLOCK), BF16)
     for b in range(EXT):
-        rest = -prow_ref[b : b + 1, :]
-        extra = jnp.zeros((16, BLOCK), F32)
-        for k in range(3):
-            piece = rest.astype(BF16).astype(F32)
-            rest = rest - piece
-            extra = jnp.where(rows == k, piece, extra)
-        extra = extra.astype(BF16)
-        field_ref[b, BLOCK : BLOCK + 16, :] = ones
-        field_ref[b, BLOCK + 16 :, :] = extra
-        swapped_ref[b, BLOCK : BLOCK + 16, :] = extra
-        swapped_ref[b, BLOCK + 16 :, :] = ones
-    turn(part_ref[0], turned_ref, swapped_ref)
+        row = prow_ref[b : b + 1, :]
+        cols_ref[b] = jnp.broadcast_to(row, (8, BLOCK))
+        if b < NB_DEV:
+            rows_ref[b] = jnp.broadcast_to(jnp.sum(pick * row, axis=1, keepdims=True), rows_ref.shape[1:])
+    cols_ref[TRASH] = jnp.zeros(cols_ref.shape[1:], F32)
+    rows_ref[TRASH] = jnp.zeros(rows_ref.shape[1:], F32)
     count = lists_ref[3]
 
     def body(first, tiles, carry):
         for u, (row, col, slot) in enumerate(tiles):
-            value = (partial_ref[first + u] + dot(turned_ref[row], field_ref[col], NN)) * scale
+            products = rows_ref[row] + cols_ref[col, 0:1, :]
+            value = (partial_ref[first + u] + dot(turned_ref[row], field_ref[col], NN) - products) * scale
             grads_ref[first + u] = jnp.where(first + u < count, value, 0.0).astype(BF16)
         return carry
 
@@ -373,6 +377,10 @@
 def shifted(shard, axis, by):
     size = lax.axis_size(axis)
     return lax.ppermute(shard, axis, [(i, (i + by) % size) for i in range(size)])
+
+
+def in_vmem(x):
+    return pltpu.with_memory_space_constraint(x, pltpu.VMEM)
 
 
 def in_hbm(x):
@@ -411,12 +419,12 @@
             (field, F32), ((NB_DEV, 8, BLOCK), F32), ((H, pats + 8, BLOCK), F32), ((2 * H, pats, BLOCK), F32),
             (cotangent.shape, F32), (tile_values.shape, BF16), ((HEAD + LISTS * (slots + UNROLL),), jnp.int32),
         ],
-        [ANY] * 6,
+        [ANY, ANY, VMEM, ANY, ANY, ANY],
         [
             pltpu.SMEM((slots,), jnp.int32), pltpu.SMEM((slots,), jnp.int32), pltpu.SMEM((1,), jnp.int32),
             pltpu.VMEM((NB_DEV, BLOCK), F32),
             pltpu.VMEM((EXT + 1, wide, BLOCK), BF16), pltpu.VMEM((EXT + 1, pats + 8, BLOCK), F32),
-            pltpu.SemaphoreType.DMA((6,)),
+            pltpu.SemaphoreType.DMA((5 + len(CHUNKS),)),
         ],
         in_hbm(tile_rows), in_hbm(tile_cols), tile_count,
         in_hbm(cotangent), in_hbm(ground.reshape(NB_DEV, BLOCK)), in_hbm(tile_values), us=4.0, last=SMEM,
@@ -437,7 +445,7 @@
         outer_kernel, "outer_sums",
         [((3 * H, pats, BLOCK), F32), ((devices, 1, 4 * pats), F32)], [SMEM] + [VMEM] * 8,
         [*work, pltpu.VMEM((H + 1, pats, BLOCK), BF16), pltpu.VMEM((H + 1, pats, BLOCK), F32)],
-        lists, cot, v, diag, tiles, spill, before, after, sums, us=60.0,
+        lists, cot, v, diag, tiles, spill, after, before, sums, us=60.0,
     )
     everyone = lax.all_to_all(moments, "blk", 0, 0)
     adjoint, low, high = call(
@@ -480,13 +488,14 @@
     scratch, sems = grad_work(2, 2 * BLOCK)
     partial, prow = call(
         near_grads_kernel, "near_grads", shares, [SMEM] * 2 + [ANY] * 5 + [VMEM] * 2, [*scratch, sems],
-        part, lists, volt, low_below, high_below, low_above, high_above, partial, prow, us=4.0,
-    )
-    scratch, sems = grad_work(1, BLOCK + 32)
+        part, lists, volt, *(in_vmem(x) for x in (low_below, high_below, low_above, high_above)), partial, prow, us=4.0,
+    )
+    scratch, sems = grad_work(1, BLOCK)
+    products = [pltpu.VMEM((EXT + 1, rows_out, BLOCK), F32), pltpu.VMEM((EXT + 1, 8, BLOCK), F32)]
     (grads,) = call(
         lambda *r: late_grads_kernel(1.0 / math.sqrt(parts * pats), *r), "late_grads",
         [((slots, rows_out, BLOCK), BF16)], [SMEM] * 2 + [ANY] * 3 + [VMEM] * 2,
-        [*scratch, pltpu.VMEM((EXT, BLOCK), F32), sems],
+        [*scratch, pltpu.VMEM((EXT, BLOCK), F32), *products, sems],
         part, lists, volt, low_opposite, high_opposite, partial, prow,
     )
     return adjoint, grads

time: 70.3 us -> 69.9 us (level); the launches traced: 70.2 us -> 70.8 us
  blocking collectives: 19.7 us -> 21.9 us
  Pallas kernels: 21.8 us -> 20.1 us
    all_to_all x1, blocking collectives: 19.7 us -> 21.9 us  [per_device(): everyone = lax.all_to_all(moments, 'blk', 0, 0)]
    pallas_call x8, Pallas kernels: 21.8 us -> 20.1 us  [call(): pl.pallas_call(kernel, name=name, out_shape=[jax.ShapeDtypeStruct(s, d) f...]
where the time goes in v5:
time: 69.9 us; the launch traced here: 70.8 us
  blocking collectives  21.9 us (31%)
  Pallas kernels  20.1 us (29%)
  starting transfers between devices  15.9 us (23%)
  waiting for transfers between devices  11.3 us (16%)
  between operations  1.61 us (2%)
    all_to_all x1, blocking collectives, per_device(): everyone = lax.all_to_all(moments, 'blk', 0, 0)  21.9 us
    pallas_call x8, Pallas kernels, call(): pl.pallas_call(kernel, name=name, out_shape=[jax.ShapeDtypeStruct(s, d) f...  20.1 us
    ppermute x12, starting transfers between devices, shifted(): lax.ppermute(shard, axis, [(i, (i + by) % size) for i in range(size)])  15.9 us
    ppermute x12, waiting for transfers between devices, shifted(): lax.ppermute(shard, axis, [(i, (i + by) % size) for i in range(size)])  11.3 us
  transfers between devices with their start and end apart: 12, of which 4 were waited for; matrix products, arithmetic and copies ran while one was open for 0% of the time, Pallas kernels for 18%

profile of v5, /device:TPU:1, one launch (start us, length us, event | category | flops | bytes accessed | tf_op | source)
XLA Modules:
  0.0 70.8 jit_solution(12890250477676095576)
XLA Ops:
  1.3 4.0 %first_product.1 = (f32[32,64,128]{2,1,0:T(8,128)S(1)}, f32[32,8,128]{2,1,0:T(8,128)S(1)}, f32[4,72,128]{2,1,0:T(8,128)S(1)}, f32[8,64,128]{2,1,0:T(8,128)S(1)},...) custom-call(s32[96]{0:T(128)} %r_0_.1, s32[96]{0:T(128)} %r_1_.1, s32[1]{0:T(128)S(6)} %copy.9.r_2_, ...), custom_call_target="tpu_custom_call" | custom-call | bytes 14760000 | tf_op jit(solution)/shard_map/first_product/pallas_call | solution.py:391
  5.3 3.8 %collective-permute-start.6 = (bf16[64,4096]{1,0:T(8,128)(2,1)S(1)}, bf16[64,4096]{1,0:T(8,128)(2,1)S(1)}, u32[]{:S(2)}, u32[]{:S(2)}) collective-permute-start(bf16[64,4096]{1,0:T(8,128)(2,1)S(1)} %copy-done), channel_id=1, source_target_pairs={{0,128},{64,192},{128,0},{192,64},{1,129},{65,193},{129,1},{193,65... | collective-permute-start | bytes 1572872 | tf_op jit(solution)/shard_map/ppermute | solution.py:379
  9.2 0.8 %collective-permute-start.5 = (bf16[64,4096]{1,0:T(8,128)(2,1)S(1)}, bf16[64,4096]{1,0:T(8,128)(2,1)S(1)}, u32[]{:S(2)}, u32[]{:S(2)}) collective-permute-start(bf16[64,4096]{1,0:T(8,128)(2,1)S(1)} %copy-done), channel_id=1, source_target_pairs={{0,192},{64,0},{128,64},{192,128},{1,193},{65,1},{129,65},{193,129... | collective-permute-start | bytes 1572872 | tf_op jit(solution)/shard_map/ppermute | solution.py:379
  9.9 0.7 collective-permute-start.4
  10.6 0.9 %collective-permute-start = (f32[8,64,128]{2,1,0:T(8,128)S(1)}, f32[8,64,128]{2,1,0:T(8,128)S(1)}, u32[]{:S(2)}, u32[]{:S(2)}) collective-permute-start(f32[8,64,128]{2,1,0:T(8,128)S(1)} %get-tuple-element.32), channel_id=1, source_target_pairs={{0,63},{1,0},{2,1},{3,2},{4,3},{5,4},{6,5},{7,6},{8,7},{9,8},{10,9... | collective-permute-start | bytes 786440 | tf_op jit(solution)/shard_map/ppermute | solution.py:379
  11.5 1.5 %collective-permute-start.1 = (f32[4,72,128]{2,1,0:T(8,128)S(1)}, f32[4,72,128]{2,1,0:T(8,128)S(1)}, u32[]{:S(2)}, u32[]{:S(2)}) collective-permute-start(f32[4,72,128]{2,1,0:T(8,128)S(1)} %get-tuple-element.31.spill_ref), channel_id=1, source_target_pairs={{0,1},{1,2},{2,3},{3,4},{4,5},{5,6},{6,7},{7,8},{8,9},{9,10},{10,1... | collective-permute-start | bytes 442376 | tf_op jit(solution)/shard_map/ppermute | solution.py:379
  13.1 1.7 %inner_sums.1.sums_ref = f32[4,64,128]{2,1,0:T(8,128)S(1)} custom-call(s32[520]{0:T(1024)S(1)} %get-tuple-element.24.lists_ref.r_1_, f32[64,4096]{1,0:T(8,128)S(1)} %get-tuple-element.25.cot_ref, f32[32,64,128]{2,1,0:T(8,128)S(1)} %get-tuple-element.26.v_ref, f32[32,8,128]{2,1,0:T(8,128)S(1)} %get-tuple-element.27.diag_ref, ...), custom_call_target="tpu_custom_call" | custom-call | bytes 18450000 | tf_op jit(solution)/shard_map/inner_sums/pallas_call | solution.py:391
  14.8 4.8 %collective-permute-done.1.before_ref = f32[4,72,128]{2,1,0:T(8,128)S(1)} collective-permute-done((f32[4,72,128]{2,1,0:T(8,128)S(1)}, f32[4,72,128]{2,1,0:T(8,128)S(1)}, u32[]{:S(2)}, u32[]{:S(2)}) %collective-permute-start.1) | collective-permute-done | bytes 147488 | tf_op jit(solution)/shard_map/ppermute | solution.py:379
  19.7 0.0 collective-permute-done.after_ref
  19.7 2.2 %outer_sums.1 = (f32[12,64,128]{2,1,0:T(8,128)S(1)}, f32[64,1,256]{2,1,0:T(1,128)S(1)}) custom-call(s32[520]{0:T(1024)S(1)} %get-tuple-element.24.lists_ref.r_1_, f32[64,4096]{1,0:T(8,128)S(1)} %get-tuple-element.25.cot_ref, f32[32,64,128]{2,1,0:T(8,128)S(1)} %get-tuple-element.26.v_ref, f32[32,8,128]{2,1,0:T(8,128)S(1)} %get-tuple-element.27.diag_ref, ...), custom_call_target="tpu_custom_call" | custom-call | bytes 221400000 | tf_op jit(solution)/shard_map/outer_sums/pallas_call | solution.py:391
  21.8 21.9 %all_to_all.5.all_ref = f32[64,1,256]{2,1,0:T(1,128)S(1)} all-to-all(f32[64,1,256]{2,1,0:T(1,128)S(1)} %get-tuple-element.33), channel_id=1, replica_groups=mesh['pat'=4,'blk'=64] {'blk'}, dimensions={0} | all-to-all | bytes 131072 | tf_op jit(solution)/shard_map/all_to_all | solution.py:450
  43.8 1.5 %combine.1 = (f32[64,4096]{1,0:T(8,128)}, bf16[18,64,128]{2,1,0:T(8,128)(2,1)S(1)}, bf16[18,64,128]{2,1,0:T(8,128)(2,1)S(1)}) custom-call(f32[64,1,256]{2,1,0:T(1,128)S(1)} %all_to_all.5.all_ref, f32[64,4096]{1,0:T(8,128)S(1)} %get-tuple-element.25.cot_ref, f32[8,64,128]{2,1,0:T(8,128)S(1)} %collective-permute-done.after_ref, ...), custom_call_target="tpu_custom_call" | custom-call | bytes 369000 | tf_op jit(solution)/shard_map/combine/pallas_call | solution.py:391
  45.3 0.4 collective-permute-start.2
  45.7 2.3 %collective-permute-start.3 = (bf16[18,64,128]{2,1,0:T(8,128)(2,1)S(1)}, bf16[18,64,128]{2,1,0:T(8,128)(2,1)}, u32[]{:S(2)}, u32[]{:S(2)}) collective-permute-start(bf16[18,64,128]{2,1,0:T(8,128)(2,1)S(1)} %get-tuple-element.37.high_hbm), channel_id=1, source_target_pairs={{0,192},{64,0},{128,64},{192,128},{1,193},{65,1},{129,65},{193,129... | collective-permute-start | bytes 884744 | tf_op jit(solution)/shard_map/ppermute | solution.py:379
  47.9 0.0 collective-permute-done.6.opposite_hbm
  47.9 0.0 collective-permute-done.5.above_hbm
  47.9 0.0 collective-permute-done.4.below_hbm
  48.0 1.2 %collective-permute-start.7 = (bf16[4,64,512]{2,1,0:T(8,128)(2,1)S(1)}, bf16[4,64,512]{2,1,0:T(8,128)(2,1)S(1)}, u32[]{:S(2)}, u32[]{:S(2)}) collective-permute-start(bf16[4,64,512]{2,1,0:T(8,128)(2,1)S(1)} %pad_maximum_fusion), channel_id=1, source_target_pairs={{0,63},{1,0},{2,1},{3,2},{4,3},{5,4},{6,5},{7,6},{8,7},{9,8},{10,9... | collective-permute-start | bytes 786440 | tf_op jit(solution)/shard_map/ppermute | solution.py:379
  49.2 0.8 %collective-permute-start.11 = (bf16[18,64,128]{2,1,0:T(8,128)(2,1)S(1)}, bf16[18,64,128]{2,1,0:T(8,128)(2,1)}, u32[]{:S(2)}, u32[]{:S(2)}) collective-permute-start(bf16[18,64,128]{2,1,0:T(8,128)(2,1)S(1)} %get-tuple-element.36.low_hbm), channel_id=1, source_target_pairs={{0,192},{64,0},{128,64},{192,128},{1,193},{65,1},{129,65},{193,129... | collective-permute-start | bytes 884744 | tf_op jit(solution)/shard_map/ppermute | solution.py:379
  50.0 0.7 collective-permute-start.10
  50.7 3.8 %collective-permute-done.7.far_hbm = bf16[4,64,512]{2,1,0:T(8,128)(2,1)S(1)} collective-permute-done((bf16[4,64,512]{2,1,0:T(8,128)(2,1)S(1)}, bf16[4,64,512]{2,1,0:T(8,128)(2,1)S(1)}, u32[]{:S(2)}, u32[]{:S(2)}) %collective-permute-start.7) | collective-permute-done | bytes 262176 | tf_op jit(solution)/shard_map/ppermute | solution.py:379
  54.4 0.6 volt_blocks.1.volt_hbm.r_2_
  55.1 0.0 collective-permute-done.2.low0_hbm
  55.1 0.1 collective-permute-start.8
  55.2 2.7 %collective-permute-start.9 = (bf16[18,64,128]{2,1,0:T(8,128)(2,1)}, bf16[18,64,128]{2,1,0:T(8,128)(2,1)S(1)}, u32[]{:S(2)}, u32[]{:S(2)}) collective-permute-start(bf16[18,64,128]{2,1,0:T(8,128)(2,1)} %collective-permute-done.3.high1_hbm), channel_id=1, source_target_pairs={{0,192},{64,0},{128,64},{192,128},{1,193},{65,1},{129,65},{193,129... | collective-permute-start | bytes 884744 | tf_op jit(solution)/shard_map/ppermute | solution.py:379
  57.8 2.4 %own_grads.1 = (f32[96,32,128]{2,1,0:T(8,128)S(1)}, f32[36,128]{1,0:T(8,128)S(1)}) custom-call(s32[1]{0:T(128)} %bitcast.1.part_ref.r_0_, s32[520]{0:T(1024)S(1)} %get-tuple-element.24.lists_ref.r_1_, bf16[36,256,128]{2,1,0:T(8,128)(2,1)S(1)} %volt_blocks.1.volt_hbm.r_2_, bf16[18,64,128]{2,1,0:T(8,128)(2,1)S(1)} %get-tuple-element.36.low_hbm, ...), custom_call_target="tpu_custom_call" | custom-call | bytes 11070000 | tf_op jit(solution)/shard_map/own_grads/pallas_call | solution.py:391
  60.2 0.0 collective-permute-done.11.low1_hbm
  60.3 0.8 %collective-permute-done.10.high0_hbm = bf16[18,64,128]{2,1,0:T(8,128)(2,1)} collective-permute-done((bf16[18,64,128]{2,1,0:T(8,128)(2,1)S(1)}, bf16[18,64,128]{2,1,0:T(8,128)(2,1)}, u32[]{:S(2)}, u32[]{:S(2)}) %collective-permute-start.10) | collective-permute-done | bytes 294944 | tf_op jit(solution)/shard_map/ppermute | solution.py:379
  61.1 4.4 %near_grads.1 = (f32[96,32,128]{2,1,0:T(8,128)S(1)}, f32[36,128]{1,0:T(8,128)S(1)}) custom-call(s32[1]{0:T(128)} %bitcast.1.part_ref.r_0_, s32[520]{0:T(1024)S(1)} %get-tuple-element.24.lists_ref.r_1_, bf16[36,256,128]{2,1,0:T(8,128)(2,1)S(1)} %volt_blocks.1.volt_hbm.r_2_, bf16[18,64,128]{2,1,0:T(8,128)(2,1)} %collective-permute-done.2.low0_hbm, ...), custom_call_target="tpu_custom_call" | custom-call | bytes 14760000 | tf_op jit(solution)/shard_map/near_grads/pallas_call | solution.py:391
  65.5 1.8 %collective-permute-done.8.r_3_ = bf16[18,64,128]{2,1,0:T(8,128)(2,1)S(1)} collective-permute-done((bf16[18,64,128]{2,1,0:T(8,128)(2,1)}, bf16[18,64,128]{2,1,0:T(8,128)(2,1)S(1)}, u32[]{:S(2)}, u32[]{:S(2)}) %collective-permute-start.8) | collective-permute-done | bytes 294944 | tf_op jit(solution)/shard_map/ppermute | solution.py:379
  67.3 0.0 collective-permute-done.9.r_4_
  67.3 3.3 %late_grads.1 = bf16[96,32,128]{2,1,0:T(8,128)(2,1)} custom-call(s32[1]{0:T(128)} %bitcast.1.part_ref.r_0_, s32[520]{0:T(1024)S(1)} %get-tuple-element.24.lists_ref.r_1_, bf16[36,256,128]{2,1,0:T(8,128)(2,1)S(1)} %volt_blocks.1.volt_hbm.r_2_, bf16[18,64,128]{2,1,0:T(8,128)(2,1)S(1)} %collective-permute-done.8.r_3_, ...), custom_call_target="tpu_custom_call" | custom-call | bytes 3690000 | tf_op jit(solution)/shard_map/late_grads/pallas_call | solution.py:391
  (4 shorter events, 0.0 us)
Async XLA Ops:
  0.6 4.7 %copy-start = (bf16[64,4096]{1,0:T(8,128)(2,1)S(1)}, bf16[64,4096]{1,0:T(8,128)(2,1)}, u32[]{:S(2)}) copy-start(bf16[64,4096]{1,0:T(8,128)(2,1)} %own_hbm.1) | copy-start | bytes 1572868
  5.3 42.6 %collective-permute-start.6 = (bf16[64,4096]{1,0:T(8,128)(2,1)S(1)}, bf16[64,4096]{1,0:T(8,128)(2,1)S(1)}, u32[]{:S(2)}, u32[]{:S(2)}) collective-permute-start(bf16[64,4096]{1,0:T(8,128)(2,1)S(1)} %copy-done), channel_id=1, source_target_pairs={{0,128},{64,192},{128,0},{192,64},{1,129},{65,193},{129,1},{193,65... | collective-permute-start | bytes 1572872 | tf_op jit(solution)/shard_map/ppermute | solution.py:379
  9.2 38.8 %collective-permute-start.5 = (bf16[64,4096]{1,0:T(8,128)(2,1)S(1)}, bf16[64,4096]{1,0:T(8,128)(2,1)S(1)}, u32[]{:S(2)}, u32[]{:S(2)}) collective-permute-start(bf16[64,4096]{1,0:T(8,128)(2,1)S(1)} %copy-done), channel_id=1, source_target_pairs={{0,192},{64,0},{128,64},{192,128},{1,193},{65,1},{129,65},{193,129... | collective-permute-start | bytes 1572872 | tf_op jit(solution)/shard_map/ppermute | solution.py:379
  9.9 38.0 %collective-permute-start.4 = (bf16[64,4096]{1,0:T(8,128)(2,1)S(1)}, bf16[64,4096]{1,0:T(8,128)(2,1)S(1)}, u32[]{:S(2)}, u32[]{:S(2)}) collective-permute-start(bf16[64,4096]{1,0:T(8,128)(2,1)S(1)} %copy-done), channel_id=1, source_target_pairs={{0,64},{64,128},{128,192},{192,0},{1,65},{65,129},{129,193},{193,1... | collective-permute-start | bytes 1572872 | tf_op jit(solution)/shard_map/ppermute | solution.py:379
  10.6 9.0 %collective-permute-start = (f32[8,64,128]{2,1,0:T(8,128)S(1)}, f32[8,64,128]{2,1,0:T(8,128)S(1)}, u32[]{:S(2)}, u32[]{:S(2)}) collective-permute-start(f32[8,64,128]{2,1,0:T(8,128)S(1)} %get-tuple-element.32), channel_id=1, source_target_pairs={{0,63},{1,0},{2,1},{3,2},{4,3},{5,4},{6,5},{7,6},{8,7},{9,8},{10,9... | collective-permute-start | bytes 786440 | tf_op jit(solution)/shard_map/ppermute | solution.py:379
  11.5 8.1 %collective-permute-start.1 = (f32[4,72,128]{2,1,0:T(8,128)S(1)}, f32[4,72,128]{2,1,0:T(8,128)S(1)}, u32[]{:S(2)}, u32[]{:S(2)}) collective-permute-start(f32[4,72,128]{2,1,0:T(8,128)S(1)} %get-tuple-element.31.spill_ref), channel_id=1, source_target_pairs={{0,1},{1,2},{2,3},{3,4},{4,5},{5,6},{6,7},{7,8},{8,9},{9,10},{10,1... | collective-permute-start | bytes 442376 | tf_op jit(solution)/shard_map/ppermute | solution.py:379
  45.3 9.8 %collective-permute-start.2 = (bf16[18,64,128]{2,1,0:T(8,128)(2,1)S(1)}, bf16[18,64,128]{2,1,0:T(8,128)(2,1)}, u32[]{:S(2)}, u32[]{:S(2)}) collective-permute-start(bf16[18,64,128]{2,1,0:T(8,128)(2,1)S(1)} %get-tuple-element.36.low_hbm), channel_id=1, source_target_pairs={{0,64},{64,128},{128,192},{192,0},{1,65},{65,129},{129,193},{193,1... | collective-permute-start | bytes 884744 | tf_op jit(solution)/shard_map/ppermute | solution.py:379
  45.7 9.4 %collective-permute-start.3 = (bf16[18,64,128]{2,1,0:T(8,128)(2,1)S(1)}, bf16[18,64,128]{2,1,0:T(8,128)(2,1)}, u32[]{:S(2)}, u32[]{:S(2)}) collective-permute-start(bf16[18,64,128]{2,1,0:T(8,128)(2,1)S(1)} %get-tuple-element.37.high_hbm), channel_id=1, source_target_pairs={{0,192},{64,0},{128,64},{192,128},{1,193},{65,1},{129,65},{193,129... | collective-permute-start | bytes 884744 | tf_op jit(solution)/shard_map/ppermute | solution.py:379
  48.0 6.5 %collective-permute-start.7 = (bf16[4,64,512]{2,1,0:T(8,128)(2,1)S(1)}, bf16[4,64,512]{2,1,0:T(8,128)(2,1)S(1)}, u32[]{:S(2)}, u32[]{:S(2)}) collective-permute-start(bf16[4,64,512]{2,1,0:T(8,128)(2,1)S(1)} %pad_maximum_fusion), channel_id=1, source_target_pairs={{0,63},{1,0},{2,1},{3,2},{4,3},{5,4},{6,5},{7,6},{8,7},{9,8},{10,9... | collective-permute-start | bytes 786440 | tf_op jit(solution)/shard_map/ppermute | solution.py:379
  49.2 11.1 %collective-permute-start.11 = (bf16[18,64,128]{2,1,0:T(8,128)(2,1)S(1)}, bf16[18,64,128]{2,1,0:T(8,128)(2,1)}, u32[]{:S(2)}, u32[]{:S(2)}) collective-permute-start(bf16[18,64,128]{2,1,0:T(8,128)(2,1)S(1)} %get-tuple-element.36.low_hbm), channel_id=1, source_target_pairs={{0,192},{64,0},{128,64},{192,128},{1,193},{65,1},{129,65},{193,129... | collective-permute-start | bytes 884744 | tf_op jit(solution)/shard_map/ppermute | solution.py:379
  50.0 11.1 %collective-permute-start.10 = (bf16[18,64,128]{2,1,0:T(8,128)(2,1)S(1)}, bf16[18,64,128]{2,1,0:T(8,128)(2,1)}, u32[]{:S(2)}, u32[]{:S(2)}) collective-permute-start(bf16[18,64,128]{2,1,0:T(8,128)(2,1)S(1)} %get-tuple-element.37.high_hbm), channel_id=1, source_target_pairs={{0,64},{64,128},{128,192},{192,0},{1,65},{65,129},{129,193},{193,1... | collective-permute-start | bytes 884744 | tf_op jit(solution)/shard_map/ppermute | solution.py:379
  55.1 12.2 %collective-permute-start.8 = (bf16[18,64,128]{2,1,0:T(8,128)(2,1)}, bf16[18,64,128]{2,1,0:T(8,128)(2,1)S(1)}, u32[]{:S(2)}, u32[]{:S(2)}) collective-permute-start(bf16[18,64,128]{2,1,0:T(8,128)(2,1)} %collective-permute-done.2.low0_hbm), channel_id=1, source_target_pairs={{0,64},{64,128},{128,192},{192,0},{1,65},{65,129},{129,193},{193,1... | collective-permute-start | bytes 884744 | tf_op jit(solution)/shard_map/ppermute | solution.py:379
  55.2 12.1 %collective-permute-start.9 = (bf16[18,64,128]{2,1,0:T(8,128)(2,1)}, bf16[18,64,128]{2,1,0:T(8,128)(2,1)S(1)}, u32[]{:S(2)}, u32[]{:S(2)}) collective-permute-start(bf16[18,64,128]{2,1,0:T(8,128)(2,1)} %collective-permute-done.3.high1_hbm), channel_id=1, source_target_pairs={{0,192},{64,0},{128,64},{192,128},{1,193},{65,1},{129,65},{193,129... | collective-permute-start | bytes 884744 | tf_op jit(solution)/shard_map/ppermute | solution.py:379

commit v6 on v5

--- a/solution.py
+++ b/solution.py
@@ -174,9 +174,11 @@
 
 
 def outer_kernel(
-    lists_ref, cot_ref, v_ref, diag_ref, tiles_ref, spill_ref, after_ref, before_ref, sums_ref,
-    edges_ref, moments_ref, exact_ref, pair_ref, halo_ref, cross_ref,
+    lists_hbm, cot_ref, v_ref, diag_ref, tiles_ref, spill_ref, after_ref, before_ref, sums_ref,
+    edges_ref, moments_ref, exact_ref, pair_ref, halo_ref, cross_ref, lists_ref, sem,
 ):
+    fetch = pltpu.make_async_copy(lists_hbm, lists_ref, sem)
+    fetch.start()
     pats = cot_ref.shape[0]
     zero = jnp.zeros((pats, BLOCK), F32)
     for b in range(H):
@@ -185,14 +187,12 @@
     halo_ref[H] = jnp.zeros((pats, BLOCK), BF16)
     cross_ref[H] = zero
 
-    def body(first, tiles, carry):
-        parts = [dot(halo_ref[col - NB_DEV], tiles_ref[slot], NT) for row, col, slot in tiles]
-        for (row, col, slot), part in zip(tiles, parts):
-            cross_ref[jnp.minimum(row - (NB_DEV - H), H)] += part
-        return carry
-
-    listed(lists_ref, 1, body, 0, 8)
     m1, m2, m3 = sums_ref[1], sums_ref[2], sums_ref[3]
+
+    def place(where, value):
+        exact_ref[where] = value
+        pair_ref[where] = split(value)
+
     for b in range(H):
         c = cot_ref[:, cols_of(b)]
         degree = before_ref[b, pats : pats + 1, :]
@@ -201,6 +201,22 @@
         m2 = m2 + v * v
         m3 = m3 + (diag_ref[b, 0:1, :] + degree) * (v * v)
         edges_ref[b] = v
+        beyond = after_ref[H + b] + spill_ref[b, pats : pats + 1, :] * after_ref[b] - spill_ref[b, :pats, :]
+        edges_ref[2 * H + b] = beyond
+        place(b, v)
+        place(NB_DEV + b, beyond)
+        place(H + b, v_ref[H + b])
+        place(NB_DEV - 2 * H + b, v_ref[NB_DEV - 2 * H + b])
+    fetch.wait()
+
+    def body(first, tiles, carry):
+        parts = [dot(halo_ref[col - NB_DEV], tiles_ref[slot], NT) for row, col, slot in tiles]
+        for (row, col, slot), part in zip(tiles, parts):
+            cross_ref[jnp.minimum(row - (NB_DEV - H), H)] += part
+        return carry
+
+    listed(lists_ref, 1, body, 0, 8)
+    for b in range(H):
         last = NB_DEV - H + b
         c = cot_ref[:, cols_of(last)]
         u = v_ref[last] - cross_ref[b]
@@ -208,11 +224,7 @@
         m2 = m2 + u * u
         m3 = m3 + diag_ref[last, 0:1, :] * (u * u)
         edges_ref[H + b] = u
-        beyond = after_ref[H + b] + spill_ref[b, pats : pats + 1, :] * after_ref[b] - spill_ref[b, :pats, :]
-        edges_ref[2 * H + b] = beyond
-        for where, value in ((b, v), (last, u), (NB_DEV + b, beyond), (H + b, v_ref[H + b]), (last - H, v_ref[last - H])):
-            exact_ref[where] = value
-            pair_ref[where] = split(value)
+        place(last, u)
     exact_ref[TRASH] = zero
     pair_ref[TRASH] = jnp.zeros((2 * pats, BLOCK), BF16)
     m3 = m3 - 2.0 * quadratic(lists_ref, 2, tiles_ref, exact_ref, pair_ref, 16)
@@ -278,7 +290,7 @@
             volt_ref[NB_DEV + b, k * pats : (k + 1) * pats, :] = far_ref[k, :, cols_of(b)]
 
 
-def gather_fields(part, groups, field_ref, turned_ref, swapped_ref, prow_ref, sems):
+def gather_fields(lists_hbm, lists_ref, groups, field_ref, turned_ref, swapped_ref, prow_ref, sems):
     copies = []
 
     def copy(src, dst):
@@ -294,6 +306,7 @@
             copy(volt, ref.at[pl.ds(0, EXT), pl.ds(at + volt_at, pats), :])
             copy(low_hbm, ref.at[pl.ds(0, half), pl.ds(at + lam_at, pats), :])
             copy(high_hbm, ref.at[pl.ds(half, EXT - half), pl.ds(at + lam_at, pats), :])
+    copy(lists_hbm, lists_ref)
     for made in copies:
         made.wait()
     count = len(groups)
@@ -314,11 +327,11 @@
         turned_ref[b] = dot(pick, swapped_ref[b], NT).astype(BF16)
 
 
-def own_grads_kernel(part_ref, lists_ref, volt_hbm, low_hbm, high_hbm, partial_ref, prow_ref, *refs):
-    field_ref, turned_ref, swapped_ref, sems = refs
+def own_grads_kernel(lists_hbm, volt_hbm, low_hbm, high_hbm, partial_ref, prow_ref, *refs):
+    field_ref, turned_ref, swapped_ref, lists_ref, sems = refs
     prow_ref[...] = jnp.zeros_like(prow_ref)
-    gather_fields(part_ref[0], [(0, volt_hbm, low_hbm, high_hbm)], field_ref, turned_ref, swapped_ref, prow_ref, sems)
-    turn(part_ref[0], turned_ref, swapped_ref)
+    gather_fields(lists_hbm, lists_ref, [(0, volt_hbm, low_hbm, high_hbm)], field_ref, turned_ref, swapped_ref, prow_ref, sems)
+    turn(lax.axis_index("pat"), turned_ref, swapped_ref)
 
     def body(first, tiles, carry):
         for u, (row, col, slot) in enumerate(tiles):
@@ -329,13 +342,13 @@
 
 
 def near_grads_kernel(
-    part_ref, lists_ref, volt_hbm, low0_hbm, high0_hbm, low1_hbm, high1_hbm, before_ref, prow0_ref,
-    partial_ref, prow_ref, field_ref, turned_ref, swapped_ref, sems,
+    lists_hbm, volt_hbm, low0_hbm, high0_hbm, low1_hbm, high1_hbm, before_ref, prow0_ref,
+    partial_ref, prow_ref, field_ref, turned_ref, swapped_ref, lists_ref, sems,
 ):
     prow_ref[...] = prow0_ref[...]
     groups = [(1, volt_hbm, low0_hbm, high0_hbm), (2, volt_hbm, low1_hbm, high1_hbm)]
-    gather_fields(part_ref[0], groups, field_ref, turned_ref, swapped_ref, prow_ref, sems)
-    turn(part_ref[0], turned_ref, swapped_ref)
+    gather_fields(lists_hbm, lists_ref, groups, field_ref, turned_ref, swapped_ref, prow_ref, sems)
+    turn(lax.axis_index("pat"), turned_ref, swapped_ref)
 
     def body(first, tiles, carry):
         for u, (row, col, slot) in enumerate(tiles):
@@ -346,14 +359,14 @@
 
 
 def late_grads_kernel(
-    scale, part_ref, lists_ref, volt_hbm, low_hbm, high_hbm, partial_ref, prow0_ref, grads_ref,
-    field_ref, turned_ref, swapped_ref, prow_ref, rows_ref, cols_ref, sems,
+    scale, lists_hbm, volt_hbm, low_hbm, high_hbm, partial_ref, prow0_ref, grads_ref,
+    field_ref, turned_ref, swapped_ref, prow_ref, rows_ref, cols_ref, lists_ref, sems,
 ):
     grads_ref[...] = jnp.zeros_like(grads_ref)
     prow_ref[...] = prow0_ref[...]
-    gather_fields(part_ref[0], [(3, volt_hbm, low_hbm, high_hbm)], field_ref, turned_ref, swapped_ref, prow_ref, sems)
-    turn(part_ref[0], turned_ref, swapped_ref)
-    pick = chosen(part_ref[0]).astype(F32)
+    gather_fields(lists_hbm, lists_ref, [(3, volt_hbm, low_hbm, high_hbm)], field_ref, turned_ref, swapped_ref, prow_ref, sems)
+    turn(lax.axis_index("pat"), turned_ref, swapped_ref)
+    pick = chosen(lax.axis_index("pat")).astype(F32)
     ones = jnp.ones((BLOCK, BLOCK), BF16)
     for b in range(EXT):
         row = prow_ref[b : b + 1, :]
@@ -408,7 +421,6 @@
     blocks_all = NB_DEV * devices
     wide = pats + 16
     half = EXT // 2
-    part = lax.axis_index("pat").astype(jnp.int32).reshape(1)
     field = (NB_DEV, pats, BLOCK)
     edge = (H, pats, BLOCK)
     rows_out = BLOCK // parts
@@ -443,8 +455,11 @@
     )
     edges, moments = call(
         outer_kernel, "outer_sums",
-        [((3 * H, pats, BLOCK), F32), ((devices, 1, 4 * pats), F32)], [SMEM] + [VMEM] * 8,
-        [*work, pltpu.VMEM((H + 1, pats, BLOCK), BF16), pltpu.VMEM((H + 1, pats, BLOCK), F32)],
+        [((3 * H, pats, BLOCK), F32), ((devices, 1, 4 * pats), F32)], [ANY] + [VMEM] * 8,
+        [
+            *work, pltpu.VMEM((H + 1, pats, BLOCK), BF16), pltpu.VMEM((H + 1, pats, BLOCK), F32),
+            pltpu.SMEM(lists.shape, jnp.int32), pltpu.SemaphoreType.DMA,
+        ],
         lists, cot, v, diag, tiles, spill, after, before, sums, us=60.0,
     )
     everyone = lax.all_to_all(moments, "blk", 0, 0)
@@ -474,12 +489,12 @@
             pltpu.VMEM((EXT + 1, depth, BLOCK), BF16),
             pltpu.VMEM((EXT + 1, rows_out, depth), BF16),
             pltpu.VMEM((EXT + 1, depth, BLOCK), BF16),
-        ], pltpu.SemaphoreType.DMA((6 * groups,))
+        ], [pltpu.SMEM(lists.shape, jnp.int32), pltpu.SemaphoreType.DMA((6 * groups + 1,))]
 
     shares = [((slots, rows_out, BLOCK), F32), ((EXT, BLOCK), F32)]
     scratch, sems = grad_work(1, BLOCK)
     partial, prow = call(
-        own_grads_kernel, "own_grads", shares, [SMEM] * 2 + [ANY] * 3, [*scratch, sems], part, lists, volt, low, high,
+        own_grads_kernel, "own_grads", shares, [ANY] * 4, [*scratch, *sems], lists, volt, low, high,
         us=3.0,
     )
     low_below, high_above, volt = lax.optimization_barrier((low_below, high_above, volt))
@@ -487,16 +502,16 @@
     high_opposite = shifted(high_above, "pat", -1)
     scratch, sems = grad_work(2, 2 * BLOCK)
     partial, prow = call(
-        near_grads_kernel, "near_grads", shares, [SMEM] * 2 + [ANY] * 5 + [VMEM] * 2, [*scratch, sems],
-        part, lists, volt, *(in_vmem(x) for x in (low_below, high_below, low_above, high_above)), partial, prow, us=4.0,
+        near_grads_kernel, "near_grads", shares, [ANY] * 6 + [VMEM] * 2, [*scratch, *sems],
+        lists, volt, *(in_vmem(x) for x in (low_below, high_below, low_above, high_above)), partial, prow, us=4.0,
     )
     scratch, sems = grad_work(1, BLOCK)
     products = [pltpu.VMEM((EXT + 1, rows_out, BLOCK), F32), pltpu.VMEM((EXT + 1, 8, BLOCK), F32)]
     (grads,) = call(
         lambda *r: late_grads_kernel(1.0 / math.sqrt(parts * pats), *r), "late_grads",
-        [((slots, rows_out, BLOCK), BF16)], [SMEM] * 2 + [ANY] * 3 + [VMEM] * 2,
-        [*scratch, pltpu.VMEM((EXT, BLOCK), F32), *products, sems],
-        part, lists, volt, low_opposite, high_opposite, partial, prow,
+        [((slots, rows_out, BLOCK), BF16)], [ANY] * 4 + [VMEM] * 2,
+        [*scratch, pltpu.VMEM((EXT, BLOCK), F32), *products, *sems],
+        lists, volt, low_opposite, high_opposite, partial, prow,
     )
     return adjoint, grads
 

time: 69.9 us -> 68.3 us (0.977); the launches traced: 70.8 us -> 67.9 us
  Pallas kernels: 20.1 us -> 18.2 us
  blocking collectives: 21.9 us -> 20.2 us
  waiting for transfers between devices: 11.3 us -> 12 us
    pallas_call x8, Pallas kernels: 20.1 us -> 18.2 us  [call(): pl.pallas_call(kernel, name=name, out_shape=[jax.ShapeDtypeStruct(s, d) f...]
    all_to_all x1, blocking collectives: 21.9 us -> 20.2 us  [per_device(): everyone = lax.all_to_all(moments, 'blk', 0, 0)]
    ppermute x12, waiting for transfers between devices: 11.3 us -> 12 us  [shifted(): lax.ppermute(shard, axis, [(i, (i + by) % size) for i in range(size)])]
  transfers between devices with their start and end apart: 12 -> 12, of which waited for: 4 -> 4; matrix products, arithmetic and copies ran while one was open for 0% -> 0% of each run, Pallas kernels for 18% -> 16%
where the time goes in v6:
time: 68.3 us; the launch traced here: 67.9 us
  blocking collectives  20.2 us (30%)
  Pallas kernels  18.2 us (27%)
  starting transfers between devices  15.8 us (23%)
  waiting for transfers between devices  12 us (18%)
  between operations  1.61 us (2%)
    all_to_all x1, blocking collectives, per_device(): everyone = lax.all_to_all(moments, 'blk', 0, 0)  20.2 us
    pallas_call x8, Pallas kernels, call(): pl.pallas_call(kernel, name=name, out_shape=[jax.ShapeDtypeStruct(s, d) f...  18.2 us
    ppermute x12, starting transfers between devices, shifted(): lax.ppermute(shard, axis, [(i, (i + by) % size) for i in range(size)])  15.8 us
    ppermute x12, waiting for transfers between devices, shifted(): lax.ppermute(shard, axis, [(i, (i + by) % size) for i in range(size)])  12 us
  transfers between devices with their start and end apart: 12, of which 4 were waited for; matrix products, arithmetic and copies ran while one was open for 0% of the time, Pallas kernels for 16%

profile of v6, /device:TPU:1, one launch (start us, length us, event | category | flops | bytes accessed | tf_op | source)
XLA Modules:
  0.0 67.9 jit_solution(64685155463802272)
XLA Ops:
  1.3 4.0 %first_product.1 = (f32[32,64,128]{2,1,0:T(8,128)S(1)}, f32[32,8,128]{2,1,0:T(8,128)S(1)}, f32[4,72,128]{2,1,0:T(8,128)S(1)}, f32[8,64,128]{2,1,0:T(8,128)S(1)},...) custom-call(s32[96]{0:T(128)} %r_0_.1, s32[96]{0:T(128)} %r_1_.1, s32[1]{0:T(128)S(6)} %copy.9.r_2_, ...), custom_call_target="tpu_custom_call" | custom-call | bytes 14760000 | tf_op jit(solution)/shard_map/first_product/pallas_call | solution.py:404
  5.3 3.8 %collective-permute-start.6 = (bf16[64,4096]{1,0:T(8,128)(2,1)S(1)}, bf16[64,4096]{1,0:T(8,128)(2,1)S(1)}, u32[]{:S(2)}, u32[]{:S(2)}) collective-permute-start(bf16[64,4096]{1,0:T(8,128)(2,1)S(1)} %copy-done), channel_id=1, source_target_pairs={{0,128},{64,192},{128,0},{192,64},{1,129},{65,193},{129,1},{193,65... | collective-permute-start | bytes 1572872 | tf_op jit(solution)/shard_map/ppermute | solution.py:392
  9.2 0.8 %collective-permute-start.5 = (bf16[64,4096]{1,0:T(8,128)(2,1)S(1)}, bf16[64,4096]{1,0:T(8,128)(2,1)S(1)}, u32[]{:S(2)}, u32[]{:S(2)}) collective-permute-start(bf16[64,4096]{1,0:T(8,128)(2,1)S(1)} %copy-done), channel_id=1, source_target_pairs={{0,192},{64,0},{128,64},{192,128},{1,193},{65,1},{129,65},{193,129... | collective-permute-start | bytes 1572872 | tf_op jit(solution)/shard_map/ppermute | solution.py:392
  9.9 0.7 %collective-permute-start.4 = (bf16[64,4096]{1,0:T(8,128)(2,1)S(1)}, bf16[64,4096]{1,0:T(8,128)(2,1)S(1)}, u32[]{:S(2)}, u32[]{:S(2)}) collective-permute-start(bf16[64,4096]{1,0:T(8,128)(2,1)S(1)} %copy-done), channel_id=1, source_target_pairs={{0,64},{64,128},{128,192},{192,0},{1,65},{65,129},{129,193},{193,1... | collective-permute-start | bytes 1572872 | tf_op jit(solution)/shard_map/ppermute | solution.py:392
  10.6 0.9 %collective-permute-start = (f32[8,64,128]{2,1,0:T(8,128)S(1)}, f32[8,64,128]{2,1,0:T(8,128)S(1)}, u32[]{:S(2)}, u32[]{:S(2)}) collective-permute-start(f32[8,64,128]{2,1,0:T(8,128)S(1)} %get-tuple-element.32), channel_id=1, source_target_pairs={{0,63},{1,0},{2,1},{3,2},{4,3},{5,4},{6,5},{7,6},{8,7},{9,8},{10,9... | collective-permute-start | bytes 786440 | tf_op jit(solution)/shard_map/ppermute | solution.py:392
  11.5 1.5 %collective-permute-start.1 = (f32[4,72,128]{2,1,0:T(8,128)S(1)}, f32[4,72,128]{2,1,0:T(8,128)S(1)}, u32[]{:S(2)}, u32[]{:S(2)}) collective-permute-start(f32[4,72,128]{2,1,0:T(8,128)S(1)} %get-tuple-element.31.spill_ref), channel_id=1, source_target_pairs={{0,1},{1,2},{2,3},{3,4},{4,5},{5,6},{6,7},{7,8},{8,9},{9,10},{10,1... | collective-permute-start | bytes 442376 | tf_op jit(solution)/shard_map/ppermute | solution.py:392
  13.1 1.7 %inner_sums.1.sums_ref = f32[4,64,128]{2,1,0:T(8,128)S(1)} custom-call(s32[520]{0:T(1024)S(1)} %get-tuple-element.24.lists_ref.lists_hbm.r_0_, f32[64,4096]{1,0:T(8,128)S(1)} %get-tuple-element.25.cot_ref, f32[32,64,128]{2,1,0:T(8,128)S(1)} %get-tuple-element.26.v_ref, f32[32,8,128]{2,1,0:T(8,128)S(1)} %get-tuple-element.27.diag_ref, ...), custom_call_target="tpu_custom_call" | custom-call | bytes 18450000 | tf_op jit(solution)/shard_map/inner_sums/pallas_call | solution.py:404
  14.8 4.2 %collective-permute-done.1.before_ref = f32[4,72,128]{2,1,0:T(8,128)S(1)} collective-permute-done((f32[4,72,128]{2,1,0:T(8,128)S(1)}, f32[4,72,128]{2,1,0:T(8,128)S(1)}, u32[]{:S(2)}, u32[]{:S(2)}) %collective-permute-start.1) | collective-permute-done | bytes 147488 | tf_op jit(solution)/shard_map/ppermute | solution.py:392
  19.0 0.0 collective-permute-done.after_ref
  19.1 1.6 %outer_sums.1 = (f32[12,64,128]{2,1,0:T(8,128)S(1)}, f32[64,1,256]{2,1,0:T(1,128)S(1)}) custom-call(s32[520]{0:T(1024)S(1)} %get-tuple-element.24.lists_ref.lists_hbm.r_0_, f32[64,4096]{1,0:T(8,128)S(1)} %get-tuple-element.25.cot_ref, f32[32,64,128]{2,1,0:T(8,128)S(1)} %get-tuple-element.26.v_ref, f32[32,8,128]{2,1,0:T(8,128)S(1)} %get-tuple-element.27.diag_ref, ...), custom_call_target="tpu_custom_call" | custom-call | bytes 221400000 | tf_op jit(solution)/shard_map/outer_sums/pallas_call | solution.py:404
  20.6 20.2 %all_to_all.5.all_ref = f32[64,1,256]{2,1,0:T(1,128)S(1)} all-to-all(f32[64,1,256]{2,1,0:T(1,128)S(1)} %get-tuple-element.33), channel_id=1, replica_groups=mesh['pat'=4,'blk'=64] {'blk'}, dimensions={0} | all-to-all | bytes 131072 | tf_op jit(solution)/shard_map/all_to_all | solution.py:465
  40.8 1.5 %combine.1 = (f32[64,4096]{1,0:T(8,128)}, bf16[18,64,128]{2,1,0:T(8,128)(2,1)S(1)}, bf16[18,64,128]{2,1,0:T(8,128)(2,1)S(1)}) custom-call(f32[64,1,256]{2,1,0:T(1,128)S(1)} %all_to_all.5.all_ref, f32[64,4096]{1,0:T(8,128)S(1)} %get-tuple-element.25.cot_ref, f32[8,64,128]{2,1,0:T(8,128)S(1)} %collective-permute-done.after_ref, ...), custom_call_target="tpu_custom_call" | custom-call | bytes 369000 | tf_op jit(solution)/shard_map/combine/pallas_call | solution.py:404
  42.3 0.4 collective-permute-start.2
  42.7 2.3 %collective-permute-start.3 = (bf16[18,64,128]{2,1,0:T(8,128)(2,1)S(1)}, bf16[18,64,128]{2,1,0:T(8,128)(2,1)S(1)}, u32[]{:S(2)}, u32[]{:S(2)}) collective-permute-start(bf16[18,64,128]{2,1,0:T(8,128)(2,1)S(1)} %get-tuple-element.37.high_hbm), channel_id=1, source_target_pairs={{0,192},{64,0},{128,64},{192,128},{1,193},{65,1},{129,65},{193,129... | collective-permute-start | bytes 884744 | tf_op jit(solution)/shard_map/ppermute | solution.py:392
  45.0 0.0 collective-permute-done.6.opposite_hbm
  45.0 0.0 collective-permute-done.5.above_hbm
  45.0 0.0 collective-permute-done.4.below_hbm
  45.0 1.2 %collective-permute-start.7 = (bf16[4,64,512]{2,1,0:T(8,128)(2,1)S(1)}, bf16[4,64,512]{2,1,0:T(8,128)(2,1)S(1)}, u32[]{:S(2)}, u32[]{:S(2)}) collective-permute-start(bf16[4,64,512]{2,1,0:T(8,128)(2,1)S(1)} %pad_maximum_fusion), channel_id=1, source_target_pairs={{0,63},{1,0},{2,1},{3,2},{4,3},{5,4},{6,5},{7,6},{8,7},{9,8},{10,9... | collective-permute-start | bytes 786440 | tf_op jit(solution)/shard_map/ppermute | solution.py:392
  46.2 0.8 %collective-permute-start.11 = (bf16[18,64,128]{2,1,0:T(8,128)(2,1)S(1)}, bf16[18,64,128]{2,1,0:T(8,128)(2,1)S(1)}, u32[]{:S(2)}, u32[]{:S(2)}) collective-permute-start(bf16[18,64,128]{2,1,0:T(8,128)(2,1)S(1)} %get-tuple-element.36.low_hbm), channel_id=1, source_target_pairs={{0,192},{64,0},{128,64},{192,128},{1,193},{65,1},{129,65},{193,129... | collective-permute-start | bytes 884744 | tf_op jit(solution)/shard_map/ppermute | solution.py:392
  47.0 0.7 %collective-permute-start.10 = (bf16[18,64,128]{2,1,0:T(8,128)(2,1)S(1)}, bf16[18,64,128]{2,1,0:T(8,128)(2,1)S(1)}, u32[]{:S(2)}, u32[]{:S(2)}) collective-permute-start(bf16[18,64,128]{2,1,0:T(8,128)(2,1)S(1)} %get-tuple-element.37.high_hbm), channel_id=1, source_target_pairs={{0,64},{64,128},{128,192},{192,0},{1,65},{65,129},{129,193},{193,1... | collective-permute-start | bytes 884744 | tf_op jit(solution)/shard_map/ppermute | solution.py:392
  47.7 3.7 %collective-permute-done.7.far_hbm = bf16[4,64,512]{2,1,0:T(8,128)(2,1)S(1)} collective-permute-done((bf16[4,64,512]{2,1,0:T(8,128)(2,1)S(1)}, bf16[4,64,512]{2,1,0:T(8,128)(2,1)S(1)}, u32[]{:S(2)}, u32[]{:S(2)}) %collective-permute-start.7) | collective-permute-done | bytes 262176 | tf_op jit(solution)/shard_map/ppermute | solution.py:392
  51.4 0.6 volt_blocks.1.volt_hbm.r_1_
  52.0 0.0 collective-permute-done.2.low0_hbm
  52.0 0.0 collective-permute-done.3.high1_hbm
  52.0 0.1 collective-permute-start.8
  52.1 2.7 %collective-permute-start.9 = (bf16[18,64,128]{2,1,0:T(8,128)(2,1)S(1)}, bf16[18,64,128]{2,1,0:T(8,128)(2,1)S(1)}, u32[]{:S(2)}, u32[]{:S(2)}) collective-permute-start(bf16[18,64,128]{2,1,0:T(8,128)(2,1)S(1)} %collective-permute-done.3.high1_hbm), channel_id=1, source_target_pairs={{0,192},{64,0},{128,64},{192,128},{1,193},{65,1},{129,65},{193,129... | collective-permute-start | bytes 884744 | tf_op jit(solution)/shard_map/ppermute | solution.py:392
  54.8 2.4 %own_grads.1 = (f32[96,32,128]{2,1,0:T(8,128)S(1)}, f32[36,128]{1,0:T(8,128)S(1)}) custom-call(s32[520]{0:T(1024)S(1)} %get-tuple-element.24.lists_ref.lists_hbm.r_0_, bf16[36,256,128]{2,1,0:T(8,128)(2,1)S(1)} %volt_blocks.1.volt_hbm.r_1_, bf16[18,64,128]{2,1,0:T(8,128)(2,1)S(1)} %get-tuple-element.36.low_hbm, ...), custom_call_target="tpu_custom_call" | custom-call | bytes 11070000 | tf_op jit(solution)/shard_map/own_grads/pallas_call | solution.py:404
  57.2 0.0 collective-permute-done.11.low1_hbm
  57.2 0.8 %collective-permute-done.10.high0_hbm = bf16[18,64,128]{2,1,0:T(8,128)(2,1)S(1)} collective-permute-done((bf16[18,64,128]{2,1,0:T(8,128)(2,1)S(1)}, bf16[18,64,128]{2,1,0:T(8,128)(2,1)S(1)}, u32[]{:S(2)}, u32[]{:S(2)}) %collective-permute-start.10) | collective-permute-done | bytes 294944 | tf_op jit(solution)/shard_map/ppermute | solution.py:392
  58.0 3.1 %near_grads.1 = (f32[96,32,128]{2,1,0:T(8,128)S(1)}, f32[36,128]{1,0:T(8,128)S(1)}) custom-call(s32[520]{0:T(1024)S(1)} %get-tuple-element.24.lists_ref.lists_hbm.r_0_, bf16[36,256,128]{2,1,0:T(8,128)(2,1)S(1)} %volt_blocks.1.volt_hbm.r_1_, bf16[18,64,128]{2,1,0:T(8,128)(2,1)S(1)} %collective-permute-done.2.low0_hbm, ...), custom_call_target="tpu_custom_call" | custom-call | bytes 14760000 | tf_op jit(solution)/shard_map/near_grads/pallas_call | solution.py:404
  61.1 3.2 %collective-permute-done.8.r_2_ = bf16[18,64,128]{2,1,0:T(8,128)(2,1)S(1)} collective-permute-done((bf16[18,64,128]{2,1,0:T(8,128)(2,1)S(1)}, bf16[18,64,128]{2,1,0:T(8,128)(2,1)S(1)}, u32[]{:S(2)}, u32[]{:S(2)}) %collective-permute-start.8) | collective-permute-done | bytes 294944 | tf_op jit(solution)/shard_map/ppermute | solution.py:392
  64.3 3.4 %late_grads.1 = bf16[96,32,128]{2,1,0:T(8,128)(2,1)} custom-call(s32[520]{0:T(1024)S(1)} %get-tuple-element.24.lists_ref.lists_hbm.r_0_, bf16[36,256,128]{2,1,0:T(8,128)(2,1)S(1)} %volt_blocks.1.volt_hbm.r_1_, bf16[18,64,128]{2,1,0:T(8,128)(2,1)S(1)} %collective-permute-done.8.r_2_, bf16[18,64,128]{2,1,0:T(8,128)(2,1)S(1)} %collective-permute-done.9.r_3_, ...), custom_call_target="tpu_custom_call" | custom-call | bytes 3690000 | tf_op jit(solution)/shard_map/late_grads/pallas_call | solution.py:404
  (4 shorter events, 0.0 us)
Async XLA Ops:
  0.6 4.7 %copy-start = (bf16[64,4096]{1,0:T(8,128)(2,1)S(1)}, bf16[64,4096]{1,0:T(8,128)(2,1)}, u32[]{:S(2)}) copy-start(bf16[64,4096]{1,0:T(8,128)(2,1)} %own_hbm.1) | copy-start | bytes 1572868
  5.3 39.6 %collective-permute-start.6 = (bf16[64,4096]{1,0:T(8,128)(2,1)S(1)}, bf16[64,4096]{1,0:T(8,128)(2,1)S(1)}, u32[]{:S(2)}, u32[]{:S(2)}) collective-permute-start(bf16[64,4096]{1,0:T(8,128)(2,1)S(1)} %copy-done), channel_id=1, source_target_pairs={{0,128},{64,192},{128,0},{192,64},{1,129},{65,193},{129,1},{193,65... | collective-permute-start | bytes 1572872 | tf_op jit(solution)/shard_map/ppermute | solution.py:392
  9.2 35.8 %collective-permute-start.5 = (bf16[64,4096]{1,0:T(8,128)(2,1)S(1)}, bf16[64,4096]{1,0:T(8,128)(2,1)S(1)}, u32[]{:S(2)}, u32[]{:S(2)}) collective-permute-start(bf16[64,4096]{1,0:T(8,128)(2,1)S(1)} %copy-done), channel_id=1, source_target_pairs={{0,192},{64,0},{128,64},{192,128},{1,193},{65,1},{129,65},{193,129... | collective-permute-start | bytes 1572872 | tf_op jit(solution)/shard_map/ppermute | solution.py:392
  9.9 35.0 %collective-permute-start.4 = (bf16[64,4096]{1,0:T(8,128)(2,1)S(1)}, bf16[64,4096]{1,0:T(8,128)(2,1)S(1)}, u32[]{:S(2)}, u32[]{:S(2)}) collective-permute-start(bf16[64,4096]{1,0:T(8,128)(2,1)S(1)} %copy-done), channel_id=1, source_target_pairs={{0,64},{64,128},{128,192},{192,0},{1,65},{65,129},{129,193},{193,1... | collective-permute-start | bytes 1572872 | tf_op jit(solution)/shard_map/ppermute | solution.py:392
  10.6 8.4 %collective-permute-start = (f32[8,64,128]{2,1,0:T(8,128)S(1)}, f32[8,64,128]{2,1,0:T(8,128)S(1)}, u32[]{:S(2)}, u32[]{:S(2)}) collective-permute-start(f32[8,64,128]{2,1,0:T(8,128)S(1)} %get-tuple-element.32), channel_id=1, source_target_pairs={{0,63},{1,0},{2,1},{3,2},{4,3},{5,4},{6,5},{7,6},{8,7},{9,8},{10,9... | collective-permute-start | bytes 786440 | tf_op jit(solution)/shard_map/ppermute | solution.py:392
  11.5 7.5 %collective-permute-start.1 = (f32[4,72,128]{2,1,0:T(8,128)S(1)}, f32[4,72,128]{2,1,0:T(8,128)S(1)}, u32[]{:S(2)}, u32[]{:S(2)}) collective-permute-start(f32[4,72,128]{2,1,0:T(8,128)S(1)} %get-tuple-element.31.spill_ref), channel_id=1, source_target_pairs={{0,1},{1,2},{2,3},{3,4},{4,5},{5,6},{6,7},{7,8},{8,9},{9,10},{10,1... | collective-permute-start | bytes 442376 | tf_op jit(solution)/shard_map/ppermute | solution.py:392
  42.3 9.7 %collective-permute-start.2 = (bf16[18,64,128]{2,1,0:T(8,128)(2,1)S(1)}, bf16[18,64,128]{2,1,0:T(8,128)(2,1)S(1)}, u32[]{:S(2)}, u32[]{:S(2)}) collective-permute-start(bf16[18,64,128]{2,1,0:T(8,128)(2,1)S(1)} %get-tuple-element.36.low_hbm), channel_id=1, source_target_pairs={{0,64},{64,128},{128,192},{192,0},{1,65},{65,129},{129,193},{193,1... | collective-permute-start | bytes 884744 | tf_op jit(solution)/shard_map/ppermute | solution.py:392
  42.7 9.3 %collective-permute-start.3 = (bf16[18,64,128]{2,1,0:T(8,128)(2,1)S(1)}, bf16[18,64,128]{2,1,0:T(8,128)(2,1)S(1)}, u32[]{:S(2)}, u32[]{:S(2)}) collective-permute-start(bf16[18,64,128]{2,1,0:T(8,128)(2,1)S(1)} %get-tuple-element.37.high_hbm), channel_id=1, source_target_pairs={{0,192},{64,0},{128,64},{192,128},{1,193},{65,1},{129,65},{193,129... | collective-permute-start | bytes 884744 | tf_op jit(solution)/shard_map/ppermute | solution.py:392
  45.0 6.3 %collective-permute-start.7 = (bf16[4,64,512]{2,1,0:T(8,128)(2,1)S(1)}, bf16[4,64,512]{2,1,0:T(8,128)(2,1)S(1)}, u32[]{:S(2)}, u32[]{:S(2)}) collective-permute-start(bf16[4,64,512]{2,1,0:T(8,128)(2,1)S(1)} %pad_maximum_fusion), channel_id=1, source_target_pairs={{0,63},{1,0},{2,1},{3,2},{4,3},{5,4},{6,5},{7,6},{8,7},{9,8},{10,9... | collective-permute-start | bytes 786440 | tf_op jit(solution)/shard_map/ppermute | solution.py:392
  46.2 10.9 %collective-permute-start.11 = (bf16[18,64,128]{2,1,0:T(8,128)(2,1)S(1)}, bf16[18,64,128]{2,1,0:T(8,128)(2,1)S(1)}, u32[]{:S(2)}, u32[]{:S(2)}) collective-permute-start(bf16[18,64,128]{2,1,0:T(8,128)(2,1)S(1)} %get-tuple-element.36.low_hbm), channel_id=1, source_target_pairs={{0,192},{64,0},{128,64},{192,128},{1,193},{65,1},{129,65},{193,129... | collective-permute-start | bytes 884744 | tf_op jit(solution)/shard_map/ppermute | solution.py:392
  47.0 11.0 %collective-permute-start.10 = (bf16[18,64,128]{2,1,0:T(8,128)(2,1)S(1)}, bf16[18,64,128]{2,1,0:T(8,128)(2,1)S(1)}, u32[]{:S(2)}, u32[]{:S(2)}) collective-permute-start(bf16[18,64,128]{2,1,0:T(8,128)(2,1)S(1)} %get-tuple-element.37.high_hbm), channel_id=1, source_target_pairs={{0,64},{64,128},{128,192},{192,0},{1,65},{65,129},{129,193},{193,1... | collective-permute-start | bytes 884744 | tf_op jit(solution)/shard_map/ppermute | solution.py:392
  52.0 12.3 %collective-permute-start.8 = (bf16[18,64,128]{2,1,0:T(8,128)(2,1)S(1)}, bf16[18,64,128]{2,1,0:T(8,128)(2,1)S(1)}, u32[]{:S(2)}, u32[]{:S(2)}) collective-permute-start(bf16[18,64,128]{2,1,0:T(8,128)(2,1)S(1)} %collective-permute-done.2.low0_hbm), channel_id=1, source_target_pairs={{0,64},{64,128},{128,192},{192,0},{1,65},{65,129},{129,193},{193,1... | collective-permute-start | bytes 884744 | tf_op jit(solution)/shard_map/ppermute | solution.py:392
  52.1 12.2 %collective-permute-start.9 = (bf16[18,64,128]{2,1,0:T(8,128)(2,1)S(1)}, bf16[18,64,128]{2,1,0:T(8,128)(2,1)S(1)}, u32[]{:S(2)}, u32[]{:S(2)}) collective-permute-start(bf16[18,64,128]{2,1,0:T(8,128)(2,1)S(1)} %collective-permute-done.3.high1_hbm), channel_id=1, source_target_pairs={{0,192},{64,0},{128,64},{192,128},{1,193},{65,1},{129,65},{193,129... | collective-permute-start | bytes 884744 | tf_op jit(solution)/shard_map/ppermute | solution.py:392

commit v7 on v6

--- a/solution.py
+++ b/solution.py
@@ -235,7 +235,7 @@
     moments_ref[:, :, BLOCK:] = jnp.broadcast_to(high[None], (devices, 1, BLOCK))
 
 
-def combine_kernel(all_ref, cot_ref, after_ref, v_ref, edges_ref, adjoint_ref, low_ref, high_ref):
+def combine_kernel(all_ref, cot_ref, after_ref, v_ref, edges_ref, coef_ref, low_ref, high_ref):
     pats = cot_ref.shape[0]
     total = jnp.sum(all_ref[...], axis=0)
     low = jnp.broadcast_to(total[:, :BLOCK], (8, BLOCK)).T
@@ -251,21 +251,29 @@
     on_c = jnp.broadcast_to((alpha + second * grown)[:, 0:1], (pats, BLOCK))
     on_v = jnp.broadcast_to((-alpha * second)[:, 0:1], (pats, BLOCK))
     half = low_ref.shape[0]
+    coef_ref[0] = on_c
+    coef_ref[1] = on_v
+    for b in range(EXT):
+        c = cot_ref[:, cols_of(b)] if b < NB_DEV else after_ref[b - NB_DEV]
+        value = (on_c * c + on_v * image_block(v_ref, edges_ref, b)).astype(BF16)
+        if b < half:
+            low_ref[b] = value
+        else:
+            high_ref[b - half] = value
+
+
+def image_block(v_ref, edges_ref, b):
+    if b < H:
+        return edges_ref[b]
+    if b < NB_DEV - H:
+        return v_ref[b]
+    return edges_ref[2 * H + b - NB_DEV]
+
+
+def adjoint_kernel(coef_ref, cot_ref, v_ref, edges_ref, adjoint_ref):
+    on_c, on_v = coef_ref[0], coef_ref[1]
     for b in range(NB_DEV):
-        if b < H:
-            v = edges_ref[b]
-        elif b < NB_DEV - H:
-            v = v_ref[b]
-        else:
-            v = edges_ref[2 * H + b - NB_DEV]
-        value = on_c * cot_ref[:, cols_of(b)] + on_v * v
-        adjoint_ref[:, cols_of(b)] = value
-        if b < half:
-            low_ref[b] = value.astype(BF16)
-        else:
-            high_ref[b - half] = value.astype(BF16)
-    for b in range(H):
-        high_ref[NB_DEV + b - half] = (on_c * after_ref[b] + on_v * edges_ref[2 * H + b]).astype(BF16)
+        adjoint_ref[:, cols_of(b)] = on_c * cot_ref[:, cols_of(b)] + on_v * image_block(v_ref, edges_ref, b)
 
 
 def chosen(part):
@@ -463,9 +471,9 @@
         lists, cot, v, diag, tiles, spill, after, before, sums, us=60.0,
     )
     everyone = lax.all_to_all(moments, "blk", 0, 0)
-    adjoint, low, high = call(
+    coef, low, high = call(
         combine_kernel, "combine",
-        [(cotangent.shape, F32), ((half, pats, BLOCK), BF16), ((EXT - half, pats, BLOCK), BF16)], [VMEM] * 5, [],
+        [((2, pats, BLOCK), F32), ((half, pats, BLOCK), BF16), ((EXT - half, pats, BLOCK), BF16)], [VMEM] * 5, [],
         everyone, cot, after, v, edges, us=0.1,
     )
     low_below = shifted(low, "pat", 1)
@@ -504,6 +512,10 @@
     partial, prow = call(
         near_grads_kernel, "near_grads", shares, [ANY] * 6 + [VMEM] * 2, [*scratch, *sems],
         lists, volt, *(in_vmem(x) for x in (low_below, high_below, low_above, high_above)), partial, prow, us=4.0,
+    )
+    prow, coef = lax.optimization_barrier((prow, coef))
+    (adjoint,) = call(
+        adjoint_kernel, "adjoint", [(cotangent.shape, F32)], [VMEM] * 4, [], coef, cot, v, edges,
     )
     scratch, sems = grad_work(1, BLOCK)
     products = [pltpu.VMEM((EXT + 1, rows_out, BLOCK), F32), pltpu.VMEM((EXT + 1, 8, BLOCK), F32)]

time: 68.3 us -> 67.7 us (level)
  waiting for transfers between devices: 12 us -> 10.3 us
  starting transfers between devices: 15.8 us -> 17.1 us
    ppermute x12, waiting for transfers between devices: 12 us -> 10.3 us  [shifted(): lax.ppermute(shard, axis, [(i, (i + by) % size) for i in range(size)])]
    ppermute x12, starting transfers between devices: 15.8 us -> 17.1 us  [shifted(): lax.ppermute(shard, axis, [(i, (i + by) % size) for i in range(size)])]
    pallas_call x8 -> x9, Pallas kernels: 18.2 us -> 18.4 us  [call(): pl.pallas_call(kernel, name=name, out_shape=[jax.ShapeDtypeStruct(s, d) f...]
where the time goes in v7:
time: 67.7 us; the launch traced here: 67.6 us
  blocking collectives  20.2 us (30%)
  Pallas kernels  18.4 us (27%)
  starting transfers between devices  17.1 us (25%)
  waiting for transfers between devices  10.3 us (15%)
  between operations  1.61 us (2%)
    all_to_all x1, blocking collectives, per_device(): everyone = lax.all_to_all(moments, 'blk', 0, 0)  20.2 us
    pallas_call x9, Pallas kernels, call(): pl.pallas_call(kernel, name=name, out_shape=[jax.ShapeDtypeStruct(s, d) f...  18.4 us
    ppermute x12, starting transfers between devices, shifted(): lax.ppermute(shard, axis, [(i, (i + by) % size) for i in range(size)])  17.1 us
    ppermute x12, waiting for transfers between devices, shifted(): lax.ppermute(shard, axis, [(i, (i + by) % size) for i in range(size)])  10.3 us
  transfers between devices with their start and end apart: 12, of which 4 were waited for; matrix products, arithmetic and copies ran while one was open for 0% of the time, Pallas kernels for 16%

profile of v7, /device:TPU:1, one launch (start us, length us, event | category | flops | bytes accessed | tf_op | source)
XLA Modules:
  0.0 67.6 jit_solution(15324474249547714641)
XLA Ops:
  1.3 4.0 %first_product.1 = (f32[32,64,128]{2,1,0:T(8,128)S(1)}, f32[32,8,128]{2,1,0:T(8,128)S(1)}, f32[4,72,128]{2,1,0:T(8,128)S(1)}, f32[8,64,128]{2,1,0:T(8,128)S(1)},...) custom-call(s32[96]{0:T(128)} %r_0_.1, s32[96]{0:T(128)} %r_1_.1, s32[1]{0:T(128)S(6)} %copy.9.r_2_, ...), custom_call_target="tpu_custom_call" | custom-call | bytes 14760000 | tf_op jit(solution)/shard_map/first_product/pallas_call | solution.py:412
  5.3 2.2 %collective-permute-start.4 = (bf16[64,4096]{1,0:T(8,128)(2,1)S(1)}, bf16[64,4096]{1,0:T(8,128)(2,1)S(1)}, u32[]{:S(2)}, u32[]{:S(2)}) collective-permute-start(bf16[64,4096]{1,0:T(8,128)(2,1)S(1)} %copy-done), channel_id=1, source_target_pairs={{0,64},{64,128},{128,192},{192,0},{1,65},{65,129},{129,193},{193,1... | collective-permute-start | bytes 1572872 | tf_op jit(solution)/shard_map/ppermute | solution.py:400
  7.5 1.5 %collective-permute-start.5 = (bf16[64,4096]{1,0:T(8,128)(2,1)S(1)}, bf16[64,4096]{1,0:T(8,128)(2,1)S(1)}, u32[]{:S(2)}, u32[]{:S(2)}) collective-permute-start(bf16[64,4096]{1,0:T(8,128)(2,1)S(1)} %copy-done), channel_id=1, source_target_pairs={{0,192},{64,0},{128,64},{192,128},{1,193},{65,1},{129,65},{193,129... | collective-permute-start | bytes 1572872 | tf_op jit(solution)/shard_map/ppermute | solution.py:400
  9.1 1.6 %collective-permute-start.6 = (bf16[64,4096]{1,0:T(8,128)(2,1)S(1)}, bf16[64,4096]{1,0:T(8,128)(2,1)S(1)}, u32[]{:S(2)}, u32[]{:S(2)}) collective-permute-start(bf16[64,4096]{1,0:T(8,128)(2,1)S(1)} %copy-done), channel_id=1, source_target_pairs={{0,128},{64,192},{128,0},{192,64},{1,129},{65,193},{129,1},{193,65... | collective-permute-start | bytes 1572872 | tf_op jit(solution)/shard_map/ppermute | solution.py:400
  10.6 0.9 %collective-permute-start = (f32[8,64,128]{2,1,0:T(8,128)S(1)}, f32[8,64,128]{2,1,0:T(8,128)S(1)}, u32[]{:S(2)}, u32[]{:S(2)}) collective-permute-start(f32[8,64,128]{2,1,0:T(8,128)S(1)} %get-tuple-element.34), channel_id=1, source_target_pairs={{0,63},{1,0},{2,1},{3,2},{4,3},{5,4},{6,5},{7,6},{8,7},{9,8},{10,9... | collective-permute-start | bytes 786440 | tf_op jit(solution)/shard_map/ppermute | solution.py:400
  11.5 1.5 %collective-permute-start.1 = (f32[4,72,128]{2,1,0:T(8,128)S(1)}, f32[4,72,128]{2,1,0:T(8,128)S(1)}, u32[]{:S(2)}, u32[]{:S(2)}) collective-permute-start(f32[4,72,128]{2,1,0:T(8,128)S(1)} %get-tuple-element.33.spill_ref), channel_id=1, source_target_pairs={{0,1},{1,2},{2,3},{3,4},{4,5},{5,6},{6,7},{7,8},{8,9},{9,10},{10,1... | collective-permute-start | bytes 442376 | tf_op jit(solution)/shard_map/ppermute | solution.py:400
  13.1 1.8 %inner_sums.1.sums_ref = f32[4,64,128]{2,1,0:T(8,128)S(1)} custom-call(s32[520]{0:T(1024)S(1)} %get-tuple-element.26.lists_ref.lists_hbm.r_0_, f32[64,4096]{1,0:T(8,128)S(1)} %get-tuple-element.27.cot_ref, f32[32,64,128]{2,1,0:T(8,128)S(1)} %get-tuple-element.28.v_ref, f32[32,8,128]{2,1,0:T(8,128)S(1)} %get-tuple-element.29.diag_ref, ...), custom_call_target="tpu_custom_call" | custom-call | bytes 18450000 | tf_op jit(solution)/shard_map/inner_sums/pallas_call | solution.py:412
  14.8 4.8 %collective-permute-done.1.before_ref = f32[4,72,128]{2,1,0:T(8,128)S(1)} collective-permute-done((f32[4,72,128]{2,1,0:T(8,128)S(1)}, f32[4,72,128]{2,1,0:T(8,128)S(1)}, u32[]{:S(2)}, u32[]{:S(2)}) %collective-permute-start.1) | collective-permute-done | bytes 147488 | tf_op jit(solution)/shard_map/ppermute | solution.py:400
  19.6 0.0 collective-permute-done.after_ref
  19.7 1.6 %outer_sums.1 = (f32[12,64,128]{2,1,0:T(8,128)S(1)}, f32[64,1,256]{2,1,0:T(1,128)S(1)}) custom-call(s32[520]{0:T(1024)S(1)} %get-tuple-element.26.lists_ref.lists_hbm.r_0_, f32[64,4096]{1,0:T(8,128)S(1)} %get-tuple-element.27.cot_ref, f32[32,64,128]{2,1,0:T(8,128)S(1)} %get-tuple-element.28.v_ref, f32[32,8,128]{2,1,0:T(8,128)S(1)} %get-tuple-element.29.diag_ref, ...), custom_call_target="tpu_custom_call" | custom-call | bytes 221400000 | tf_op jit(solution)/shard_map/outer_sums/pallas_call | solution.py:412
  21.2 20.2 %all_to_all.5.all_ref = f32[64,1,256]{2,1,0:T(1,128)S(1)} all-to-all(f32[64,1,256]{2,1,0:T(1,128)S(1)} %get-tuple-element.35), channel_id=1, replica_groups=mesh['pat'=4,'blk'=64] {'blk'}, dimensions={0} | all-to-all | bytes 131072 | tf_op jit(solution)/shard_map/all_to_all | solution.py:473
  41.4 0.5 combine.1
  41.9 0.5 collective-permute-start.2
  42.4 2.3 %collective-permute-start.3 = (bf16[18,64,128]{2,1,0:T(8,128)(2,1)S(1)}, bf16[18,64,128]{2,1,0:T(8,128)(2,1)S(1)}, u32[]{:S(2)}, u32[]{:S(2)}) collective-permute-start(bf16[18,64,128]{2,1,0:T(8,128)(2,1)S(1)} %get-tuple-element.38.high_hbm), channel_id=1, source_target_pairs={{0,192},{64,0},{128,64},{192,128},{1,193},{65,1},{129,65},{193,129... | collective-permute-start | bytes 884744 | tf_op jit(solution)/shard_map/ppermute | solution.py:400
  44.7 0.0 collective-permute-done.4.below_hbm
  44.7 0.0 collective-permute-done.5.above_hbm
  44.7 0.0 collective-permute-done.6.opposite_hbm
  44.7 1.2 %collective-permute-start.7 = (bf16[4,64,512]{2,1,0:T(8,128)(2,1)S(1)}, bf16[4,64,512]{2,1,0:T(8,128)(2,1)S(1)}, u32[]{:S(2)}, u32[]{:S(2)}) collective-permute-start(bf16[4,64,512]{2,1,0:T(8,128)(2,1)S(1)} %pad_maximum_fusion), channel_id=1, source_target_pairs={{0,63},{1,0},{2,1},{3,2},{4,3},{5,4},{6,5},{7,6},{8,7},{9,8},{10,9... | collective-permute-start | bytes 786440 | tf_op jit(solution)/shard_map/ppermute | solution.py:400
  45.9 0.0 collective-permute-start.8
  45.9 2.7 %collective-permute-start.9 = (bf16[18,64,128]{2,1,0:T(8,128)(2,1)S(1)}, bf16[18,64,128]{2,1,0:T(8,128)(2,1)S(1)}, u32[]{:S(2)}, u32[]{:S(2)}) collective-permute-start(bf16[18,64,128]{2,1,0:T(8,128)(2,1)S(1)} %get-tuple-element.37.low_hbm), channel_id=1, source_target_pairs={{0,192},{64,0},{128,64},{192,128},{1,193},{65,1},{129,65},{193,129... | collective-permute-start | bytes 884744 | tf_op jit(solution)/shard_map/ppermute | solution.py:400
  48.6 2.5 %collective-permute-done.7.far_hbm = bf16[4,64,512]{2,1,0:T(8,128)(2,1)S(1)} collective-permute-done((bf16[4,64,512]{2,1,0:T(8,128)(2,1)S(1)}, bf16[4,64,512]{2,1,0:T(8,128)(2,1)S(1)}, u32[]{:S(2)}, u32[]{:S(2)}) %collective-permute-start.7) | collective-permute-done | bytes 262176 | tf_op jit(solution)/shard_map/ppermute | solution.py:400
  51.1 0.6 volt_blocks.1.volt_hbm.r_1_
  51.7 0.0 collective-permute-done.2.low0_hbm
  51.7 0.0 collective-permute-done.3.high1_hbm
  51.7 0.1 collective-permute-start.10
  51.8 2.7 %collective-permute-start.11 = (bf16[18,64,128]{2,1,0:T(8,128)(2,1)S(1)}, bf16[18,64,128]{2,1,0:T(8,128)(2,1)S(1)}, u32[]{:S(2)}, u32[]{:S(2)}) collective-permute-start(bf16[18,64,128]{2,1,0:T(8,128)(2,1)S(1)} %collective-permute-done.3.high1_hbm), channel_id=1, source_target_pairs={{0,192},{64,0},{128,64},{192,128},{1,193},{65,1},{129,65},{193,129... | collective-permute-start | bytes 884744 | tf_op jit(solution)/shard_map/ppermute | solution.py:400
  54.5 2.4 %own_grads.1 = (f32[96,32,128]{2,1,0:T(8,128)S(1)}, f32[36,128]{1,0:T(8,128)S(1)}) custom-call(s32[520]{0:T(1024)S(1)} %get-tuple-element.26.lists_ref.lists_hbm.r_0_, bf16[36,256,128]{2,1,0:T(8,128)(2,1)S(1)} %volt_blocks.1.volt_hbm.r_1_, bf16[18,64,128]{2,1,0:T(8,128)(2,1)S(1)} %get-tuple-element.37.low_hbm, ...), custom_call_target="tpu_custom_call" | custom-call | bytes 11070000 | tf_op jit(solution)/shard_map/own_grads/pallas_call | solution.py:412
  56.9 0.9 %collective-permute-done.8.high0_hbm = bf16[18,64,128]{2,1,0:T(8,128)(2,1)S(1)} collective-permute-done((bf16[18,64,128]{2,1,0:T(8,128)(2,1)S(1)}, bf16[18,64,128]{2,1,0:T(8,128)(2,1)S(1)}, u32[]{:S(2)}, u32[]{:S(2)}) %collective-permute-start.8) | collective-permute-done | bytes 294944 | tf_op jit(solution)/shard_map/ppermute | solution.py:400
  57.7 3.1 %near_grads.1 = (f32[96,32,128]{2,1,0:T(8,128)S(1)}, f32[36,128]{1,0:T(8,128)S(1)}) custom-call(s32[520]{0:T(1024)S(1)} %get-tuple-element.26.lists_ref.lists_hbm.r_0_, bf16[36,256,128]{2,1,0:T(8,128)(2,1)S(1)} %volt_blocks.1.volt_hbm.r_1_, bf16[18,64,128]{2,1,0:T(8,128)(2,1)S(1)} %collective-permute-done.2.low0_hbm, ...), custom_call_target="tpu_custom_call" | custom-call | bytes 14760000 | tf_op jit(solution)/shard_map/near_grads/pallas_call | solution.py:412
  60.8 1.1 %adjoint.1 = f32[64,4096]{1,0:T(8,128)} custom-call(f32[2,64,128]{2,1,0:T(8,128)S(1)} %get-tuple-element.47.coef_ref, f32[64,4096]{1,0:T(8,128)S(1)} %get-tuple-element.27.cot_ref, f32[32,64,128]{2,1,0:T(8,128)S(1)} %get-tuple-element.28.v_ref, f32[12,64,128]{2,1,0:T(8,128)S(1)} %get-tuple-element.36.edges_ref), custom_call_target="tpu_custom_call" | custom-call | bytes 3690000 | tf_op jit(solution)/shard_map/adjoint/pallas_call | solution.py:412
  61.9 2.1 %collective-permute-done.10.r_2_ = bf16[18,64,128]{2,1,0:T(8,128)(2,1)S(1)} collective-permute-done((bf16[18,64,128]{2,1,0:T(8,128)(2,1)S(1)}, bf16[18,64,128]{2,1,0:T(8,128)(2,1)S(1)}, u32[]{:S(2)}, u32[]{:S(2)}) %collective-permute-start.10) | collective-permute-done | bytes 294944 | tf_op jit(solution)/shard_map/ppermute | solution.py:400
  64.0 3.4 %late_grads.1 = bf16[96,32,128]{2,1,0:T(8,128)(2,1)} custom-call(s32[520]{0:T(1024)S(1)} %get-tuple-element.26.lists_ref.lists_hbm.r_0_, bf16[36,256,128]{2,1,0:T(8,128)(2,1)S(1)} %volt_blocks.1.volt_hbm.r_1_, bf16[18,64,128]{2,1,0:T(8,128)(2,1)S(1)} %collective-permute-done.10.r_2_, bf16[18,64,128]{2,1,0:T(8,128)(2,1)S(1)} %collective-permute-done.11.r_3_, ...), custom_call_target="tpu_custom_call" | custom-call | bytes 3690000 | tf_op jit(solution)/shard_map/late_grads/pallas_call | solution.py:412
  (5 shorter events, 0.0 us)
Async XLA Ops:
  0.6 4.7 %copy-start = (bf16[64,4096]{1,0:T(8,128)(2,1)S(1)}, bf16[64,4096]{1,0:T(8,128)(2,1)}, u32[]{:S(2)}) copy-start(bf16[64,4096]{1,0:T(8,128)(2,1)} %own_hbm.1) | copy-start | bytes 1572868
  5.3 39.4 %collective-permute-start.4 = (bf16[64,4096]{1,0:T(8,128)(2,1)S(1)}, bf16[64,4096]{1,0:T(8,128)(2,1)S(1)}, u32[]{:S(2)}, u32[]{:S(2)}) collective-permute-start(bf16[64,4096]{1,0:T(8,128)(2,1)S(1)} %copy-done), channel_id=1, source_target_pairs={{0,64},{64,128},{128,192},{192,0},{1,65},{65,129},{129,193},{193,1... | collective-permute-start | bytes 1572872 | tf_op jit(solution)/shard_map/ppermute | solution.py:400
  7.5 37.1 %collective-permute-start.5 = (bf16[64,4096]{1,0:T(8,128)(2,1)S(1)}, bf16[64,4096]{1,0:T(8,128)(2,1)S(1)}, u32[]{:S(2)}, u32[]{:S(2)}) collective-permute-start(bf16[64,4096]{1,0:T(8,128)(2,1)S(1)} %copy-done), channel_id=1, source_target_pairs={{0,192},{64,0},{128,64},{192,128},{1,193},{65,1},{129,65},{193,129... | collective-permute-start | bytes 1572872 | tf_op jit(solution)/shard_map/ppermute | solution.py:400
  9.1 35.6 %collective-permute-start.6 = (bf16[64,4096]{1,0:T(8,128)(2,1)S(1)}, bf16[64,4096]{1,0:T(8,128)(2,1)S(1)}, u32[]{:S(2)}, u32[]{:S(2)}) collective-permute-start(bf16[64,4096]{1,0:T(8,128)(2,1)S(1)} %copy-done), channel_id=1, source_target_pairs={{0,128},{64,192},{128,0},{192,64},{1,129},{65,193},{129,1},{193,65... | collective-permute-start | bytes 1572872 | tf_op jit(solution)/shard_map/ppermute | solution.py:400
  10.6 9.0 %collective-permute-start = (f32[8,64,128]{2,1,0:T(8,128)S(1)}, f32[8,64,128]{2,1,0:T(8,128)S(1)}, u32[]{:S(2)}, u32[]{:S(2)}) collective-permute-start(f32[8,64,128]{2,1,0:T(8,128)S(1)} %get-tuple-element.34), channel_id=1, source_target_pairs={{0,63},{1,0},{2,1},{3,2},{4,3},{5,4},{6,5},{7,6},{8,7},{9,8},{10,9... | collective-permute-start | bytes 786440 | tf_op jit(solution)/shard_map/ppermute | solution.py:400
  11.5 8.1 %collective-permute-start.1 = (f32[4,72,128]{2,1,0:T(8,128)S(1)}, f32[4,72,128]{2,1,0:T(8,128)S(1)}, u32[]{:S(2)}, u32[]{:S(2)}) collective-permute-start(f32[4,72,128]{2,1,0:T(8,128)S(1)} %get-tuple-element.33.spill_ref), channel_id=1, source_target_pairs={{0,1},{1,2},{2,3},{3,4},{4,5},{5,6},{6,7},{7,8},{8,9},{9,10},{10,1... | collective-permute-start | bytes 442376 | tf_op jit(solution)/shard_map/ppermute | solution.py:400
  41.9 9.8 %collective-permute-start.2 = (bf16[18,64,128]{2,1,0:T(8,128)(2,1)S(1)}, bf16[18,64,128]{2,1,0:T(8,128)(2,1)S(1)}, u32[]{:S(2)}, u32[]{:S(2)}) collective-permute-start(bf16[18,64,128]{2,1,0:T(8,128)(2,1)S(1)} %get-tuple-element.37.low_hbm), channel_id=1, source_target_pairs={{0,64},{64,128},{128,192},{192,0},{1,65},{65,129},{129,193},{193,1... | collective-permute-start | bytes 884744 | tf_op jit(solution)/shard_map/ppermute | solution.py:400
  42.4 9.3 %collective-permute-start.3 = (bf16[18,64,128]{2,1,0:T(8,128)(2,1)S(1)}, bf16[18,64,128]{2,1,0:T(8,128)(2,1)S(1)}, u32[]{:S(2)}, u32[]{:S(2)}) collective-permute-start(bf16[18,64,128]{2,1,0:T(8,128)(2,1)S(1)} %get-tuple-element.38.high_hbm), channel_id=1, source_target_pairs={{0,192},{64,0},{128,64},{192,128},{1,193},{65,1},{129,65},{193,129... | collective-permute-start | bytes 884744 | tf_op jit(solution)/shard_map/ppermute | solution.py:400
  44.7 6.3 %collective-permute-start.7 = (bf16[4,64,512]{2,1,0:T(8,128)(2,1)S(1)}, bf16[4,64,512]{2,1,0:T(8,128)(2,1)S(1)}, u32[]{:S(2)}, u32[]{:S(2)}) collective-permute-start(bf16[4,64,512]{2,1,0:T(8,128)(2,1)S(1)} %pad_maximum_fusion), channel_id=1, source_target_pairs={{0,63},{1,0},{2,1},{3,2},{4,3},{5,4},{6,5},{7,6},{8,7},{9,8},{10,9... | collective-permute-start | bytes 786440 | tf_op jit(solution)/shard_map/ppermute | solution.py:400
  45.9 11.8 %collective-permute-start.8 = (bf16[18,64,128]{2,1,0:T(8,128)(2,1)S(1)}, bf16[18,64,128]{2,1,0:T(8,128)(2,1)S(1)}, u32[]{:S(2)}, u32[]{:S(2)}) collective-permute-start(bf16[18,64,128]{2,1,0:T(8,128)(2,1)S(1)} %get-tuple-element.38.high_hbm), channel_id=1, source_target_pairs={{0,64},{64,128},{128,192},{192,0},{1,65},{65,129},{129,193},{193,1... | collective-permute-start | bytes 884744 | tf_op jit(solution)/shard_map/ppermute | solution.py:400
  45.9 11.8 %collective-permute-start.9 = (bf16[18,64,128]{2,1,0:T(8,128)(2,1)S(1)}, bf16[18,64,128]{2,1,0:T(8,128)(2,1)S(1)}, u32[]{:S(2)}, u32[]{:S(2)}) collective-permute-start(bf16[18,64,128]{2,1,0:T(8,128)(2,1)S(1)} %get-tuple-element.37.low_hbm), channel_id=1, source_target_pairs={{0,192},{64,0},{128,64},{192,128},{1,193},{65,1},{129,65},{193,129... | collective-permute-start | bytes 884744 | tf_op jit(solution)/shard_map/ppermute | solution.py:400
  51.7 12.3 %collective-permute-start.10 = (bf16[18,64,128]{2,1,0:T(8,128)(2,1)S(1)}, bf16[18,64,128]{2,1,0:T(8,128)(2,1)S(1)}, u32[]{:S(2)}, u32[]{:S(2)}) collective-permute-start(bf16[18,64,128]{2,1,0:T(8,128)(2,1)S(1)} %collective-permute-done.2.low0_hbm), channel_id=1, source_target_pairs={{0,64},{64,128},{128,192},{192,0},{1,65},{65,129},{129,193},{193,1... | collective-permute-start | bytes 884744 | tf_op jit(solution)/shard_map/ppermute | solution.py:400
  51.8 12.2 %collective-permute-start.11 = (bf16[18,64,128]{2,1,0:T(8,128)(2,1)S(1)}, bf16[18,64,128]{2,1,0:T(8,128)(2,1)S(1)}, u32[]{:S(2)}, u32[]{:S(2)}) collective-permute-start(bf16[18,64,128]{2,1,0:T(8,128)(2,1)S(1)} %collective-permute-done.3.high1_hbm), channel_id=1, source_target_pairs={{0,192},{64,0},{128,64},{192,128},{1,193},{65,1},{129,65},{193,129... | collective-permute-start | bytes 884744 | tf_op jit(solution)/shard_map/ppermute | solution.py:400

commit v8 on v7

--- a/solution.py
+++ b/solution.py
@@ -139,6 +139,10 @@
     return jnp.concatenate([high, low], axis=0)
 
 
+def rounding(c):
+    return c - c.astype(BF16).astype(F32)
+
+
 def quadratic(lists_ref, k, tiles_ref, exact_ref, pair_ref, unroll):
     pats = exact_ref.shape[1]
 
@@ -154,7 +158,7 @@
 def inner_kernel(lists_ref, cot_ref, v_ref, diag_ref, tiles_ref, sums_ref, exact_ref, pair_ref):
     pats = cot_ref.shape[0]
     zero = jnp.zeros((pats, BLOCK), F32)
-    m0, m1, m2, m3 = zero, zero, zero, zero
+    m0, m1, m2, m3, m4 = zero, zero, zero, zero, zero
     for b in range(NB_DEV):
         c = cot_ref[:, cols_of(b)]
         m0 = m0 + c * c
@@ -163,6 +167,7 @@
             m1 = m1 + c * v
             m2 = m2 + v * v
             m3 = m3 + diag_ref[b, 0:1, :] * (v * v)
+            m4 = m4 + rounding(c) * (diag_ref[b, 0:1, :] * c - v)
             exact_ref[b] = v
             pair_ref[b] = split(v)
     exact_ref[TRASH] = zero
@@ -170,6 +175,7 @@
     sums_ref[0] = m0
     sums_ref[1] = m1
     sums_ref[2] = m2
+    sums_ref[4] = m4
     sums_ref[3] = m3 - 2.0 * quadratic(lists_ref, 0, tiles_ref, exact_ref, pair_ref, UNROLL)
 
 
@@ -187,7 +193,7 @@
     halo_ref[H] = jnp.zeros((pats, BLOCK), BF16)
     cross_ref[H] = zero
 
-    m1, m2, m3 = sums_ref[1], sums_ref[2], sums_ref[3]
+    m1, m2, m3, m4 = sums_ref[1], sums_ref[2], sums_ref[3], sums_ref[4]
 
     def place(where, value):
         exact_ref[where] = value
@@ -200,6 +206,7 @@
         m1 = m1 + c * v
         m2 = m2 + v * v
         m3 = m3 + (diag_ref[b, 0:1, :] + degree) * (v * v)
+        m4 = m4 + rounding(c) * ((diag_ref[b, 0:1, :] + degree) * c - v)
         edges_ref[b] = v
         beyond = after_ref[H + b] + spill_ref[b, pats : pats + 1, :] * after_ref[b] - spill_ref[b, :pats, :]
         edges_ref[2 * H + b] = beyond
@@ -223,6 +230,7 @@
         m1 = m1 + c * u
         m2 = m2 + u * u
         m3 = m3 + diag_ref[last, 0:1, :] * (u * u)
+        m4 = m4 + rounding(c) * (diag_ref[last, 0:1, :] * c - u)
         edges_ref[H + b] = u
         place(last, u)
     exact_ref[TRASH] = zero
@@ -230,21 +238,24 @@
     m3 = m3 - 2.0 * quadratic(lists_ref, 2, tiles_ref, exact_ref, pair_ref, 16)
     low = jnp.sum(jnp.concatenate([sums_ref[0], m1], axis=0).T, axis=0, keepdims=True)
     high = jnp.sum(jnp.concatenate([m2, m3], axis=0).T, axis=0, keepdims=True)
+    last = jnp.sum(jnp.concatenate([m4, zero], axis=0).T, axis=0, keepdims=True)
     devices = moments_ref.shape[0]
     moments_ref[:, :, :BLOCK] = jnp.broadcast_to(low[None], (devices, 1, BLOCK))
-    moments_ref[:, :, BLOCK:] = jnp.broadcast_to(high[None], (devices, 1, BLOCK))
+    moments_ref[:, :, BLOCK : 2 * BLOCK] = jnp.broadcast_to(high[None], (devices, 1, BLOCK))
+    moments_ref[:, :, 2 * BLOCK :] = jnp.broadcast_to(last[None], (devices, 1, BLOCK))
 
 
 def combine_kernel(all_ref, cot_ref, after_ref, v_ref, edges_ref, coef_ref, low_ref, high_ref):
     pats = cot_ref.shape[0]
     total = jnp.sum(all_ref[...], axis=0)
     low = jnp.broadcast_to(total[:, :BLOCK], (8, BLOCK)).T
-    high = jnp.broadcast_to(total[:, BLOCK:], (8, BLOCK)).T
+    high = jnp.broadcast_to(total[:, BLOCK : 2 * BLOCK], (8, BLOCK)).T
+    m4 = jnp.broadcast_to(total[:, 2 * BLOCK :], (8, BLOCK)).T[:pats]
     m0, m1, m2, m3 = low[:pats], low[pats:], high[:pats], high[pats:]
     alpha = m0 / m1
     norm = jnp.maximum(alpha * alpha * m2 - m0, 0.0)
     grown = 1.0 + norm / m0
-    curvature = alpha * alpha * m3 - grown * grown * m1
+    curvature = alpha * alpha * m3 - grown * grown * m1 + m4 * grown * (2.0 - grown)
     positive = curvature > 0.0
     second = jnp.where(positive, norm / jnp.where(positive, curvature, 1.0), 0.0)
     second = jnp.minimum(second, 1.0 / MIN_GROUND)
@@ -458,12 +469,12 @@
     work = [pltpu.VMEM((EXT + 1, pats, BLOCK), F32), pltpu.VMEM((EXT + 1, 2 * pats, BLOCK), BF16)]
     (sums,) = call(
         inner_kernel, "inner_sums",
-        [((4, pats, BLOCK), F32)], [SMEM] + [VMEM] * 4, work,
+        [((5, pats, BLOCK), F32)], [SMEM] + [VMEM] * 4, work,
         lists, cot, v, diag, tiles, us=5.0,
     )
     edges, moments = call(
         outer_kernel, "outer_sums",
-        [((3 * H, pats, BLOCK), F32), ((devices, 1, 4 * pats), F32)], [ANY] + [VMEM] * 8,
+        [((3 * H, pats, BLOCK), F32), ((devices, 1, 6 * pats), F32)], [ANY] + [VMEM] * 8,
         [
             *work, pltpu.VMEM((H + 1, pats, BLOCK), BF16), pltpu.VMEM((H + 1, pats, BLOCK), F32),
             pltpu.SMEM(lists.shape, jnp.int32), pltpu.SemaphoreType.DMA,

time: 67.7 us -> 68.5 us (1.012)
  blocking collectives: 20.2 us -> 21.8 us
  Pallas kernels: 18.4 us -> 16.8 us
    all_to_all x1, blocking collectives: 20.2 us -> 21.8 us  [per_device(): everyone = lax.all_to_all(moments, 'blk', 0, 0)]
    pallas_call x9, Pallas kernels: 18.4 us -> 16.8 us  [call(): pl.pallas_call(kernel, name=name, out_shape=[jax.ShapeDtypeStruct(s, d) f...]
  transfers between devices with their start and end apart: 12 -> 12, of which waited for: 4 -> 4; matrix products, arithmetic and copies ran while one was open for 0% -> 0% of each run, Pallas kernels for 16% -> 15%
where the time goes in v8:
time: 68.5 us; the launch traced here: 68.3 us
  blocking collectives  21.8 us (32%)
  starting transfers between devices  17.7 us (26%)
  Pallas kernels  16.8 us (25%)
  waiting for transfers between devices  10.3 us (15%)
  between operations  1.61 us (2%)
    all_to_all x1, blocking collectives, per_device(): everyone = lax.all_to_all(moments, 'blk', 0, 0)  21.8 us
    ppermute x12, starting transfers between devices, shifted(): lax.ppermute(shard, axis, [(i, (i + by) % size) for i in range(size)])  17.7 us
    pallas_call x9, Pallas kernels, call(): pl.pallas_call(kernel, name=name, out_shape=[jax.ShapeDtypeStruct(s, d) f...  16.8 us
    ppermute x12, waiting for transfers between devices, shifted(): lax.ppermute(shard, axis, [(i, (i + by) % size) for i in range(size)])  10.3 us
  transfers between devices with their start and end apart: 12, of which 4 were waited for; matrix products, arithmetic and copies ran while one was open for 0% of the time, Pallas kernels for 15%

profile of v8, /device:TPU:1, one launch (start us, length us, event | category | flops | bytes accessed | tf_op | source)
XLA Modules:
  0.0 68.3 jit_solution(14980534114806198031)
XLA Ops:
  1.3 3.4 %first_product.1 = (f32[32,64,128]{2,1,0:T(8,128)S(1)}, f32[32,8,128]{2,1,0:T(8,128)S(1)}, f32[4,72,128]{2,1,0:T(8,128)S(1)}, f32[8,64,128]{2,1,0:T(8,128)S(1)},...) custom-call(s32[96]{0:T(128)} %r_0_.1, s32[96]{0:T(128)} %r_1_.1, s32[1]{0:T(128)S(6)} %copy.9.r_2_, ...), custom_call_target="tpu_custom_call" | custom-call | bytes 14760000 | tf_op jit(solution)/shard_map/first_product/pallas_call | solution.py:423
  4.7 2.2 %collective-permute-start.4 = (bf16[64,4096]{1,0:T(8,128)(2,1)S(1)}, bf16[64,4096]{1,0:T(8,128)(2,1)S(1)}, u32[]{:S(2)}, u32[]{:S(2)}) collective-permute-start(bf16[64,4096]{1,0:T(8,128)(2,1)S(1)} %copy-done), channel_id=1, source_target_pairs={{0,64},{64,128},{128,192},{192,0},{1,65},{65,129},{129,193},{193,1... | collective-permute-start | bytes 1572872 | tf_op jit(solution)/shard_map/ppermute | solution.py:411
  6.9 1.5 %collective-permute-start.5 = (bf16[64,4096]{1,0:T(8,128)(2,1)S(1)}, bf16[64,4096]{1,0:T(8,128)(2,1)S(1)}, u32[]{:S(2)}, u32[]{:S(2)}) collective-permute-start(bf16[64,4096]{1,0:T(8,128)(2,1)S(1)} %copy-done), channel_id=1, source_target_pairs={{0,192},{64,0},{128,64},{192,128},{1,193},{65,1},{129,65},{193,129... | collective-permute-start | bytes 1572872 | tf_op jit(solution)/shard_map/ppermute | solution.py:411
  8.5 1.6 %collective-permute-start.6 = (bf16[64,4096]{1,0:T(8,128)(2,1)S(1)}, bf16[64,4096]{1,0:T(8,128)(2,1)S(1)}, u32[]{:S(2)}, u32[]{:S(2)}) collective-permute-start(bf16[64,4096]{1,0:T(8,128)(2,1)S(1)} %copy-done), channel_id=1, source_target_pairs={{0,128},{64,192},{128,0},{192,64},{1,129},{65,193},{129,1},{193,65... | collective-permute-start | bytes 1572872 | tf_op jit(solution)/shard_map/ppermute | solution.py:411
  10.0 2.1 %collective-permute-start = (f32[8,64,128]{2,1,0:T(8,128)S(1)}, f32[8,64,128]{2,1,0:T(8,128)S(1)}, u32[]{:S(2)}, u32[]{:S(2)}) collective-permute-start(f32[8,64,128]{2,1,0:T(8,128)S(1)} %get-tuple-element.34), channel_id=1, source_target_pairs={{0,63},{1,0},{2,1},{3,2},{4,3},{5,4},{6,5},{7,6},{8,7},{9,8},{10,9... | collective-permute-start | bytes 786440 | tf_op jit(solution)/shard_map/ppermute | solution.py:411
  12.1 0.9 %collective-permute-start.1 = (f32[4,72,128]{2,1,0:T(8,128)S(1)}, f32[4,72,128]{2,1,0:T(8,128)S(1)}, u32[]{:S(2)}, u32[]{:S(2)}) collective-permute-start(f32[4,72,128]{2,1,0:T(8,128)S(1)} %get-tuple-element.33.spill_ref), channel_id=1, source_target_pairs={{0,1},{1,2},{2,3},{3,4},{4,5},{5,6},{6,7},{7,8},{8,9},{9,10},{10,1... | collective-permute-start | bytes 442376 | tf_op jit(solution)/shard_map/ppermute | solution.py:411
  13.1 1.9 %inner_sums.1.sums_ref = f32[5,64,128]{2,1,0:T(8,128)S(1)} custom-call(s32[520]{0:T(1024)S(1)} %get-tuple-element.26.lists_ref.lists_hbm.r_0_, f32[64,4096]{1,0:T(8,128)S(1)} %get-tuple-element.27.cot_ref, f32[32,64,128]{2,1,0:T(8,128)S(1)} %get-tuple-element.28.v_ref, f32[32,8,128]{2,1,0:T(8,128)S(1)} %get-tuple-element.29.diag_ref, ...), custom_call_target="tpu_custom_call" | custom-call | bytes 18450000 | tf_op jit(solution)/shard_map/inner_sums/pallas_call | solution.py:423
  15.0 4.0 %collective-permute-done.1.before_ref = f32[4,72,128]{2,1,0:T(8,128)S(1)} collective-permute-done((f32[4,72,128]{2,1,0:T(8,128)S(1)}, f32[4,72,128]{2,1,0:T(8,128)S(1)}, u32[]{:S(2)}, u32[]{:S(2)}) %collective-permute-start.1) | collective-permute-done | bytes 147488 | tf_op jit(solution)/shard_map/ppermute | solution.py:411
  19.0 0.0 collective-permute-done.after_ref
  19.0 1.6 %outer_sums.1 = (f32[12,64,128]{2,1,0:T(8,128)S(1)}, f32[64,1,384]{2,1,0:T(1,128)S(1)}) custom-call(s32[520]{0:T(1024)S(1)} %get-tuple-element.26.lists_ref.lists_hbm.r_0_, f32[64,4096]{1,0:T(8,128)S(1)} %get-tuple-element.27.cot_ref, f32[32,64,128]{2,1,0:T(8,128)S(1)} %get-tuple-element.28.v_ref, f32[32,8,128]{2,1,0:T(8,128)S(1)} %get-tuple-element.29.diag_ref, ...), custom_call_target="tpu_custom_call" | custom-call | bytes 221400000 | tf_op jit(solution)/shard_map/outer_sums/pallas_call | solution.py:423
  20.7 21.8 %all_to_all.5.all_ref = f32[64,1,384]{2,1,0:T(1,128)S(1)} all-to-all(f32[64,1,384]{2,1,0:T(1,128)S(1)} %get-tuple-element.35), channel_id=1, replica_groups=mesh['pat'=4,'blk'=64] {'blk'}, dimensions={0} | all-to-all | bytes 196608 | tf_op jit(solution)/shard_map/all_to_all | solution.py:484
  42.5 0.5 combine.1
  43.0 0.5 collective-permute-start.2
  43.5 2.3 %collective-permute-start.3 = (bf16[18,64,128]{2,1,0:T(8,128)(2,1)S(1)}, bf16[18,64,128]{2,1,0:T(8,128)(2,1)S(1)}, u32[]{:S(2)}, u32[]{:S(2)}) collective-permute-start(bf16[18,64,128]{2,1,0:T(8,128)(2,1)S(1)} %get-tuple-element.38.high_hbm), channel_id=1, source_target_pairs={{0,192},{64,0},{128,64},{192,128},{1,193},{65,1},{129,65},{193,129... | collective-permute-start | bytes 884744 | tf_op jit(solution)/shard_map/ppermute | solution.py:411
  45.8 0.0 collective-permute-done.4.below_hbm
  45.8 0.0 collective-permute-done.5.above_hbm
  45.8 0.0 collective-permute-done.6.opposite_hbm
  45.8 1.2 %collective-permute-start.7 = (bf16[4,64,512]{2,1,0:T(8,128)(2,1)S(1)}, bf16[4,64,512]{2,1,0:T(8,128)(2,1)S(1)}, u32[]{:S(2)}, u32[]{:S(2)}) collective-permute-start(bf16[4,64,512]{2,1,0:T(8,128)(2,1)S(1)} %pad_maximum_fusion), channel_id=1, source_target_pairs={{0,63},{1,0},{2,1},{3,2},{4,3},{5,4},{6,5},{7,6},{8,7},{9,8},{10,9... | collective-permute-start | bytes 786440 | tf_op jit(solution)/shard_map/ppermute | solution.py:411
  47.0 0.0 collective-permute-start.8
  47.0 2.7 %collective-permute-start.9 = (bf16[18,64,128]{2,1,0:T(8,128)(2,1)S(1)}, bf16[18,64,128]{2,1,0:T(8,128)(2,1)S(1)}, u32[]{:S(2)}, u32[]{:S(2)}) collective-permute-start(bf16[18,64,128]{2,1,0:T(8,128)(2,1)S(1)} %get-tuple-element.37.low_hbm), channel_id=1, source_target_pairs={{0,192},{64,0},{128,64},{192,128},{1,193},{65,1},{129,65},{193,129... | collective-permute-start | bytes 884744 | tf_op jit(solution)/shard_map/ppermute | solution.py:411
  49.7 2.5 %collective-permute-done.7.far_hbm = bf16[4,64,512]{2,1,0:T(8,128)(2,1)S(1)} collective-permute-done((bf16[4,64,512]{2,1,0:T(8,128)(2,1)S(1)}, bf16[4,64,512]{2,1,0:T(8,128)(2,1)S(1)}, u32[]{:S(2)}, u32[]{:S(2)}) %collective-permute-start.7) | collective-permute-done | bytes 262176 | tf_op jit(solution)/shard_map/ppermute | solution.py:411
  52.2 0.6 volt_blocks.1.volt_hbm.r_1_
  52.8 0.0 collective-permute-done.2.low0_hbm
  52.8 0.0 collective-permute-done.3.high1_hbm
  52.8 0.1 collective-permute-start.10
  52.9 2.7 %collective-permute-start.11 = (bf16[18,64,128]{2,1,0:T(8,128)(2,1)S(1)}, bf16[18,64,128]{2,1,0:T(8,128)(2,1)S(1)}, u32[]{:S(2)}, u32[]{:S(2)}) collective-permute-start(bf16[18,64,128]{2,1,0:T(8,128)(2,1)S(1)} %collective-permute-done.3.high1_hbm), channel_id=1, source_target_pairs={{0,192},{64,0},{128,64},{192,128},{1,193},{65,1},{129,65},{193,129... | collective-permute-start | bytes 884744 | tf_op jit(solution)/shard_map/ppermute | solution.py:411
  55.6 2.0 %own_grads.1 = (f32[96,32,128]{2,1,0:T(8,128)S(1)}, f32[36,128]{1,0:T(8,128)S(1)}) custom-call(s32[520]{0:T(1024)S(1)} %get-tuple-element.26.lists_ref.lists_hbm.r_0_, bf16[36,256,128]{2,1,0:T(8,128)(2,1)S(1)} %volt_blocks.1.volt_hbm.r_1_, bf16[18,64,128]{2,1,0:T(8,128)(2,1)S(1)} %get-tuple-element.37.low_hbm, ...), custom_call_target="tpu_custom_call" | custom-call | bytes 11070000 | tf_op jit(solution)/shard_map/own_grads/pallas_call | solution.py:423
  57.6 1.2 %collective-permute-done.8.high0_hbm = bf16[18,64,128]{2,1,0:T(8,128)(2,1)S(1)} collective-permute-done((bf16[18,64,128]{2,1,0:T(8,128)(2,1)S(1)}, bf16[18,64,128]{2,1,0:T(8,128)(2,1)S(1)}, u32[]{:S(2)}, u32[]{:S(2)}) %collective-permute-start.8) | collective-permute-done | bytes 294944 | tf_op jit(solution)/shard_map/ppermute | solution.py:411
  58.8 2.7 %near_grads.1 = (f32[96,32,128]{2,1,0:T(8,128)S(1)}, f32[36,128]{1,0:T(8,128)S(1)}) custom-call(s32[520]{0:T(1024)S(1)} %get-tuple-element.26.lists_ref.lists_hbm.r_0_, bf16[36,256,128]{2,1,0:T(8,128)(2,1)S(1)} %volt_blocks.1.volt_hbm.r_1_, bf16[18,64,128]{2,1,0:T(8,128)(2,1)S(1)} %collective-permute-done.2.low0_hbm, ...), custom_call_target="tpu_custom_call" | custom-call | bytes 14760000 | tf_op jit(solution)/shard_map/near_grads/pallas_call | solution.py:423
  61.5 1.1 %adjoint.1 = f32[64,4096]{1,0:T(8,128)} custom-call(f32[2,64,128]{2,1,0:T(8,128)S(1)} %get-tuple-element.47.coef_ref, f32[64,4096]{1,0:T(8,128)S(1)} %get-tuple-element.27.cot_ref, f32[32,64,128]{2,1,0:T(8,128)S(1)} %get-tuple-element.28.v_ref, f32[12,64,128]{2,1,0:T(8,128)S(1)} %get-tuple-element.36.edges_ref), custom_call_target="tpu_custom_call" | custom-call | bytes 3690000 | tf_op jit(solution)/shard_map/adjoint/pallas_call | solution.py:423
  62.6 2.6 %collective-permute-done.10.r_2_ = bf16[18,64,128]{2,1,0:T(8,128)(2,1)S(1)} collective-permute-done((bf16[18,64,128]{2,1,0:T(8,128)(2,1)S(1)}, bf16[18,64,128]{2,1,0:T(8,128)(2,1)S(1)}, u32[]{:S(2)}, u32[]{:S(2)}) %collective-permute-start.10) | collective-permute-done | bytes 294944 | tf_op jit(solution)/shard_map/ppermute | solution.py:411
  65.1 3.0 %late_grads.1 = bf16[96,32,128]{2,1,0:T(8,128)(2,1)} custom-call(s32[520]{0:T(1024)S(1)} %get-tuple-element.26.lists_ref.lists_hbm.r_0_, bf16[36,256,128]{2,1,0:T(8,128)(2,1)S(1)} %volt_blocks.1.volt_hbm.r_1_, bf16[18,64,128]{2,1,0:T(8,128)(2,1)S(1)} %collective-permute-done.10.r_2_, bf16[18,64,128]{2,1,0:T(8,128)(2,1)S(1)} %collective-permute-done.11.r_3_, ...), custom_call_target="tpu_custom_call" | custom-call | bytes 3690000 | tf_op jit(solution)/shard_map/late_grads/pallas_call | solution.py:423
  (5 shorter events, 0.0 us)
Async XLA Ops:
  0.6 4.1 %copy-start = (bf16[64,4096]{1,0:T(8,128)(2,1)S(1)}, bf16[64,4096]{1,0:T(8,128)(2,1)}, u32[]{:S(2)}) copy-start(bf16[64,4096]{1,0:T(8,128)(2,1)} %own_hbm.1) | copy-start | bytes 1572868
  4.7 41.0 %collective-permute-start.4 = (bf16[64,4096]{1,0:T(8,128)(2,1)S(1)}, bf16[64,4096]{1,0:T(8,128)(2,1)S(1)}, u32[]{:S(2)}, u32[]{:S(2)}) collective-permute-start(bf16[64,4096]{1,0:T(8,128)(2,1)S(1)} %copy-done), channel_id=1, source_target_pairs={{0,64},{64,128},{128,192},{192,0},{1,65},{65,129},{129,193},{193,1... | collective-permute-start | bytes 1572872 | tf_op jit(solution)/shard_map/ppermute | solution.py:411
  6.9 38.8 %collective-permute-start.5 = (bf16[64,4096]{1,0:T(8,128)(2,1)S(1)}, bf16[64,4096]{1,0:T(8,128)(2,1)S(1)}, u32[]{:S(2)}, u32[]{:S(2)}) collective-permute-start(bf16[64,4096]{1,0:T(8,128)(2,1)S(1)} %copy-done), channel_id=1, source_target_pairs={{0,192},{64,0},{128,64},{192,128},{1,193},{65,1},{129,65},{193,129... | collective-permute-start | bytes 1572872 | tf_op jit(solution)/shard_map/ppermute | solution.py:411
  8.5 37.3 %collective-permute-start.6 = (bf16[64,4096]{1,0:T(8,128)(2,1)S(1)}, bf16[64,4096]{1,0:T(8,128)(2,1)S(1)}, u32[]{:S(2)}, u32[]{:S(2)}) collective-permute-start(bf16[64,4096]{1,0:T(8,128)(2,1)S(1)} %copy-done), channel_id=1, source_target_pairs={{0,128},{64,192},{128,0},{192,64},{1,129},{65,193},{129,1},{193,65... | collective-permute-start | bytes 1572872 | tf_op jit(solution)/shard_map/ppermute | solution.py:411
  10.0 9.0 %collective-permute-start = (f32[8,64,128]{2,1,0:T(8,128)S(1)}, f32[8,64,128]{2,1,0:T(8,128)S(1)}, u32[]{:S(2)}, u32[]{:S(2)}) collective-permute-start(f32[8,64,128]{2,1,0:T(8,128)S(1)} %get-tuple-element.34), channel_id=1, source_target_pairs={{0,63},{1,0},{2,1},{3,2},{4,3},{5,4},{6,5},{7,6},{8,7},{9,8},{10,9... | collective-permute-start | bytes 786440 | tf_op jit(solution)/shard_map/ppermute | solution.py:411
  12.1 6.9 %collective-permute-start.1 = (f32[4,72,128]{2,1,0:T(8,128)S(1)}, f32[4,72,128]{2,1,0:T(8,128)S(1)}, u32[]{:S(2)}, u32[]{:S(2)}) collective-permute-start(f32[4,72,128]{2,1,0:T(8,128)S(1)} %get-tuple-element.33.spill_ref), channel_id=1, source_target_pairs={{0,1},{1,2},{2,3},{3,4},{4,5},{5,6},{6,7},{7,8},{8,9},{9,10},{10,1... | collective-permute-start | bytes 442376 | tf_op jit(solution)/shard_map/ppermute | solution.py:411
  43.0 9.8 %collective-permute-start.2 = (bf16[18,64,128]{2,1,0:T(8,128)(2,1)S(1)}, bf16[18,64,128]{2,1,0:T(8,128)(2,1)S(1)}, u32[]{:S(2)}, u32[]{:S(2)}) collective-permute-start(bf16[18,64,128]{2,1,0:T(8,128)(2,1)S(1)} %get-tuple-element.37.low_hbm), channel_id=1, source_target_pairs={{0,64},{64,128},{128,192},{192,0},{1,65},{65,129},{129,193},{193,1... | collective-permute-start | bytes 884744 | tf_op jit(solution)/shard_map/ppermute | solution.py:411
  43.5 9.3 %collective-permute-start.3 = (bf16[18,64,128]{2,1,0:T(8,128)(2,1)S(1)}, bf16[18,64,128]{2,1,0:T(8,128)(2,1)S(1)}, u32[]{:S(2)}, u32[]{:S(2)}) collective-permute-start(bf16[18,64,128]{2,1,0:T(8,128)(2,1)S(1)} %get-tuple-element.38.high_hbm), channel_id=1, source_target_pairs={{0,192},{64,0},{128,64},{192,128},{1,193},{65,1},{129,65},{193,129... | collective-permute-start | bytes 884744 | tf_op jit(solution)/shard_map/ppermute | solution.py:411
  45.8 6.3 %collective-permute-start.7 = (bf16[4,64,512]{2,1,0:T(8,128)(2,1)S(1)}, bf16[4,64,512]{2,1,0:T(8,128)(2,1)S(1)}, u32[]{:S(2)}, u32[]{:S(2)}) collective-permute-start(bf16[4,64,512]{2,1,0:T(8,128)(2,1)S(1)} %pad_maximum_fusion), channel_id=1, source_target_pairs={{0,63},{1,0},{2,1},{3,2},{4,3},{5,4},{6,5},{7,6},{8,7},{9,8},{10,9... | collective-permute-start | bytes 786440 | tf_op jit(solution)/shard_map/ppermute | solution.py:411
  47.0 11.8 %collective-permute-start.8 = (bf16[18,64,128]{2,1,0:T(8,128)(2,1)S(1)}, bf16[18,64,128]{2,1,0:T(8,128)(2,1)S(1)}, u32[]{:S(2)}, u32[]{:S(2)}) collective-permute-start(bf16[18,64,128]{2,1,0:T(8,128)(2,1)S(1)} %get-tuple-element.38.high_hbm), channel_id=1, source_target_pairs={{0,64},{64,128},{128,192},{192,0},{1,65},{65,129},{129,193},{193,1... | collective-permute-start | bytes 884744 | tf_op jit(solution)/shard_map/ppermute | solution.py:411
  47.0 11.8 %collective-permute-start.9 = (bf16[18,64,128]{2,1,0:T(8,128)(2,1)S(1)}, bf16[18,64,128]{2,1,0:T(8,128)(2,1)S(1)}, u32[]{:S(2)}, u32[]{:S(2)}) collective-permute-start(bf16[18,64,128]{2,1,0:T(8,128)(2,1)S(1)} %get-tuple-element.37.low_hbm), channel_id=1, source_target_pairs={{0,192},{64,0},{128,64},{192,128},{1,193},{65,1},{129,65},{193,129... | collective-permute-start | bytes 884744 | tf_op jit(solution)/shard_map/ppermute | solution.py:411
  52.8 12.3 %collective-permute-start.10 = (bf16[18,64,128]{2,1,0:T(8,128)(2,1)S(1)}, bf16[18,64,128]{2,1,0:T(8,128)(2,1)S(1)}, u32[]{:S(2)}, u32[]{:S(2)}) collective-permute-start(bf16[18,64,128]{2,1,0:T(8,128)(2,1)S(1)} %collective-permute-done.2.low0_hbm), channel_id=1, source_target_pairs={{0,64},{64,128},{128,192},{192,0},{1,65},{65,129},{129,193},{193,1... | collective-permute-start | bytes 884744 | tf_op jit(solution)/shard_map/ppermute | solution.py:411
  52.9 12.2 %collective-permute-start.11 = (bf16[18,64,128]{2,1,0:T(8,128)(2,1)S(1)}, bf16[18,64,128]{2,1,0:T(8,128)(2,1)S(1)}, u32[]{:S(2)}, u32[]{:S(2)}) collective-permute-start(bf16[18,64,128]{2,1,0:T(8,128)(2,1)S(1)} %collective-permute-done.3.high1_hbm), channel_id=1, source_target_pairs={{0,192},{64,0},{128,64},{192,128},{1,193},{65,1},{129,65},{193,129... | collective-permute-start | bytes 884744 | tf_op jit(solution)/shard_map/ppermute | solution.py:411
